TPU v7x, 128 devices: a whole 4x4x4 slice. The times are simulated.
128 devices in a mesh: section: 4 (over z), space: 16 (over y, x), batch: 2 (over core).
Axes of the slice: x: 4, y: 4, z: 4, core: 2. Of those that a mesh axis runs over, the one named last changes fastest.
Arguments:
- frames: bfloat16 [2, 2, 64, 32, 256], P(None, 'batch', 'space'), may hold values from -6 to 6
- cotangent: bfloat16 [2, 2, 64, 32, 256], P(None, 'batch', 'space'), may hold values from -6 to 6
- first_hidden: bfloat16 [4, 2, 64, 32, 256], P('section', 'batch', 'space'), may hold values from -0.8984375 to 0.8984375
- first_cell: float32 [4, 2, 64, 32, 256], P('section', 'batch', 'space'), may hold values from -5 to 5
- gate_bias: float32 [4, 1024], P('section'), may hold values from -4 to 4
- gate_weight: bfloat16 [4, 4608, 1024], P('section'), may hold values from -0.09375 to 0.09375
Outputs:
- weight_grad: float32 [4, 4608, 1024], P('section', ('space', 'batch'))
All inputs are finite; a program needn't handle non-finite values.
Results may differ from a plain program's by a relative error of at most 0.0035.
Values may be sent and summed in bfloat16 or wider, within the bound.
A program may use at most 128 MiB of HBM per device.

v0:
```python
import jax
import jax.numpy as jnp
from jax import lax
from jax.sharding import PartitionSpec as P


def with_halo(cells, sides, width):
    for axis, dim in sides:
        count = lax.axis_size(axis)
        ends = count - 1
        head = lax.slice_in_dim(cells, 0, width, axis=dim)
        tail = lax.slice_in_dim(cells, cells.shape[dim] - width, cells.shape[dim], axis=dim)
        cells = jnp.concatenate(
            [
                lax.ppermute(tail, axis, [(i, (i + 1) % count) for i in range(ends)]),
                cells,
                lax.ppermute(head, axis, [((i + 1) % count, i) for i in range(ends)]),
            ],
            axis=dim,
        )
    return cells


def passed_along(value, axis, steps):
    count = lax.axis_size(axis)
    first, last = (max(0, -steps), min(count, count - steps))
    return lax.ppermute(value, axis, [(source, source + steps) for source in range(first, last)])


def gate_patches(padded, out_rows, out_cols):
    pieces = [
        padded[..., row_off : row_off + out_rows, col_off : col_off + out_cols, :]
        for row_off in range(3)
        for col_off in range(3)
    ]
    return jnp.concatenate(pieces, axis=-1)


def adjoint_conv(grad_pad, weight, out_rows, out_cols):
    channels = weight.shape[0] // 9
    gate_count = weight.shape[1]
    kernel = weight.reshape(3, 3, channels, gate_count)
    total_sum = None
    for row_off in range(3):
        for col_off in range(3):
            window = grad_pad[
                ..., 2 - row_off : 2 - row_off + out_rows, 2 - col_off : 2 - col_off + out_cols, :
            ]
            flat_rows = window.reshape(-1, gate_count)
            product = lax.dot_general(
                flat_rows,
                kernel[row_off, col_off],
                (((1,), (1,)), ((), ())),
                preferred_element_type=jnp.float32,
            )
            total_sum = product if total_sum is None else total_sum + product
    return total_sum


def activate(preact, unit_count):
    return jnp.concatenate(
        [jax.nn.sigmoid(preact[:, : 3 * unit_count]), jnp.tanh(preact[:, 3 * unit_count :])],
        axis=-1,
    )


def cell_backward(grad_h, grad_cell_next, gate_values, cell_state, new_cell, unit_count):
    input_gate = gate_values[:, :unit_count]
    forget_gate = gate_values[:, unit_count : 2 * unit_count]
    output_gate = gate_values[:, 2 * unit_count : 3 * unit_count]
    candidate = gate_values[:, 3 * unit_count :]
    squash = jnp.tanh(new_cell)
    grad_cell_now = grad_cell_next + grad_h * output_gate * (1.0 - squash * squash)
    grad_pre = jnp.concatenate(
        [
            grad_cell_now * candidate * input_gate * (1.0 - input_gate),
            grad_cell_now * cell_state * forget_gate * (1.0 - forget_gate),
            grad_h * squash * output_gate * (1.0 - output_gate),
            grad_cell_now * input_gate * (1.0 - candidate * candidate),
        ],
        axis=-1,
    ).astype(jnp.bfloat16)
    return (grad_pre, grad_cell_now * forget_gate)


def conv_gates(padded, weight, bias_row, tile_rows, tile_cols):
    patches = gate_patches(padded, tile_rows, tile_cols).reshape(tile_rows * tile_cols, -1)
    return jnp.dot(patches, weight, preferred_element_type=jnp.float32) + bias_row


def store_at(buffer, value, time_slot, active):
    return jnp.where(active, lax.dynamic_update_index_in_dim(buffer, value, time_slot, 0), buffer)


def on_device(frames, cotangent, first_hidden, first_cell, gate_bias, gate_weight):
    steps_count = frames.shape[0]
    tile_rows = frames.shape[2]
    tile_cols = frames.shape[3]
    unit_count = frames.shape[4]
    cell_count = tile_rows * tile_cols
    section_count = lax.axis_size("section")
    section_index = lax.axis_index("section")
    weight = gate_weight[0]
    bias_row = gate_bias[0]
    local_frames = frames[:, 0]
    local_targets = cotangent[:, 0]
    hidden = first_hidden[0, 0]
    cell_state = first_cell[0, 0].reshape(cell_count, unit_count)
    arriving = jnp.zeros((tile_rows, tile_cols, unit_count), jnp.bfloat16)
    saved_inputs = jnp.zeros(
        (steps_count, tile_rows + 2, tile_cols + 2, 2 * unit_count), jnp.bfloat16
    )
    saved_gates = jnp.zeros((steps_count, cell_count, 4 * unit_count), jnp.float32)
    saved_old = jnp.zeros((steps_count, cell_count, unit_count), jnp.float32)
    saved_new = jnp.zeros((steps_count, cell_count, unit_count), jnp.float32)
    empty_gates = jnp.zeros((cell_count, 4 * unit_count), jnp.float32)
    for wave_step in range(steps_count + section_count - 1):
        moment = wave_step - section_index
        active = (moment >= 0) & (moment < steps_count)
        time_slot = jnp.clip(moment, 0, steps_count - 1)
        frame_now = lax.dynamic_index_in_dim(local_frames, time_slot, 0, keepdims=False)
        lower_input = jnp.where(section_index == 0, frame_now, arriving)
        joined = jnp.concatenate([lower_input, hidden], axis=-1)
        padded = with_halo(joined, (("space", 0),), 1)
        padded = jnp.pad(padded, ((0, 0), (1, 1), (0, 0)))
        preact = lax.cond(
            active,
            lambda operand: conv_gates(operand, weight, bias_row, tile_rows, tile_cols),
            lambda operand: empty_gates,
            padded,
        )
        gate_values = activate(preact, unit_count)
        new_cell = (
            gate_values[:, unit_count : 2 * unit_count] * cell_state
            + gate_values[:, :unit_count] * gate_values[:, 3 * unit_count :]
        )
        new_hidden = (
            (gate_values[:, 2 * unit_count : 3 * unit_count] * jnp.tanh(new_cell))
            .astype(jnp.bfloat16)
            .reshape(tile_rows, tile_cols, unit_count)
        )
        saved_inputs = store_at(saved_inputs, padded, time_slot, active)
        saved_gates = store_at(saved_gates, gate_values, time_slot, active)
        saved_old = store_at(saved_old, cell_state, time_slot, active)
        saved_new = store_at(saved_new, new_cell, time_slot, active)
        hidden = jnp.where(active, new_hidden, hidden)
        cell_state = jnp.where(active, new_cell, cell_state)
        leaving = jnp.where(active, new_hidden, jnp.zeros_like(new_hidden))
        arriving = passed_along(leaving, "section", 1)
    grad_hidden = jnp.zeros((tile_rows, tile_cols, unit_count), jnp.bfloat16)
    grad_cell = jnp.zeros((cell_count, unit_count), jnp.float32)
    grad_arriving = jnp.zeros((tile_rows, tile_cols, unit_count), jnp.bfloat16)
    saved_grads = jnp.zeros((steps_count, cell_count, 4 * unit_count), jnp.bfloat16)
    is_top = section_index == section_count - 1
    for wave_step in range(steps_count + section_count - 1):
        moment = steps_count - 1 - wave_step + (section_count - 1 - section_index)
        active = (moment >= 0) & (moment < steps_count)
        time_slot = jnp.clip(moment, 0, steps_count - 1)
        gate_values = lax.dynamic_index_in_dim(saved_gates, time_slot, 0, keepdims=False)
        old_cell = lax.dynamic_index_in_dim(saved_old, time_slot, 0, keepdims=False)
        new_cell = lax.dynamic_index_in_dim(saved_new, time_slot, 0, keepdims=False)
        target = lax.dynamic_index_in_dim(local_targets, time_slot, 0, keepdims=False)
        grad_h = (
            grad_arriving.astype(jnp.float32)
            + grad_hidden.astype(jnp.float32)
            + jnp.where(is_top, target.astype(jnp.float32), 0.0)
        )
        grad_h = grad_h.reshape(cell_count, unit_count)
        grad_pre, carry_cell = cell_backward(
            grad_h, grad_cell, gate_values, old_cell, new_cell, unit_count
        )
        grad_pre = jnp.where(active, grad_pre, jnp.zeros_like(grad_pre))
        saved_grads = store_at(saved_grads, grad_pre, time_slot, active)
        grad_map = grad_pre.reshape(tile_rows, tile_cols, 4 * unit_count)
        grad_pad = with_halo(grad_map, (("space", 0),), 1)
        grad_pad = jnp.pad(grad_pad, ((0, 0), (1, 1), (0, 0)))
        grad_joined = lax.cond(
            active,
            lambda operand: adjoint_conv(operand, weight, tile_rows, tile_cols),
            lambda operand: jnp.zeros((cell_count, 2 * unit_count), jnp.float32),
            grad_pad,
        )
        grad_joined = grad_joined.astype(jnp.bfloat16).reshape(tile_rows, tile_cols, 2 * unit_count)
        grad_hidden = jnp.where(active, grad_joined[..., unit_count:], grad_hidden)
        grad_cell = jnp.where(active, carry_cell, grad_cell)
        leaving = jnp.where(active, grad_joined[..., :unit_count], jnp.zeros_like(grad_hidden))
        grad_arriving = passed_along(leaving, "section", -1)
    patches_all = jnp.concatenate(
        [
            gate_patches(saved_inputs[moment], tile_rows, tile_cols).reshape(cell_count, -1)
            for moment in range(steps_count)
        ],
        axis=0,
    )
    grads_all = saved_grads.reshape(steps_count * cell_count, 4 * unit_count)
    mine = lax.psum_scatter(
        lax.dot_general(
            patches_all, grads_all, (((0,), (0,)), ((), ())), preferred_element_type=jnp.float32
        ),
        ("space", "batch"),
        scatter_dimension=0,
        tiled=True,
    )
    return mine[None]


def solution(mesh):
    return jax.shard_map(
        on_device,
        mesh=mesh,
        in_specs=(
            P(None, "batch", "space", None, None),
            P(None, "batch", "space", None, None),
            P("section", "batch", "space", None, None),
            P("section", "batch", "space", None, None),
            P("section", None),
            P("section", None, None),
        ),
        out_specs=P("section", ("space", "batch"), None),
        check_vma=False,
    )
```

profile of v0, /device:TPU:1, one launch (start us, length us, event | category | flops | bytes accessed | tf_op | source)
XLA Modules:
  0.0 363.4 jit_solution(2151800629446021783)
XLA Ops:
  6.5 0.9 select_bitcast_fusion
  8.2 3.9 %collective-permute-start = (bf16[1,32,512]{2,1,0:T(8,128)(2,1)S(1)}, bf16[1,32,512]{2,1,0:T(8,128)(2,1)S(1)}, u32[]{:S(2)}, u32[]{:S(2)}) collective-permute-start(bf16[1,32,512]{2,1,0:T(8,128)(2,1)S(1)} %get-tuple-element.320), channel_id=1, source_target_pairs={{0,2},{2,4},{4,6},{6,8},{8,10},{10,12},{12,14},{14,16},{16,18},{18... | collective-permute-start | bytes 98312 | tf_op jit(solution)/shard_map/ppermute | solution.py:15
  12.1 1.3 collective-permute-start.1
  13.4 0.9 broadcast_select_fusion
  15.1 1.7 collective-permute-done.1
  17.0 5.4 %conditional.9 = (f32[128,1024]{1,0:T(8,128)S(1)}) conditional(s32[]{:T(128)} %convert_element_type.167, () %tuple.123, (bf16[6,34,512]{2,1,0:T(8,128)(2,1)S(1)}, bf16[4608,1024]{1,0:T(8,128)(2,1)}, f32[1,1024]{1,0:T(1,128)S(1)}) %tuple.249), branch_computations={%region_0.1_spmd, %region_1.2_spmd} | conditional | flops 1208090624 | bytes 13504520 | solution.py:126
  17.3 5.1 %convolution_add_fusion = f32[128,1024]{1,0:T(8,128)S(1)} fusion(bf16[128,4608]{1,0:T(8,128)(2,1)S(1)} %bitcast.586, bf16[4608,1024]{1,0:T(8,128)(2,1)} %get-tuple-element.147, f32[1024]{0:T(1024)S(1)} %bitcast.672), kind=kOutput, calls=%fused_computation | convolution fusion | flops 1208090624 | bytes 11145216 | tf_op jit(solution)/shard_map/cond/branch_1_fun/dot_general | solution.py:88
  23.4 1.3 collective-permute-start.2
  24.7 1.3 collective-permute-done.2
  26.1 3.1 collective-permute-start.3
  29.2 1.3 collective-permute-start.4
  30.7 3.2 collective-permute-done.4
  33.9 5.7 %conditional.10 = (f32[128,256]{1,0:T(8,128)S(1)}, f32[128,768]{1,0:T(8,128)S(1)}) conditional(s32[]{:T(128)} %convert_element_type.169, () %tuple.125, (bf16[6,34,512]{2,1,0:T(8,128)(2,1)S(1)}, bf16[4608,1024]{1,0:T(8,128)(2,1)}, f32[1,1024]{1,0:T(1,128)S(1)}) %tuple.250), branch_computations={%region_2.3_spmd, %region_3.4_spmd} | conditional | flops 1208188928 | bytes 14553104 | solution.py:126
  34.3 5.2 %convolution_add_fusion.1 = f32[128,1024]{1,0:T(8,128)S(1)} fusion(bf16[128,4608]{1,0:T(8,128)(2,1)S(1)} %bitcast.587, bf16[4608,1024]{1,0:T(8,128)(2,1)} %get-tuple-element.150, f32[1024]{0:T(1024)S(1)} %bitcast.673), kind=kOutput, calls=%fused_computation.10 | convolution fusion | flops 1208090624 | bytes 11145216 | tf_op jit(solution)/shard_map/cond/branch_1_fun/dot_general | solution.py:88
  40.5 3.7 %collective-permute-start.5 = (bf16[4,32,256]{2,1,0:T(8,128)(2,1)S(1)}, bf16[4,32,256]{2,1,0:T(8,128)(2,1)S(1)}, u32[]{:S(2)}, u32[]{:S(2)}) collective-permute-start(bf16[4,32,256]{2,1,0:T(8,128)(2,1)S(1)} %get-tuple-element.326), channel_id=1, source_target_pairs={{0,32},{32,64},{64,96},{1,33},{33,65},{65,97},{2,34},{34,66},{66,9... | collective-permute-start | bytes 196616 | tf_op jit(solution)/shard_map/ppermute | solution.py:27
  44.3 1.2 collective-permute-done.5
  45.5 4.7 %collective-permute-start.6 = (bf16[1,32,512]{2,1,0:T(8,128)(2,1)S(1)}, bf16[1,32,512]{2,1,0:T(8,128)(2,1)S(1)}, u32[]{:S(2)}, u32[]{:S(2)}) collective-permute-start(bf16[1,32,512]{2,1,0:T(8,128)(2,1)S(1)} %get-tuple-element.316), channel_id=1, source_target_pairs={{0,2},{2,4},{4,6},{6,8},{8,10},{10,12},{12,14},{14,16},{16,18},{18... | collective-permute-start | bytes 98312 | tf_op jit(solution)/shard_map/ppermute | solution.py:15
  50.3 1.3 collective-permute-start.7
  51.7 3.2 collective-permute-done.7
  55.1 1.0 fusion.98
  56.2 9.3 %collective-permute-start.8 = (bf16[4,32,256]{2,1,0:T(8,128)(2,1)S(1)}, bf16[4,32,256]{2,1,0:T(8,128)(2,1)S(1)}, u32[]{:S(2)}, u32[]{:S(2)}) collective-permute-start(bf16[4,32,256]{2,1,0:T(8,128)(2,1)S(1)} %get-tuple-element.324), channel_id=1, source_target_pairs={{0,32},{32,64},{64,96},{1,33},{33,65},{65,97},{2,34},{34,66},{66,9... | collective-permute-start | bytes 196616 | tf_op jit(solution)/shard_map/ppermute | solution.py:27
  65.6 1.2 collective-permute-done.8
  66.9 4.4 %collective-permute-start.9 = (bf16[1,32,512]{2,1,0:T(8,128)(2,1)S(1)}, bf16[1,32,512]{2,1,0:T(8,128)(2,1)S(1)}, u32[]{:S(2)}, u32[]{:S(2)}) collective-permute-start(bf16[1,32,512]{2,1,0:T(8,128)(2,1)S(1)} %get-tuple-element.314), channel_id=1, source_target_pairs={{0,2},{2,4},{4,6},{6,8},{8,10},{10,12},{12,14},{14,16},{16,18},{18... | collective-permute-start | bytes 98312 | tf_op jit(solution)/shard_map/ppermute | solution.py:15
  71.3 1.3 collective-permute-start.10
  72.7 3.2 collective-permute-done.10
  76.3 3.7 %collective-permute-start.11 = (bf16[4,32,256]{2,1,0:T(8,128)(2,1)S(1)}, bf16[4,32,256]{2,1,0:T(8,128)(2,1)S(1)}, u32[]{:S(2)}, u32[]{:S(2)}) collective-permute-start(bf16[4,32,256]{2,1,0:T(8,128)(2,1)S(1)} %get-tuple-element.322), channel_id=1, source_target_pairs={{0,32},{32,64},{64,96},{1,33},{33,65},{65,97},{2,34},{34,66},{66,9... | collective-permute-start | bytes 196616 | tf_op jit(solution)/shard_map/ppermute | solution.py:27
  80.1 1.2 collective-permute-done.11
  81.4 4.0 %collective-permute-start.12 = (bf16[1,32,512]{2,1,0:T(8,128)(2,1)S(1)}, bf16[1,32,512]{2,1,0:T(8,128)(2,1)S(1)}, u32[]{:S(2)}, u32[]{:S(2)}) collective-permute-start(bf16[1,32,512]{2,1,0:T(8,128)(2,1)S(1)} %get-tuple-element.312), channel_id=1, source_target_pairs={{0,2},{2,4},{4,6},{6,8},{8,10},{10,12},{12,14},{14,16},{16,18},{18... | collective-permute-start | bytes 98312 | tf_op jit(solution)/shard_map/ppermute | solution.py:15
  85.4 1.3 collective-permute-start.13
  86.8 3.2 collective-permute-done.13
  97.4 1.2 dynamic-slice_bitcast_fusion
  98.9 4.2 %collective-permute-start.14 = (bf16[1,32,1024]{2,1,0:T(8,128)(2,1)S(1)}, bf16[1,32,1024]{2,1,0:T(8,128)(2,1)S(1)}, u32[]{:S(2)}, u32[]{:S(2)}) collective-permute-start(bf16[1,32,1024]{2,1,0:T(8,128)(2,1)S(1)} %get-tuple-element.310), channel_id=1, source_target_pairs={{0,2},{2,4},{4,6},{6,8},{8,10},{10,12},{12,14},{14,16},{16,18},{18... | collective-permute-start | bytes 196616 | tf_op jit(solution)/shard_map/ppermute | solution.py:15
  103.0 1.3 collective-permute-start.15
  104.4 3.6 %collective-permute-done.15 = bf16[1,32,1024]{2,1,0:T(8,128)(2,1)S(1)} collective-permute-done((bf16[1,32,1024]{2,1,0:T(8,128)(2,1)S(1)}, bf16[1,32,1024]{2,1,0:T(8,128)(2,1)S(1)}, u32[]{:S(2)}, u32[]{:S(2)}) %collective-permute-start.15) | collective-permute-done | bytes 65568 | tf_op jit(solution)/shard_map/ppermute | solution.py:17
  108.1 1.3 conditional.14
  109.4 1.4 collective-permute-start.16
  111.0 8.0 %collective-permute-done.16 = bf16[4,32,256]{2,1,0:T(8,128)(2,1)S(1)} collective-permute-done((bf16[4,32,256]{2,1,0:T(8,128)(2,1)S(1)}, bf16[4,32,256]{2,1,0:T(8,128)(2,1)S(1)}, u32[]{:S(2)}, u32[]{:S(2)}) %collective-permute-start.16) | collective-permute-done | bytes 65568 | tf_op jit(solution)/shard_map/ppermute | solution.py:27
  119.3 4.0 %collective-permute-start.17 = (bf16[1,32,1024]{2,1,0:T(8,128)(2,1)S(1)}, bf16[1,32,1024]{2,1,0:T(8,128)(2,1)S(1)}, u32[]{:S(2)}, u32[]{:S(2)}) collective-permute-start(bf16[1,32,1024]{2,1,0:T(8,128)(2,1)S(1)} %get-tuple-element.308), channel_id=1, source_target_pairs={{0,2},{2,4},{4,6},{6,8},{8,10},{10,12},{12,14},{14,16},{16,18},{18... | collective-permute-start | bytes 196616 | tf_op jit(solution)/shard_map/ppermute | solution.py:15
  123.3 1.3 collective-permute-start.18
  124.7 3.6 %collective-permute-done.18 = bf16[1,32,1024]{2,1,0:T(8,128)(2,1)S(1)} collective-permute-done((bf16[1,32,1024]{2,1,0:T(8,128)(2,1)S(1)}, bf16[1,32,1024]{2,1,0:T(8,128)(2,1)S(1)}, u32[]{:S(2)}, u32[]{:S(2)}) %collective-permute-start.18) | collective-permute-done | bytes 65568 | tf_op jit(solution)/shard_map/ppermute | solution.py:17
  128.5 1.3 collective-permute-start.19
  129.8 1.0 fusion.32
  130.8 3.0 collective-permute-done.19
  133.8 1.5 bitcast_add_fusion.2
  135.3 1.6 multiply_convert_fusion.5
  137.0 3.8 %collective-permute-start.20 = (bf16[1,32,1024]{2,1,0:T(8,128)(2,1)S(1)}, bf16[1,32,1024]{2,1,0:T(8,128)(2,1)S(1)}, u32[]{:S(2)}, u32[]{:S(2)}) collective-permute-start(bf16[1,32,1024]{2,1,0:T(8,128)(2,1)S(1)} %get-tuple-element.306), channel_id=1, source_target_pairs={{0,2},{2,4},{4,6},{6,8},{8,10},{10,12},{12,14},{14,16},{16,18},{18... | collective-permute-start | bytes 196616 | tf_op jit(solution)/shard_map/ppermute | solution.py:15
  140.8 1.3 collective-permute-start.21
  142.2 3.6 %collective-permute-done.21 = bf16[1,32,1024]{2,1,0:T(8,128)(2,1)S(1)} collective-permute-done((bf16[1,32,1024]{2,1,0:T(8,128)(2,1)S(1)}, bf16[1,32,1024]{2,1,0:T(8,128)(2,1)S(1)}, u32[]{:S(2)}, u32[]{:S(2)}) %collective-permute-start.21) | collective-permute-done | bytes 65568 | tf_op jit(solution)/shard_map/ppermute | solution.py:17
  146.2 1.4 collective-permute-start.22
  147.8 32.8 %collective-permute-done.22 = bf16[4,32,256]{2,1,0:T(8,128)(2,1)S(1)} collective-permute-done((bf16[4,32,256]{2,1,0:T(8,128)(2,1)S(1)}, bf16[4,32,256]{2,1,0:T(8,128)(2,1)S(1)}, u32[]{:S(2)}, u32[]{:S(2)}) %collective-permute-start.22) | collective-permute-done | bytes 65568 | tf_op jit(solution)/shard_map/ppermute | solution.py:27
  180.6 0.9 bitcast_add_fusion.1
  181.7 4.0 %collective-permute-start.23 = (bf16[1,32,1024]{2,1,0:T(8,128)(2,1)S(1)}, bf16[1,32,1024]{2,1,0:T(8,128)(2,1)S(1)}, u32[]{:S(2)}, u32[]{:S(2)}) collective-permute-start(bf16[1,32,1024]{2,1,0:T(8,128)(2,1)S(1)} %get-tuple-element.304), channel_id=1, source_target_pairs={{0,2},{2,4},{4,6},{6,8},{8,10},{10,12},{12,14},{14,16},{16,18},{18... | collective-permute-start | bytes 196616 | tf_op jit(solution)/shard_map/ppermute | solution.py:15
  185.8 1.3 collective-permute-start.24
  187.1 3.7 %collective-permute-done.24 = bf16[1,32,1024]{2,1,0:T(8,128)(2,1)S(1)} collective-permute-done((bf16[1,32,1024]{2,1,0:T(8,128)(2,1)S(1)}, bf16[1,32,1024]{2,1,0:T(8,128)(2,1)S(1)}, u32[]{:S(2)}, u32[]{:S(2)}) %collective-permute-start.24) | collective-permute-done | bytes 65568 | tf_op jit(solution)/shard_map/ppermute | solution.py:17
  190.9 10.5 %conditional.17 = (bf16[4,32,256]{2,1,0:T(8,128)(2,1)S(1)}, bf16[4,32,256]{2,1,0:T(8,128)(2,1)S(1)}) conditional(s32[]{:T(128)} %convert_element_type.169, () %tuple.139, (bf16[6,32,1024]{2,1,0:T(8,128)(2,1)S(1)}, bf16[1,4608,1024]{2,1,0:T(8,128)(2,1)}, bf16[]{:T(256)}) %tuple.140), branch_computations={%region_16.17_spmd, %region_17.18_spmd} | conditional | flops 1208549376 | bytes 57671728 | solution.py:177
  191.2 1.9 fusion.11
  193.1 2.3 convolution_add_fusion.36
  195.4 1.7 convolution_add_fusion.35
  197.1 1.7 convolution_add_fusion.34
  201.4 1.4 collective-permute-start.25
  202.9 3.6 collective-permute-done.25
  206.9 1.0 copy-done.7
  207.9 9.1 %fusion.12 = f32[4608,1024]{1,0:T(8,128)} fusion(bf16[256,1024]{1,0:T(8,128)(2,1)S(1)} %bitcast.585, bf16[128,4608]{1,0:T(8,128)(2,1)} %bitcast.110, bf16[128,4608]{1,0:T(8,128)(2,1)S(1)} %bitcast.591), kind=kOutput, calls=%fused_computation.162 | convolution fusion | flops 2420637696 | bytes 21757952 | tf_op jit(solution)/shard_map/dot_general | solution.py:197
  217.0 139.6 %reduce-scatter.2.cloned.1.call-done = f32[144,1024]{1,0:T(8,128)} async-done(((f32[4608,1024]{1,0:T(8,128)}), f32[144,1024]{1,0:T(8,128)}) %reduce-scatter.2.cloned.1.call-update) | async-done | bytes 589840 | tf_op jit(solution)/shard_map/reduce_scatter | solution.py:196
  (205 shorter events, 19.3 us)
Async XLA Ops:
  6.5 10.3 %copy-start.20 = (bf16[1,1,4,32,256]{4,3,2,1,0:T(8,128)(2,1)S(1)}, bf16[1,1,4,32,256]{4,3,2,1,0:T(8,128)(2,1)}, u32[]{:S(2)}) copy-start(bf16[1,1,4,32,256]{4,3,2,1,0:T(8,128)(2,1)} %param.26) | copy-start | bytes 196612
  6.5 7.9 %copy-start.13 = (bf16[2,1,4,32,256]{4,3,2,1,0:T(8,128)(2,1)S(1)}, bf16[2,1,4,32,256]{4,3,2,1,0:T(8,128)(2,1)}, u32[]{:S(2)}) copy-start(bf16[2,1,4,32,256]{4,3,2,1,0:T(8,128)(2,1)} %param.25) | copy-start | bytes 393220
  6.5 350.1 %reduce-scatter.2.cloned.1.call-start = ((), (), s32[]{:S(2)}) async-start(), calls=%async_computation.1 | async-start | bytes 19464192 | tf_op jit(solution)/shard_map/reduce_scatter | solution.py:196
  7.4 9.5 %copy-start.24 = (f32[1,1024]{1,0:T(1,128)S(1)}, f32[1,1024]{1,0:T(1,128)}, u32[]{:S(2)}) copy-start(f32[1,1024]{1,0:T(1,128)} %param.28) | copy-start | bytes 12292
  8.2 6.9 %collective-permute-start = (bf16[1,32,512]{2,1,0:T(8,128)(2,1)S(1)}, bf16[1,32,512]{2,1,0:T(8,128)(2,1)S(1)}, u32[]{:S(2)}, u32[]{:S(2)}) collective-permute-start(bf16[1,32,512]{2,1,0:T(8,128)(2,1)S(1)} %get-tuple-element.320), channel_id=1, source_target_pairs={{0,2},{2,4},{4,6},{6,8},{8,10},{10,12},{12,14},{14,16},{16,18},{18... | collective-permute-start | bytes 98312 | tf_op jit(solution)/shard_map/ppermute | solution.py:15
  12.1 4.7 %collective-permute-start.1 = (bf16[1,32,512]{2,1,0:T(8,128)(2,1)S(1)}, bf16[1,32,512]{2,1,0:T(8,128)(2,1)S(1)}, u32[]{:S(2)}, u32[]{:S(2)}) collective-permute-start(bf16[1,32,512]{2,1,0:T(8,128)(2,1)S(1)} %get-tuple-element.321), channel_id=1, source_target_pairs={{2,0},{4,2},{6,4},{8,6},{10,8},{12,10},{14,12},{16,14},{18,16},{20... | collective-permute-start | bytes 98312 | tf_op jit(solution)/shard_map/ppermute | solution.py:17
  22.4 0.9 copy-start.22
  22.5 3.5 copy-start.10
  23.4 2.6 collective-permute-start.2
  26.1 4.6 %collective-permute-start.3 = (bf16[1,32,512]{2,1,0:T(8,128)(2,1)S(1)}, bf16[1,32,512]{2,1,0:T(8,128)(2,1)S(1)}, u32[]{:S(2)}, u32[]{:S(2)}) collective-permute-start(bf16[1,32,512]{2,1,0:T(8,128)(2,1)S(1)} %get-tuple-element.318), channel_id=1, source_target_pairs={{0,2},{2,4},{4,6},{6,8},{8,10},{10,12},{12,14},{14,16},{16,18},{18... | collective-permute-start | bytes 98312 | tf_op jit(solution)/shard_map/ppermute | solution.py:15
  29.2 4.7 %collective-permute-start.4 = (bf16[1,32,512]{2,1,0:T(8,128)(2,1)S(1)}, bf16[1,32,512]{2,1,0:T(8,128)(2,1)S(1)}, u32[]{:S(2)}, u32[]{:S(2)}) collective-permute-start(bf16[1,32,512]{2,1,0:T(8,128)(2,1)S(1)} %get-tuple-element.319), channel_id=1, source_target_pairs={{2,0},{4,2},{6,4},{8,6},{10,8},{12,10},{14,12},{16,14},{18,16},{20... | collective-permute-start | bytes 98312 | tf_op jit(solution)/shard_map/ppermute | solution.py:17
  40.5 5.0 %collective-permute-start.5 = (bf16[4,32,256]{2,1,0:T(8,128)(2,1)S(1)}, bf16[4,32,256]{2,1,0:T(8,128)(2,1)S(1)}, u32[]{:S(2)}, u32[]{:S(2)}) collective-permute-start(bf16[4,32,256]{2,1,0:T(8,128)(2,1)S(1)} %get-tuple-element.326), channel_id=1, source_target_pairs={{0,32},{32,64},{64,96},{1,33},{33,65},{65,97},{2,34},{34,66},{66,9... | collective-permute-start | bytes 196616 | tf_op jit(solution)/shard_map/ppermute | solution.py:27
  45.5 6.1 %collective-permute-start.6 = (bf16[1,32,512]{2,1,0:T(8,128)(2,1)S(1)}, bf16[1,32,512]{2,1,0:T(8,128)(2,1)S(1)}, u32[]{:S(2)}, u32[]{:S(2)}) collective-permute-start(bf16[1,32,512]{2,1,0:T(8,128)(2,1)S(1)} %get-tuple-element.316), channel_id=1, source_target_pairs={{0,2},{2,4},{4,6},{6,8},{8,10},{10,12},{12,14},{14,16},{16,18},{18... | collective-permute-start | bytes 98312 | tf_op jit(solution)/shard_map/ppermute | solution.py:15
  50.3 4.7 %collective-permute-start.7 = (bf16[1,32,512]{2,1,0:T(8,128)(2,1)S(1)}, bf16[1,32,512]{2,1,0:T(8,128)(2,1)S(1)}, u32[]{:S(2)}, u32[]{:S(2)}) collective-permute-start(bf16[1,32,512]{2,1,0:T(8,128)(2,1)S(1)} %get-tuple-element.317), channel_id=1, source_target_pairs={{2,0},{4,2},{6,4},{8,6},{10,8},{12,10},{14,12},{16,14},{18,16},{20... | collective-permute-start | bytes 98312 | tf_op jit(solution)/shard_map/ppermute | solution.py:17
  56.1 10.7 %copy-start.11 = (bf16[2,1,4,32,256]{4,3,2,1,0:T(8,128)(2,1)S(1)}, bf16[2,1,4,32,256]{4,3,2,1,0:T(8,128)(2,1)}, u32[]{:S(2)}) copy-start(bf16[2,1,4,32,256]{4,3,2,1,0:T(8,128)(2,1)} %param.24) | copy-start | bytes 393220
  56.2 10.6 %collective-permute-start.8 = (bf16[4,32,256]{2,1,0:T(8,128)(2,1)S(1)}, bf16[4,32,256]{2,1,0:T(8,128)(2,1)S(1)}, u32[]{:S(2)}, u32[]{:S(2)}) collective-permute-start(bf16[4,32,256]{2,1,0:T(8,128)(2,1)S(1)} %get-tuple-element.324), channel_id=1, source_target_pairs={{0,32},{32,64},{64,96},{1,33},{33,65},{65,97},{2,34},{34,66},{66,9... | collective-permute-start | bytes 196616 | tf_op jit(solution)/shard_map/ppermute | solution.py:27
  66.9 5.9 %collective-permute-start.9 = (bf16[1,32,512]{2,1,0:T(8,128)(2,1)S(1)}, bf16[1,32,512]{2,1,0:T(8,128)(2,1)S(1)}, u32[]{:S(2)}, u32[]{:S(2)}) collective-permute-start(bf16[1,32,512]{2,1,0:T(8,128)(2,1)S(1)} %get-tuple-element.314), channel_id=1, source_target_pairs={{0,2},{2,4},{4,6},{6,8},{8,10},{10,12},{12,14},{14,16},{16,18},{18... | collective-permute-start | bytes 98312 | tf_op jit(solution)/shard_map/ppermute | solution.py:15
  71.3 4.7 %collective-permute-start.10 = (bf16[1,32,512]{2,1,0:T(8,128)(2,1)S(1)}, bf16[1,32,512]{2,1,0:T(8,128)(2,1)S(1)}, u32[]{:S(2)}, u32[]{:S(2)}) collective-permute-start(bf16[1,32,512]{2,1,0:T(8,128)(2,1)S(1)} %get-tuple-element.315), channel_id=1, source_target_pairs={{2,0},{4,2},{6,4},{8,6},{10,8},{12,10},{14,12},{16,14},{18,16},{20... | collective-permute-start | bytes 98312 | tf_op jit(solution)/shard_map/ppermute | solution.py:17
  76.2 5.1 %copy-start.12 = (bf16[2,1,4,32,256]{4,3,2,1,0:T(8,128)(2,1)S(1)}, bf16[2,1,4,32,256]{4,3,2,1,0:T(8,128)(2,1)}, u32[]{:S(2)}) copy-start(bf16[2,1,4,32,256]{4,3,2,1,0:T(8,128)(2,1)} %param.24) | copy-start | bytes 393220
  76.3 5.0 %collective-permute-start.11 = (bf16[4,32,256]{2,1,0:T(8,128)(2,1)S(1)}, bf16[4,32,256]{2,1,0:T(8,128)(2,1)S(1)}, u32[]{:S(2)}, u32[]{:S(2)}) collective-permute-start(bf16[4,32,256]{2,1,0:T(8,128)(2,1)S(1)} %get-tuple-element.322), channel_id=1, source_target_pairs={{0,32},{32,64},{64,96},{1,33},{33,65},{65,97},{2,34},{34,66},{66,9... | collective-permute-start | bytes 196616 | tf_op jit(solution)/shard_map/ppermute | solution.py:27
  81.4 5.5 %collective-permute-start.12 = (bf16[1,32,512]{2,1,0:T(8,128)(2,1)S(1)}, bf16[1,32,512]{2,1,0:T(8,128)(2,1)S(1)}, u32[]{:S(2)}, u32[]{:S(2)}) collective-permute-start(bf16[1,32,512]{2,1,0:T(8,128)(2,1)S(1)} %get-tuple-element.312), channel_id=1, source_target_pairs={{0,2},{2,4},{4,6},{6,8},{8,10},{10,12},{12,14},{14,16},{16,18},{18... | collective-permute-start | bytes 98312 | tf_op jit(solution)/shard_map/ppermute | solution.py:15
  85.4 4.7 %collective-permute-start.13 = (bf16[1,32,512]{2,1,0:T(8,128)(2,1)S(1)}, bf16[1,32,512]{2,1,0:T(8,128)(2,1)S(1)}, u32[]{:S(2)}, u32[]{:S(2)}) collective-permute-start(bf16[1,32,512]{2,1,0:T(8,128)(2,1)S(1)} %get-tuple-element.313), channel_id=1, source_target_pairs={{2,0},{4,2},{6,4},{8,6},{10,8},{12,10},{14,12},{16,14},{18,16},{20... | collective-permute-start | bytes 98312 | tf_op jit(solution)/shard_map/ppermute | solution.py:17
  91.1 5.6 %copy-start.6 = (bf16[4,32,4608]{2,1,0:T(8,128)(2,1)}, bf16[4,32,4608]{2,1,0:T(8,128)(2,1)S(1)}, u32[]{:S(2)}) copy-start(bf16[4,32,4608]{2,1,0:T(8,128)(2,1)S(1)} %slice_dynamic-update-slice_fusion.54) | copy-start | bytes 3538948
  93.3 5.4 %copy-start.23 = (f32[1,1,4,32,256]{4,3,2,1,0:T(8,128)S(1)}, f32[1,1,4,32,256]{4,3,2,1,0:T(8,128)}, u32[]{:S(2)}) copy-start(f32[1,1,4,32,256]{4,3,2,1,0:T(8,128)} %convert_select_fusion) | copy-start | bytes 393220
  96.0 12.1 %copy-start = (bf16[1,4608,1024]{2,1,0:T(8,128)(2,1)S(1)}, bf16[1,4608,1024]{2,1,0:T(8,128)(2,1)}, u32[]{:S(2)}) copy-start(bf16[1,4608,1024]{2,1,0:T(8,128)(2,1)} %param.29) | copy-start | bytes 28311556
  98.9 5.5 %collective-permute-start.14 = (bf16[1,32,1024]{2,1,0:T(8,128)(2,1)S(1)}, bf16[1,32,1024]{2,1,0:T(8,128)(2,1)S(1)}, u32[]{:S(2)}, u32[]{:S(2)}) collective-permute-start(bf16[1,32,1024]{2,1,0:T(8,128)(2,1)S(1)} %get-tuple-element.310), channel_id=1, source_target_pairs={{0,2},{2,4},{4,6},{6,8},{8,10},{10,12},{12,14},{14,16},{16,18},{18... | collective-permute-start | bytes 196616 | tf_op jit(solution)/shard_map/ppermute | solution.py:15
  103.0 5.0 %collective-permute-start.15 = (bf16[1,32,1024]{2,1,0:T(8,128)(2,1)S(1)}, bf16[1,32,1024]{2,1,0:T(8,128)(2,1)S(1)}, u32[]{:S(2)}, u32[]{:S(2)}) collective-permute-start(bf16[1,32,1024]{2,1,0:T(8,128)(2,1)S(1)} %get-tuple-element.311), channel_id=1, source_target_pairs={{2,0},{4,2},{6,4},{8,6},{10,8},{12,10},{14,12},{16,14},{18,16},{20... | collective-permute-start | bytes 196616 | tf_op jit(solution)/shard_map/ppermute | solution.py:17
  109.4 9.6 %copy-start.14 = (bf16[2,1,4,32,256]{4,3,2,1,0:T(8,128)(2,1)S(1)}, bf16[2,1,4,32,256]{4,3,2,1,0:T(8,128)(2,1)}, u32[]{:S(2)}) copy-start(bf16[2,1,4,32,256]{4,3,2,1,0:T(8,128)(2,1)} %param.25) | copy-start | bytes 393220
  109.4 9.7 %copy-start.4 = (f32[128,1024]{1,0:T(8,128)S(1)}, f32[128,1024]{1,0:T(8,128)}, u32[]{:S(2)}) copy-start(f32[128,1024]{1,0:T(8,128)} %get-tuple-element.282) | copy-start | bytes 1572868
  109.4 9.6 %collective-permute-start.16 = (bf16[4,32,256]{2,1,0:T(8,128)(2,1)S(1)}, bf16[4,32,256]{2,1,0:T(8,128)(2,1)S(1)}, u32[]{:S(2)}, u32[]{:S(2)}) collective-permute-start(bf16[4,32,256]{2,1,0:T(8,128)(2,1)S(1)} %broadcast_select_fusion.2), channel_id=1, source_target_pairs={{32,0},{64,32},{96,64},{33,1},{65,33},{97,65},{34,2},{66,34},{98,6... | collective-permute-start | bytes 196616 | tf_op jit(solution)/shard_map/ppermute | solution.py:27
  119.1 9.3 %copy-start.8 = (bf16[128,256]{1,0:T(8,128)(2,1)}, bf16[128,256]{1,0:T(8,128)(2,1)S(1)}, u32[]{:S(2)}) copy-start(bf16[128,256]{1,0:T(8,128)(2,1)S(1)} %get-tuple-element.221) | copy-start | bytes 196612
  119.2 9.3 %copy-start.9 = (bf16[128,256]{1,0:T(8,128)(2,1)}, bf16[128,256]{1,0:T(8,128)(2,1)S(1)}, u32[]{:S(2)}) copy-start(bf16[128,256]{1,0:T(8,128)(2,1)S(1)} %get-tuple-element.287) | copy-start | bytes 196612
  119.3 5.4 %collective-permute-start.17 = (bf16[1,32,1024]{2,1,0:T(8,128)(2,1)S(1)}, bf16[1,32,1024]{2,1,0:T(8,128)(2,1)S(1)}, u32[]{:S(2)}, u32[]{:S(2)}) collective-permute-start(bf16[1,32,1024]{2,1,0:T(8,128)(2,1)S(1)} %get-tuple-element.308), channel_id=1, source_target_pairs={{0,2},{2,4},{4,6},{6,8},{8,10},{10,12},{12,14},{14,16},{16,18},{18... | collective-permute-start | bytes 196616 | tf_op jit(solution)/shard_map/ppermute | solution.py:15
  123.3 5.0 %collective-permute-start.18 = (bf16[1,32,1024]{2,1,0:T(8,128)(2,1)S(1)}, bf16[1,32,1024]{2,1,0:T(8,128)(2,1)S(1)}, u32[]{:S(2)}, u32[]{:S(2)}) collective-permute-start(bf16[1,32,1024]{2,1,0:T(8,128)(2,1)S(1)} %get-tuple-element.309), channel_id=1, source_target_pairs={{2,0},{4,2},{6,4},{8,6},{10,8},{12,10},{14,12},{16,14},{18,16},{20... | collective-permute-start | bytes 196616 | tf_op jit(solution)/shard_map/ppermute | solution.py:17
  128.5 5.3 %collective-permute-start.19 = (bf16[4,32,256]{2,1,0:T(8,128)(2,1)S(1)}, bf16[4,32,256]{2,1,0:T(8,128)(2,1)S(1)}, u32[]{:S(2)}, u32[]{:S(2)}) collective-permute-start(bf16[4,32,256]{2,1,0:T(8,128)(2,1)S(1)} %broadcast_select_fusion.6), channel_id=1, source_target_pairs={{32,0},{64,32},{96,64},{33,1},{65,33},{97,65},{34,2},{66,34},{98,6... | collective-permute-start | bytes 196616 | tf_op jit(solution)/shard_map/ppermute | solution.py:27
  137.0 5.2 %collective-permute-start.20 = (bf16[1,32,1024]{2,1,0:T(8,128)(2,1)S(1)}, bf16[1,32,1024]{2,1,0:T(8,128)(2,1)S(1)}, u32[]{:S(2)}, u32[]{:S(2)}) collective-permute-start(bf16[1,32,1024]{2,1,0:T(8,128)(2,1)S(1)} %get-tuple-element.306), channel_id=1, source_target_pairs={{0,2},{2,4},{4,6},{6,8},{8,10},{10,12},{12,14},{14,16},{16,18},{18... | collective-permute-start | bytes 196616 | tf_op jit(solution)/shard_map/ppermute | solution.py:15
  140.8 5.0 %collective-permute-start.21 = (bf16[1,32,1024]{2,1,0:T(8,128)(2,1)S(1)}, bf16[1,32,1024]{2,1,0:T(8,128)(2,1)S(1)}, u32[]{:S(2)}, u32[]{:S(2)}) collective-permute-start(bf16[1,32,1024]{2,1,0:T(8,128)(2,1)S(1)} %get-tuple-element.307), channel_id=1, source_target_pairs={{2,0},{4,2},{6,4},{8,6},{10,8},{12,10},{14,12},{16,14},{18,16},{20... | collective-permute-start | bytes 196616 | tf_op jit(solution)/shard_map/ppermute | solution.py:17
  145.9 34.7 %copy-start.15 = (bf16[2,1,4,32,256]{4,3,2,1,0:T(8,128)(2,1)S(1)}, bf16[2,1,4,32,256]{4,3,2,1,0:T(8,128)(2,1)}, u32[]{:S(2)}) copy-start(bf16[2,1,4,32,256]{4,3,2,1,0:T(8,128)(2,1)} %param.25) | copy-start | bytes 393220
  146.2 35.4 %copy-start.18 = (bf16[4,32,256]{2,1,0:T(8,128)(2,1)}, bf16[4,32,256]{2,1,0:T(8,128)(2,1)S(1)}, u32[]{:S(2)}) copy-start(bf16[4,32,256]{2,1,0:T(8,128)(2,1)S(1)} %get-tuple-element.198) | copy-start | bytes 196612
  146.2 35.3 %copy-start.21 = (f32[128,256]{1,0:T(8,128)S(1)}, f32[128,256]{1,0:T(8,128)}, u32[]{:S(2)}) copy-start(f32[128,256]{1,0:T(8,128)} %get-tuple-element.218) | copy-start | bytes 393220
  146.2 34.3 %collective-permute-start.22 = (bf16[4,32,256]{2,1,0:T(8,128)(2,1)S(1)}, bf16[4,32,256]{2,1,0:T(8,128)(2,1)S(1)}, u32[]{:S(2)}, u32[]{:S(2)}) collective-permute-start(bf16[4,32,256]{2,1,0:T(8,128)(2,1)S(1)} %broadcast_select_fusion.11), channel_id=1, source_target_pairs={{32,0},{64,32},{96,64},{33,1},{65,33},{97,65},{34,2},{66,34},{98,6... | collective-permute-start | bytes 196616 | tf_op jit(solution)/shard_map/ppermute | solution.py:27
  181.7 5.4 %collective-permute-start.23 = (bf16[1,32,1024]{2,1,0:T(8,128)(2,1)S(1)}, bf16[1,32,1024]{2,1,0:T(8,128)(2,1)S(1)}, u32[]{:S(2)}, u32[]{:S(2)}) collective-permute-start(bf16[1,32,1024]{2,1,0:T(8,128)(2,1)S(1)} %get-tuple-element.304), channel_id=1, source_target_pairs={{0,2},{2,4},{4,6},{6,8},{8,10},{10,12},{12,14},{14,16},{16,18},{18... | collective-permute-start | bytes 196616 | tf_op jit(solution)/shard_map/ppermute | solution.py:15
  185.8 5.0 %collective-permute-start.24 = (bf16[1,32,1024]{2,1,0:T(8,128)(2,1)S(1)}, bf16[1,32,1024]{2,1,0:T(8,128)(2,1)S(1)}, u32[]{:S(2)}, u32[]{:S(2)}) collective-permute-start(bf16[1,32,1024]{2,1,0:T(8,128)(2,1)S(1)} %get-tuple-element.305), channel_id=1, source_target_pairs={{2,0},{4,2},{6,4},{8,6},{10,8},{12,10},{14,12},{16,14},{18,16},{20... | collective-permute-start | bytes 196616 | tf_op jit(solution)/shard_map/ppermute | solution.py:17
  190.8 15.7 %copy-start.16 = (bf16[2,1,4,32,256]{4,3,2,1,0:T(8,128)(2,1)S(1)}, bf16[2,1,4,32,256]{4,3,2,1,0:T(8,128)(2,1)}, u32[]{:S(2)}) copy-start(bf16[2,1,4,32,256]{4,3,2,1,0:T(8,128)(2,1)} %param.25) | copy-start | bytes 393220
  190.8 15.7 %copy-start.17 = (bf16[4,32,256]{2,1,0:T(8,128)(2,1)S(1)}, bf16[4,32,256]{2,1,0:T(8,128)(2,1)}, u32[]{:S(2)}) copy-start(bf16[4,32,256]{2,1,0:T(8,128)(2,1)} %get-tuple-element.220) | copy-start | bytes 196612
  190.9 15.7 %copy-start.19 = (bf16[4,32,256]{2,1,0:T(8,128)(2,1)S(1)}, bf16[4,32,256]{2,1,0:T(8,128)(2,1)}, u32[]{:S(2)}) copy-start(bf16[4,32,256]{2,1,0:T(8,128)(2,1)} %copy-done.18) | copy-start | bytes 196612
  190.9 7.9 %copy-start.3 = (bf16[1,4608,1024]{2,1,0:T(8,128)(2,1)S(1)}, bf16[1,4608,1024]{2,1,0:T(8,128)(2,1)}, u32[]{:S(2)}) copy-start(bf16[1,4608,1024]{2,1,0:T(8,128)(2,1)} %get-tuple-element.168) | copy-start | bytes 28311556 | tf_op jit(solution)/shard_map/cond
  201.3 5.2 %copy-start.5 = (f32[128,1024]{1,0:T(8,128)S(1)}, f32[128,1024]{1,0:T(8,128)}, u32[]{:S(2)}) copy-start(f32[128,1024]{1,0:T(8,128)} %get-tuple-element.279) | copy-start | bytes 1572868
  201.4 5.1 %collective-permute-start.25 = (bf16[4,32,256]{2,1,0:T(8,128)(2,1)S(1)}, bf16[4,32,256]{2,1,0:T(8,128)(2,1)S(1)}, u32[]{:S(2)}, u32[]{:S(2)}) collective-permute-start(bf16[4,32,256]{2,1,0:T(8,128)(2,1)S(1)} %broadcast_select_fusion.14), channel_id=1, source_target_pairs={{32,0},{64,32},{96,64},{33,1},{65,33},{97,65},{34,2},{66,34},{98,6... | collective-permute-start | bytes 196616 | tf_op jit(solution)/shard_map/ppermute | solution.py:27
  206.6 1.3 copy-start.7
Sparse Core Ops, SparseCore 0:
  217.1 139.4 reduce-scatter.1
where the time goes:
time: 365 us; the launch traced here: 363 us
  waiting for transfers between devices  221 us (61%)
  starting transfers between devices  71.4 us (20%)
  matrix products  29.4 us (8%)
  between operations  14.6 us (4%)
  other arithmetic  13.9 us (4%)
  local copies, waits for them, and re-layouts  12.1 us (3%)
    reduce_scatter x1, waiting for transfers between devices, on_device(): lax.psum_scatter(lax.dot_general(patches_all, grads_all, (((0,), (0,)), (...  140 us
    ppermute x8, waiting for transfers between devices, passed_along(): lax.ppermute(value, axis, [(source, source + steps) for source in range(f...  52.4 us
    ppermute x9, starting transfers between devices, with_halo(): lax.ppermute(tail, axis, [(i, (i + 1) % count) for i in range(ends)])  36.2 us
    ppermute x9, waiting for transfers between devices, with_halo(): lax.ppermute(head, axis, [((i + 1) % count, i) for i in range(ends)])  29.1 us
    ppermute x8, starting transfers between devices, passed_along(): lax.ppermute(value, axis, [(source, source + steps) for source in range(f...  23.5 us
    ppermute x9, starting transfers between devices, with_halo(): lax.ppermute(head, axis, [((i + 1) % count, i) for i in range(ends)])  11.6 us
    dot_general x2, matrix products, conv_gates(): jnp.dot(patches, weight, preferred_element_type=jnp.float32) + bias_row  10.3 us
    dot_general x9, matrix products, adjoint_conv(): lax.dot_general(flat_rows, kernel[row_off, col_off], (((1,), (1,)), ((),...  10.1 us
  transfers between devices with their start and end apart: 27, of which 18 were waited for; matrix products, arithmetic and copies ran while one was open for 1% of the time, Pallas kernels for 0%

commit v1 on v0

v1 whole, which is shorter than its diff:
```python
import functools

import jax
import jax.numpy as jnp
from jax import lax
from jax.experimental import pallas as pl
from jax.experimental.pallas import tpu as pltpu
from jax.sharding import PartitionSpec as P

F32 = jnp.float32
BF16 = jnp.bfloat16
MESH = pl.DeviceIdType.MESH
LINE = 4


def dot(left, right):
    return jnp.dot(left, right, preferred_element_type=F32)


def kernel(
    frames, cotangent, first_hidden, first_cell, bias, weight, out,
    wx, wh, wxt, wht, sx, sh, sg, top_hidden, preact, gates, cells, coef, gin, gx_out, ghid,
    turned, turned_all, grads_all, acc, leaving, landed,
    w_sem, sx_r, sh_r, sg_r, gx_r, pt_r, ga_r, rv_r,
    fr_s, fh_s, sx_s, sh_s, sg_s, gx_s, pt_s, ga_s, rv_s,
):
    z, s, k = lax.axis_index("section"), lax.axis_index("space"), lax.axis_index("batch")
    y, x = s // LINE, s % LINE
    sections, tiles = lax.axis_size("section"), lax.axis_size("space")
    cols = 32
    n = first_cell.shape[0]
    hid = first_cell.shape[1]
    half = hid // 2
    gate_half = 4 * half
    mid = slice(cols, cols + n)
    high, low = slice(0, cols), slice(cols + n, 2 * cols + n)
    first_row, last_row = slice(cols, 2 * cols), slice(n, cols + n)
    centre = slice(hid, 2 * hid)
    gcentre = slice(4 * hid, 8 * hid)
    top, bottom, base, roof = s == 0, s == tiles - 1, z == 0, z == sections - 1
    pending = []

    def send(pred, make):
        if pred is None:
            make().start()
            pending.append(lambda: make().wait_send())
        else:
            pl.when(pred)(lambda: make().start())
            pending.append(lambda: pl.when(pred)(lambda: make().wait_send()))

    def remote(src, dst, send_sem, recv_sem, device):
        return pltpu.make_async_remote_copy(
            src_ref=src, dst_ref=dst, send_sem=send_sem, recv_sem=recv_sem,
            device_id=device, device_id_type=MESH,
        )

    def arrived(dst, recv_sem):
        remote(dst, dst, recv_sem, recv_sem, (z, s, 1 - k)).wait_recv()

    loads = {}
    for part, buffer in ((0, wx), (1, wh)):
        for c in range(2):
            for g in range(4):
                loads[part, c, g] = pltpu.make_async_copy(
                    weight.at[:, :, part * hid:(part + 1) * hid, pl.ds(g * hid + c * half, half)],
                    buffer.at[c, :, :, :, g * half:(g + 1) * half],
                    w_sem.at[part, c, g],
                )
    for part in (1, 0):
        for c in range(2):
            for g in range(4):
                loads[part, c, g].start()

    def weights_here(part):
        for c in range(2):
            for g in range(4):
                loads[part, c, g].wait()

    partners = [(jnp.logical_not(top), (z, s - 1, k)), (jnp.logical_not(bottom), (z, s + 1, k))]
    for step, ok in ((-1, z > 0), (1, z < sections - 1)):
        partners.append((ok, (z + step, s, k)))
        partners.append((ok & (s > 0), (z + step, s - 1, k)))
        partners.append((ok & (s < tiles - 1), (z + step, s + 1, k)))
    partners.append((None, (z, s, 1 - k)))
    for d in range(1, LINE):
        for core in range(2):
            partners.append((None, (z, y * LINE + (x + d) % LINE, core)))
            partners.append((None, (z, ((y + d) % LINE) * LINE + x, core)))
    barrier = pltpu.get_barrier_semaphore()
    expected = 0
    for pred, device in partners:
        greet = functools.partial(
            pl.semaphore_signal, barrier, inc=1, device_id=device, device_id_type=MESH
        )
        if pred is None:
            greet()
            expected = expected + 1
        else:
            pl.when(pred)(greet)
            expected = expected + jnp.where(pred, 1, 0)

    sh[0, mid, centre] = first_hidden[...]

    @pl.when(base)
    def _():
        for t in range(2):
            sx[t, mid, centre] = frames[t]

    @pl.when(roof)
    def _():
        for t in range(2):
            gin[t] = cotangent[t]

    @pl.when(top)
    def _():
        for t in range(2):
            sx[t, high, :] = jnp.zeros((cols, 3 * hid), BF16)
            sh[t, high, :] = jnp.zeros((cols, 3 * hid), BF16)
            sg[t, high, :] = jnp.zeros((cols, 12 * hid), BF16)

    @pl.when(bottom)
    def _():
        for t in range(2):
            sx[t, low, :] = jnp.zeros((cols, 3 * hid), BF16)
            sh[t, low, :] = jnp.zeros((cols, 3 * hid), BF16)
            sg[t, low, :] = jnp.zeros((cols, 12 * hid), BF16)

    pl.semaphore_wait(barrier, expected)

    def send_edges(src, dst, send_sems, recv_sems, section, pred):
        up, down = s > 0, s < tiles - 1
        if pred is not None:
            up, down = up & pred, down & pred
        send(up, lambda: remote(src[0], dst[1], send_sems.at[0], recv_sems.at[1], (section, s - 1, k)))
        send(down, lambda: remote(src[1], dst[0], send_sems.at[1], recv_sems.at[0], (section, s + 1, k)))

    for t in range(2):
        send_edges(
            (sx.at[t, first_row, centre], sx.at[t, last_row, centre]),
            (sx.at[t, high, centre], sx.at[t, low, centre]),
            fr_s.at[t], sx_r.at[t], z, base,
        )
        if t == 0:
            send_edges(
                (sh.at[t, first_row, centre], sh.at[t, last_row, centre]),
                (sh.at[t, high, centre], sh.at[t, low, centre]),
                fh_s, sh_r.at[t], z, None,
            )

    def spread(buffer, t, rows, width):
        count = rows.stop - rows.start
        value = buffer[t, rows, width:2 * width].astype(F32)
        column = lax.broadcasted_iota(jnp.int32, (count, width), 0) % cols
        buffer[t, rows, 0:width] = jnp.where(
            column == 0, 0.0, pltpu.roll(value, 1, 0)
        ).astype(BF16)
        buffer[t, rows, 2 * width:3 * width] = jnp.where(
            column == cols - 1, 0.0, pltpu.roll(value, count - 1, 0)
        ).astype(BF16)

    def edges_here(buffer, t, recv_sems, width):
        @pl.when(jnp.logical_not(top))
        def _():
            arrived(buffer.at[t, high, width:2 * width], recv_sems.at[0])
            spread(buffer, t, high, width)

        @pl.when(jnp.logical_not(bottom))
        def _():
            arrived(buffer.at[t, low, width:2 * width], recv_sems.at[1])
            spread(buffer, t, low, width)

    def conv(buffer, t, weights, c):
        total = None
        for a in range(3):
            term = dot(
                buffer[t, cols * a:cols * a + n, :],
                weights[c, a].reshape(3 * hid, gate_half),
            )
            total = term if total is None else total + term
        return total

    def turn_weights(source, target):
        def one(a, carry):
            for b in range(3):
                for c in range(2):
                    start = (2 - b) * 4 * hid + c * gate_half
                    target[a, start:start + gate_half, :] = source[c, a, b].T
            return carry

        lax.fori_loop(0, 3, one, 0)

    def turn_all_weights():
        turn_weights(wh, wht)
        pl.when(jnp.logical_not(base))(lambda: turn_weights(wx, wxt))

    def turn_patches():
        block = turned.shape[3]
        for t in range(2):
            for piece in range(18):
                window, part = piece // 2, piece % 2
                a, b = window // 3, window % 3
                buffer = sh if part else sx
                flipped = buffer[t, cols * a:cols * a + n, b * hid:(b + 1) * hid].T
                at, end = piece * hid, (piece + 1) * hid
                while at < end:
                    number = at // block
                    stop = min(end, (number + 1) * block)
                    turned[t, number // LINE, number % LINE, at - number * block:stop - number * block, :] = (
                        flipped[at - piece * hid:stop - piece * hid]
                    )
                    at = stop

    def spread_to_group(pred, views, send_sems, recv_sems):
        for d in (0, 1, 3, 2):
            for c in range(2):
                there = ((x if c == 0 else y) + d) % LINE
                chip = y * LINE + there if c == 0 else there * LINE + x
                slot = 2 * (x if c == 0 else y) + k
                src, dst = views(c, there, slot)
                make = functools.partial(
                    remote, src, dst, send_sems.at[c * LINE + d], recv_sems.at[slot], (z, chip, c)
                )
                ok = pred
                if d == 0:
                    ok = (k != c) if pred is None else pred & (k != c)
                    own = (k == c) if pred is None else pred & (k == c)
                    pl.when(own)(
                        functools.partial(
                            lambda src, dst, sem: pltpu.make_async_copy(src, dst, sem).start(),
                            src, dst, recv_sems.at[slot],
                        )
                    )
                send(ok, make)

    def lanes(slot, width):
        return pl.ds(pl.multiple_of(slot * width, width), width)

    def send_patches(pred):
        for t in range(2):
            def views(c, there, slot):
                src = turned.at[t, :, there] if c == 0 else turned.at[t, there]
                return src, turned_all.at[t, :, :, lanes(slot, n)]

            spread_to_group(pred, views, pt_s.at[t], pt_r.at[t])

    def send_grads(t, pred):
        def views(c, there, slot):
            src = sg.at[t, mid, 4 * hid + c * gate_half:4 * hid + (c + 1) * gate_half]
            return src, grads_all.at[t, lanes(slot, n), :]

        spread_to_group(pred, views, ga_s.at[t], ga_r.at[t])

    @pl.when(z >= 2)
    def _():
        weights_here(1)
        weights_here(0)
        turn_all_weights()

    for t in range(2):
        spread(sh, t, mid, hid)
        edges_here(sh, t, sh_r.at[t], hid)
        if t == 0:
            pl.when(z < 2)(lambda: weights_here(1))
        for c in range(2):
            start = jnp.concatenate(
                [bias[0:1, g * hid + c * half:g * hid + (c + 1) * half] for g in range(4)], axis=1
            )
            preact[:, c * gate_half:(c + 1) * gate_half] = conv(sh, t, wh, c) + start
        pl.when(jnp.logical_not(base))(
            lambda t=t: arrived(sx.at[t, mid, centre], sx_r.at[t, 2])
        )
        spread(sx, t, mid, hid)
        edges_here(sx, t, sx_r.at[t], hid)
        if t == 0:
            pl.when(z < 2)(lambda: weights_here(0))
        for c in range(2):
            chan = slice(c * half, (c + 1) * half)
            now = preact[:, c * gate_half:(c + 1) * gate_half] + conv(sx, t, wx, c)
            i_gate = jax.nn.sigmoid(now[:, 0:half])
            f_gate = jax.nn.sigmoid(now[:, half:2 * half])
            o_gate = jax.nn.sigmoid(now[:, 2 * half:3 * half])
            cand = jnp.tanh(now[:, 3 * half:])
            old = first_cell[:, chan] if t == 0 else cells[0, :, chan]
            new = f_gate * old + i_gate * cand
            squash = jnp.tanh(new)
            hidden = (o_gate * squash).astype(BF16)
            if t == 0:
                sh[1, mid, hid + c * half:hid + (c + 1) * half] = hidden
            else:
                top_hidden[:, chan] = hidden
            cells[t, :, chan] = new
            for index, value in enumerate((i_gate, f_gate, o_gate, cand, squash)):
                gates[index, :, chan] = value
        if t == 0:
            whole = sh.at[1, mid, centre]
            ends = (sh.at[1, first_row, centre], sh.at[1, last_row, centre])
            send_edges(
                ends, (sh.at[1, high, centre], sh.at[1, low, centre]), sh_s, sh_r.at[1], z, None
            )
        else:
            whole = top_hidden
            ends = (top_hidden.at[0:cols], top_hidden.at[n - cols:n])
        send_edges(
            ends, (sx.at[t, high, centre], sx.at[t, low, centre]),
            sx_s.at[t], sx_r.at[t], z + 1, z < sections - 1,
        )
        send(
            z < sections - 1,
            lambda whole=whole, t=t: remote(
                whole, sx.at[t, mid, centre], sx_s.at[t, 2], sx_r.at[t, 2], (z + 1, s, k)
            ),
        )
        for c in range(2):
            chan = slice(c * half, (c + 1) * half)
            i_gate, f_gate, o_gate, cand, squash = (gates[index, :, chan] for index in range(5))
            old = first_cell[:, chan] if t == 0 else cells[0, :, chan]
            coef[t, 0, :, chan] = o_gate * (1.0 - squash * squash)
            coef[t, 1, :, chan] = cand * i_gate * (1.0 - i_gate)
            coef[t, 2, :, chan] = old * f_gate * (1.0 - f_gate)
            coef[t, 3, :, chan] = squash * o_gate * (1.0 - o_gate)
            coef[t, 4, :, chan] = i_gate * (1.0 - cand * cand)
            coef[t, 5, :, chan] = f_gate

    pl.when(z < 2)(turn_all_weights)
    pl.when(jnp.logical_not(roof))(turn_patches)
    send_patches(jnp.logical_not(roof))

    def back_conv(t, weights):
        total = None
        for a in (1, 0, 2):
            term = dot(sg[t, cols * (2 - a):cols * (2 - a) + n, :], weights[a])
            total = term if total is None else total + term
        return total.astype(BF16)

    for t in (1, 0):
        pl.when(jnp.logical_not(roof))(lambda t=t: arrived(gin.at[t], gx_r.at[t]))
        for c in range(2):
            chan = slice(c * half, (c + 1) * half)
            grad_h = gin[t, :, chan].astype(F32)
            if t == 0:
                grad_h = grad_h + ghid[:, chan].astype(F32)
            grad_c = grad_h * coef[t, 0, :, chan]
            if t == 0:
                grad_c = grad_c + cells[1, :, chan]
            for g, value in enumerate((
                grad_c * coef[t, 1, :, chan],
                grad_c * coef[t, 2, :, chan],
                grad_h * coef[t, 3, :, chan],
                grad_c * coef[t, 4, :, chan],
            )):
                at = 4 * hid + c * gate_half + g * half
                sg[t, mid, at:at + half] = value.astype(BF16)
            if t == 1:
                cells[1, :, chan] = grad_c * coef[t, 5, :, chan]
        send_edges(
            (sg.at[t, first_row, gcentre], sg.at[t, last_row, gcentre]),
            (sg.at[t, high, gcentre], sg.at[t, low, gcentre]),
            sg_s.at[t], sg_r.at[t], z, None if t == 1 else jnp.logical_not(base),
        )
        if t == 0:
            send_grads(t, base)

        def input_grad(t=t):
            gx_out[t] = back_conv(t, wxt)

        def widen(t=t):
            spread(sg, t, mid, 4 * hid)
            edges_here(sg, t, sg_r.at[t], 4 * hid)

        if t == 1:
            widen()
            pl.when(jnp.logical_not(base))(input_grad)
        else:
            @pl.when(jnp.logical_not(base))
            def _():
                widen()
                input_grad()

        send(
            jnp.logical_not(base),
            lambda t=t: remote(gx_out.at[t], gin.at[t], gx_s.at[t], gx_r.at[t], (z - 1, s, k)),
        )
        if t == 1:
            ghid[...] = back_conv(t, wht)
            send_grads(t, None)
        else:
            send_grads(t, jnp.logical_not(base))

    pl.when(roof)(turn_patches)
    send_patches(roof)

    rows = out.shape[0]
    me = jnp.where(k == 0, y, x)
    for t in (1, 0):
        for slot in range(2 * LINE):
            arrived(turned_all.at[t, :, :, slot * n:(slot + 1) * n], pt_r.at[t, slot])
            arrived(grads_all.at[t, slot * n:(slot + 1) * n], ga_r.at[t, slot])
        if t == 1:
            for j in range(LINE):
                acc[j] = dot(turned_all[t, j], grads_all[t])
        else:
            for d in (1, 3, 2, 0):
                j = (me + d) % LINE
                leaving[d] = (acc[j] + dot(turned_all[t, j], grads_all[t])).astype(BF16)
                chip = jnp.where(k == 0, j * LINE + x, y * LINE + j)
                for q in range(2):
                    src, dst = leaving.at[d, q * rows:(q + 1) * rows], landed.at[k, me]
                    make = functools.partial(
                        remote, src, dst, rv_s.at[d * 2 + q], rv_r.at[k, me], (z, chip, q)
                    )
                    if d == 0:
                        pl.when(k == q)(
                            lambda src=src, dst=dst: pltpu.make_async_copy(
                                src, dst, rv_r.at[k, me]
                            ).start()
                        )
                    send(k != q if d == 0 else None, make)
    for c in range(2):
        for i in range(LINE):
            arrived(landed.at[c, i], rv_r.at[c, i])
        for g in range(4):
            total = landed[c, 0, :, g * half:(g + 1) * half].astype(F32)
            for i in range(1, LINE):
                total = total + landed[c, i, :, g * half:(g + 1) * half].astype(F32)
            out[:, g * hid + c * half:g * hid + (c + 1) * half] = total
    for wait in pending:
        wait()


def on_device(frames, cotangent, first_hidden, first_cell, gate_bias, gate_weight):
    steps, _, tile_rows, cols, hid = frames.shape
    n = tile_rows * cols
    pad = n + 2 * cols
    half = hid // 2
    gates = 4 * hid
    share = 18 * hid // (lax.axis_size("space") * lax.axis_size("batch"))
    block = 2 * share
    vmem = pl.BlockSpec(memory_space=pltpu.VMEM)
    dma = pltpu.SemaphoreType.DMA
    scratch = [
        pltpu.VMEM((2, 3, 3, hid, gates // 2), BF16),
        pltpu.VMEM((2, 3, 3, hid, gates // 2), BF16),
        pltpu.VMEM((3, 3 * gates, hid), BF16),
        pltpu.VMEM((3, 3 * gates, hid), BF16),
        pltpu.VMEM((steps, pad, 3 * hid), BF16),
        pltpu.VMEM((steps, pad, 3 * hid), BF16),
        pltpu.VMEM((steps, pad, 3 * gates), BF16),
        pltpu.VMEM((n, hid), BF16),
        pltpu.VMEM((n, gates), F32),
        pltpu.VMEM((5, n, hid), F32),
        pltpu.VMEM((steps, n, hid), F32),
        pltpu.VMEM((steps, 6, n, hid), F32),
        pltpu.VMEM((steps, n, hid), BF16),
        pltpu.VMEM((steps, n, hid), BF16),
        pltpu.VMEM((n, hid), BF16),
        pltpu.VMEM((steps, LINE, LINE, block, n), BF16),
        pltpu.VMEM((steps, LINE, block, 2 * LINE * n), BF16),
        pltpu.VMEM((steps, 2 * LINE * n, gates // 2), BF16),
        pltpu.VMEM((LINE, block, gates // 2), F32),
        pltpu.VMEM((LINE, block, gates // 2), BF16),
        pltpu.VMEM((2, LINE, share, gates // 2), BF16),
        dma((2, 2, 4)),
        dma((steps, 3)), dma((steps, 2)), dma((steps, 2)), dma((steps,)),
        dma((steps, 2 * LINE)), dma((steps, 2 * LINE)), dma((2, LINE)),
        dma((steps, 2)), dma((2,)), dma((steps, 3)), dma((2,)), dma((steps, 2)), dma((steps,)),
        dma((steps, 2 * LINE)), dma((steps, 2 * LINE)), dma((2 * LINE,)),
    ]
    result = pl.pallas_call(
        kernel,
        out_shape=jax.ShapeDtypeStruct((share, gates), F32),
        in_specs=[vmem] * 5 + [pl.BlockSpec(memory_space=pl.ANY)],
        out_specs=vmem,
        scratch_shapes=scratch,
        compiler_params=pltpu.CompilerParams(
            collective_id=0, has_side_effects=True, vmem_limit_bytes=56 * 2**20
        ),
    )(
        frames.reshape(steps, n, hid),
        cotangent.reshape(steps, n, hid),
        first_hidden.reshape(n, hid),
        first_cell.reshape(n, hid),
        gate_bias,
        gate_weight.reshape(3, 3, 2 * hid, gates),
    )
    return result[None]


def solution(mesh):
    return jax.shard_map(
        on_device,
        mesh=mesh,
        in_specs=(
            P(None, "batch", "space", None, None),
            P(None, "batch", "space", None, None),
            P("section", "batch", "space", None, None),
            P("section", "batch", "space", None, None),
            P("section", None),
            P("section", None, None),
        ),
        out_specs=P("section", ("space", "batch"), None),
        check_vma=False,
    )
```

time: 365 us -> 101 us (0.28)
  waiting for transfers between devices: 221 us -> 0 us
  Pallas kernels: 0 us -> 99 us
  starting transfers between devices: 71.4 us -> 0 us
  matrix products: 29.4 us -> 0 us
  between operations: 14.6 us -> 0.01 us
  other arithmetic: 13.9 us -> 0 us
  local copies, waits for them, and re-layouts: 12.1 us -> 1.93 us
    reduce_scatter x1 -> x0, waiting for transfers between devices: 140 us -> none  [on_device(): lax.psum_scatter(lax.dot_general(patches_all, grads_all, (((0,), (0,)), (...]
    pallas_call x0 -> x1, Pallas kernels: none -> 99 us  [on_device(): pl.pallas_call(kernel, out_shape=jax.ShapeDtypeStruct((share, gates), F32...]
    ppermute x26 -> x0, waiting for transfers between devices: 81.5 us -> none  [the longest x8 52.4 us: passed_along(): lax.ppermute(value, axis, [(source, source + steps) for source in range(f...]
    ppermute x26 -> x0, starting transfers between devices: 71.4 us -> none  [the longest x9 36.2 us: with_halo(): lax.ppermute(tail, axis, [(i, (i + 1) % count) for i in range(ends)])]
    dot_general x12 -> x0, matrix products: 29.4 us -> none  [the longest x2 10.3 us: conv_gates(): jnp.dot(patches, weight, preferred_element_type=jnp.float32) + bias_row]
    select_n x47 -> x0, other arithmetic: 7.32 us -> none  [the longest x24 5.18 us: store_at(): jnp.where(active, lax.dynamic_update_index_in_dim(buffer, value, time_slo...]
    unnamed x60 -> x1, local copies, waits for them, and re-layouts: 7.64 us -> 1.93 us
  transfers between devices with their start and end apart: 27 -> 0, of which waited for: 18 -> 0; matrix products, arithmetic and copies ran while one was open for 1% -> 0% of each run, Pallas kernels for 0% -> 0%
where the time goes in v1:
time: 101 us
  Pallas kernels  99 us (98%)
  local copies, waits for them, and re-layouts  1.93 us (2%)
    pallas_call x1, Pallas kernels, on_device(): pl.pallas_call(kernel, out_shape=jax.ShapeDtypeStruct((share, gates), F32...  99 us

profile of v1, /device:TPU:1, one launch (start us, length us, event | category | flops | bytes accessed | tf_op | source)
XLA Modules:
  0.0 101.0 jit_solution(16974699221275560580)
XLA Ops:
  0.0 99.0 %shard_map.64 = f32[144,1024]{1,0:T(8,128)} custom-call(bf16[2,128,256]{2,1,0:T(8,128)(2,1)} %bitcast.8, bf16[2,128,256]{2,1,0:T(8,128)(2,1)} %bitcast.9, bf16[128,256]{1,0:T(8,128)(2,1)} %bitcast.11, f32[128,256]{1,0:T(8,128)} %bitcast.10, f32[1,1024]{1,0:T(1,128)} %bias.1, bf16[3,3,512,1024]{3,2,1,0:T(8,128)(2,1)} %bitcast.6), custom_call_target="tpu_custom_call" | custom-call | tf_op jit(solution)/shard_map/pallas_call | solution.py:468
  99.0 1.9 %copy.8 = f32[1,144,1024]{2,1,0:T(8,128)} copy(f32[1,144,1024]{2,1,0:T(8,128)} %bitcast.7) | data formatting | bytes 1179648

commit v2 on v1

v2 whole, which is shorter than its diff:
```python
import functools

import jax
import jax.numpy as jnp
from jax import lax
from jax.experimental import pallas as pl
from jax.experimental.pallas import tpu as pltpu
from jax.sharding import PartitionSpec as P

F32 = jnp.float32
BF16 = jnp.bfloat16
MESH = pl.DeviceIdType.MESH
LINE = 4


def dot(left, right):
    return jnp.dot(left, right, preferred_element_type=F32)


def kernel(
    frames, cotangent, first_hidden, first_cell, bias, weight, out,
    wx, wh, wxt, wht, sx, sh, sg, top_hidden, preact, gates, cells, carry, coef, gin, gx_out, ghid,
    tiles_all, flipped, turned, grads_all, acc, leaving, landed,
    w_sem, sx_r, sh_r, c_r, gx_r, gh_r, ti_r, ga_r, rv_r,
    fr_s, fh_s, fc_s, ct_s, sx_s, sh_s, gx_s, gh_s, ti_s, ga_s, rv_s,
):
    z, s, k = lax.axis_index("section"), lax.axis_index("space"), lax.axis_index("batch")
    y, x = s // LINE, s % LINE
    sections, tiles = lax.axis_size("section"), lax.axis_size("space")
    cols = 32
    n = first_cell.shape[0]
    hid = first_cell.shape[1]
    half = hid // 2
    gate_half = 4 * half
    own2, above2, below2 = slice(2 * cols, 2 * cols + n), slice(0, 2 * cols), slice(2 * cols + n, 4 * cols + n)
    own1, above1, below1 = slice(cols, cols + n), slice(0, cols), slice(cols + n, 2 * cols + n)
    centre = slice(hid, 2 * hid)
    top, bottom, base, roof = s == 0, s == tiles - 1, z == 0, z == sections - 1
    inner = jnp.logical_not(base)
    pending = []

    def send(pred, make):
        if pred is None:
            make().start()
            pending.append(lambda: make().wait_send())
        else:
            pl.when(pred)(lambda: make().start())
            pending.append(lambda: pl.when(pred)(lambda: make().wait_send()))

    def remote(src, dst, send_sem, recv_sem, device):
        return pltpu.make_async_remote_copy(
            src_ref=src, dst_ref=dst, send_sem=send_sem, recv_sem=recv_sem,
            device_id=device, device_id_type=MESH,
        )

    def arrived(dst, recv_sem):
        remote(dst, dst, recv_sem, recv_sem, (z, s, 1 - k)).wait_recv()

    loads = {}
    for part, buffer in ((0, wx), (1, wh)):
        for c in range(2):
            for g in range(4):
                loads[part, c, g] = pltpu.make_async_copy(
                    weight.at[:, :, part * hid:(part + 1) * hid, pl.ds(g * hid + c * half, half)],
                    buffer.at[c, :, :, :, g * half:(g + 1) * half],
                    w_sem.at[part, c, g],
                )
    for part in (1, 0):
        for c in range(2):
            for g in range(4):
                loads[part, c, g].start()

    def weights_here(part):
        for c in range(2):
            for g in range(4):
                loads[part, c, g].wait()

    partners = [(jnp.logical_not(top), (z, s - 1, k)), (jnp.logical_not(bottom), (z, s + 1, k))]
    for step, ok in ((-1, z > 0), (1, z < sections - 1)):
        partners.append((ok, (z + step, s, k)))
        partners.append((ok & (s > 0), (z + step, s - 1, k)))
        partners.append((ok & (s < tiles - 1), (z + step, s + 1, k)))
    partners.append((None, (z, s, 1 - k)))
    for d in range(1, LINE):
        for core in range(2):
            partners.append((None, (z, y * LINE + (x + d) % LINE, core)))
            partners.append((None, (z, ((y + d) % LINE) * LINE + x, core)))
    barrier = pltpu.get_barrier_semaphore()
    expected = 0
    for pred, device in partners:
        greet = functools.partial(
            pl.semaphore_signal, barrier, inc=1, device_id=device, device_id_type=MESH
        )
        if pred is None:
            greet()
            expected = expected + 1
        else:
            pl.when(pred)(greet)
            expected = expected + jnp.where(pred, 1, 0)

    sh[0, own2, centre] = first_hidden[...]
    cells[0, own1] = first_cell[...]

    @pl.when(base)
    def _():
        for t in range(2):
            sx[t, own2, centre] = frames[t]

    @pl.when(roof)
    def _():
        for t in range(2):
            gin[t, own1] = cotangent[t]

    def clear(wide, narrow):
        for t in range(2):
            sx[t, wide, :] = jnp.zeros((2 * cols, 3 * hid), BF16)
            sh[t, wide, :] = jnp.zeros((2 * cols, 3 * hid), BF16)
            gin[t, narrow] = jnp.zeros((cols, hid), BF16)
        cells[0, narrow] = jnp.zeros((cols, hid), F32)
        ghid[narrow] = jnp.zeros((cols, hid), BF16)

    pl.when(top)(lambda: clear(above2, above1))
    pl.when(bottom)(lambda: clear(below2, below1))

    pl.semaphore_wait(barrier, expected)

    def send_edges(src, dst, send_sems, recv_sems, section, pred):
        up, down = s > 0, s < tiles - 1
        if pred is not None:
            up, down = up & pred, down & pred
        send(up, lambda: remote(src[0], dst[1], send_sems.at[0], recv_sems.at[1], (section, s - 1, k)))
        send(down, lambda: remote(src[1], dst[0], send_sems.at[1], recv_sems.at[0], (section, s + 1, k)))

    def wide(buffer, t):
        return buffer.at[t, above2, centre], buffer.at[t, below2, centre]

    def outer(ref, width):
        return ref.at[0:width], ref.at[n - width:n]

    def narrow(ref):
        return ref.at[above1], ref.at[below1]

    send_edges(outer(first_hidden, 2 * cols), wide(sh, 0), fh_s, sh_r.at[0], z, None)
    for t in range(2):
        send_edges(outer(frames.at[t], 2 * cols), wide(sx, t), fr_s.at[t], sx_r.at[t], z, base)
    send_edges(outer(first_cell, cols), narrow(cells.at[0]), fc_s, c_r, z, None)
    for t in range(2):
        send_edges(outer(cotangent.at[t], cols), narrow(gin.at[t]), ct_s.at[t], gx_r.at[t], z, roof)

    def spread_value(value, width):
        count = value.shape[0]
        column = lax.broadcasted_iota(jnp.int32, (count, width), 0) % cols
        left = jnp.where(column == 0, 0.0, pltpu.roll(value, 1, 0)).astype(BF16)
        right = jnp.where(column == cols - 1, 0.0, pltpu.roll(value, count - 1, 0)).astype(BF16)
        return left, right

    def spread(buffer, t, rows, width):
        left, right = spread_value(buffer[t, rows, width:2 * width].astype(F32), width)
        buffer[t, rows, 0:width] = left
        buffer[t, rows, 2 * width:3 * width] = right

    def when_edges(first, second):
        pl.when(jnp.logical_not(top))(first)
        pl.when(jnp.logical_not(bottom))(second)

    def wide_here(buffer, t, recv_sems):
        def here(rows, index):
            arrived(buffer.at[t, rows, centre], recv_sems.at[index])
            spread(buffer, t, rows, hid)

        when_edges(lambda: here(above2, 0), lambda: here(below2, 1))

    def narrow_here(ref, recv_sems):
        when_edges(
            lambda: arrived(ref.at[above1], recv_sems.at[0]),
            lambda: arrived(ref.at[below1], recv_sems.at[1]),
        )

    def conv(buffer, t, weights, c, offsets):
        total = None
        for a in offsets:
            term = dot(
                buffer[t, cols * (a + 1):cols * (a + 1) + n, :],
                weights[c, a].reshape(3 * hid, gate_half),
            )
            total = term if total is None else total + term
        return total

    def conv_beside(t, c):
        total = None
        for buffer, weights in ((sh, wh), (sx, wx)):
            for a in range(3):
                low = cols * (a + 1) + n
                cells_in = jnp.concatenate(
                    [buffer[t, cols * a:cols * (a + 1), :], buffer[t, low:low + cols, :]], axis=0
                )
                term = dot(cells_in, weights[c, a].reshape(3 * hid, gate_half))
                total = term if total is None else total + term
        return total

    def bias_of(c):
        return jnp.concatenate(
            [bias[0:1, g * hid + c * half:g * hid + (c + 1) * half] for g in range(4)], axis=1
        )

    def activate(now, old):
        i_gate = jax.nn.sigmoid(now[:, 0:half])
        f_gate = jax.nn.sigmoid(now[:, half:2 * half])
        o_gate = jax.nn.sigmoid(now[:, 2 * half:3 * half])
        cand = jnp.tanh(now[:, 3 * half:])
        new = f_gate * old + i_gate * cand
        return i_gate, f_gate, o_gate, cand, new, jnp.tanh(new)

    def factors(i_gate, f_gate, o_gate, cand, squash, old):
        return (
            o_gate * (1.0 - squash * squash),
            cand * i_gate * (1.0 - i_gate),
            old * f_gate * (1.0 - f_gate),
            squash * o_gate * (1.0 - o_gate),
            i_gate * (1.0 - cand * cand),
            f_gate,
        )

    def turn_weights(source, target):
        def one(a, carried):
            for b in range(3):
                for c in range(2):
                    start = (2 - b) * 4 * hid + c * gate_half
                    target[a, start:start + gate_half, :] = source[c, a, b].T
            return carried

        lax.fori_loop(0, 3, one, 0)

    def turn_all_weights():
        turn_weights(wh, wht)
        pl.when(inner)(lambda: turn_weights(wx, wxt))

    def spread_to_group(pred, view, send_sems, recv_sems):
        for d in (0, 1, 3, 2):
            for c in range(2):
                there = ((x if c == 0 else y) + d) % LINE
                chip = y * LINE + there if c == 0 else there * LINE + x
                slot = 2 * (x if c == 0 else y) + k
                src, dst = view(c, slot)
                make = functools.partial(
                    remote, src, dst, send_sems.at[c * LINE + d], recv_sems.at[slot], (z, chip, c)
                )
                ok = pred
                if d == 0:
                    ok = (k != c) if pred is None else pred & (k != c)
                    own = (k == c) if pred is None else pred & (k == c)
                    pl.when(own)(
                        functools.partial(
                            lambda src, dst, sem: pltpu.make_async_copy(src, dst, sem).start(),
                            src, dst, recv_sems.at[slot],
                        )
                    )
                send(ok, make)

    def send_tile(t, part, pred):
        src = (sh if part else sx).at[t, cols:3 * cols + n, centre]
        spread_to_group(
            pred, lambda c, slot: (src, tiles_all.at[t, part, slot]), ti_s.at[t, part], ti_r.at[t, part]
        )

    def send_grads(t, pred):
        def view(c, slot):
            src = sg.at[t, own1, 4 * hid + c * gate_half:4 * hid + (c + 1) * gate_half]
            return src, grads_all.at[t, pl.ds(pl.multiple_of(slot * n, n), n), :]

        spread_to_group(pred, view, ga_s.at[t], ga_r.at[t])

    rows = out.shape[0]
    block = 2 * rows
    me = jnp.where(k == 0, y, x)

    def turn_patches():
        for t in range(2):
            for part in range(2):
                for slot in range(2 * LINE):
                    arrived(tiles_all.at[t, part, slot], ti_r.at[t, part, slot])

            def one(slot, carried):
                for part in range(2):
                    tile = tiles_all[t, part, slot]
                    left, right = spread_value(tile.astype(F32), hid)
                    for b, moved in enumerate((left, tile, right)):
                        for a in range(3):
                            at = (a * 3 + b) * 2 * hid + part * hid
                            flipped[at:at + hid, :] = moved[cols * a:cols * a + n, :].T
                for j in range(LINE):
                    chip = jnp.where(k == 0, j * LINE + x, y * LINE + j)
                    turned[t, j, :, pl.ds(pl.multiple_of(slot * n, n), n)] = flipped[
                        pl.ds(pl.multiple_of(chip * block, 32), block), :
                    ]
                return carried

            lax.fori_loop(0, 2 * LINE, one, 0)

    @pl.when(z >= 2)
    def _():
        weights_here(1)
        weights_here(0)
        turn_all_weights()

    for t in range(2):
        spread(sh, t, own2, hid)
        if t == 0:
            pl.when(z < 2)(lambda: weights_here(1))
        part_sums = [conv(sh, t, wh, c, (1,)) + bias_of(c) for c in range(2)]
        for c in range(2):
            preact[:, c * gate_half:(c + 1) * gate_half] = part_sums[c]
        wide_here(sh, t, sh_r.at[t])
        if t == 0:
            send_tile(0, 1, inner)
        for c in range(2):
            preact[:, c * gate_half:(c + 1) * gate_half] += conv(sh, t, wh, c, (0, 2))
        pl.when(inner)(lambda t=t: arrived(sx.at[t, own2, centre], sx_r.at[t, 2]))
        spread(sx, t, own2, hid)
        if t == 0:
            pl.when(z < 2)(lambda: weights_here(0))
        for c in range(2):
            preact[:, c * gate_half:(c + 1) * gate_half] += conv(sx, t, wx, c, (1,))
        wide_here(sx, t, sx_r.at[t])
        for c in range(2):
            chan = slice(c * half, (c + 1) * half)
            now = preact[:, c * gate_half:(c + 1) * gate_half] + conv(sx, t, wx, c, (0, 2))
            i_gate, f_gate, o_gate, cand, new, squash = activate(now, cells[t, own1, chan])
            hidden = (o_gate * squash).astype(BF16)
            if t == 0:
                sh[1, own2, hid + c * half:hid + (c + 1) * half] = hidden
                cells[1, own1, chan] = new
            else:
                top_hidden[:, chan] = hidden
            for index, value in enumerate((i_gate, f_gate, o_gate, cand, squash)):
                gates[index, :, chan] = value
        whole = sh.at[1, own2, centre] if t == 0 else top_hidden
        send(
            z < sections - 1,
            lambda whole=whole, t=t: remote(
                whole, sx.at[t, own2, centre], sx_s.at[t, 2], sx_r.at[t, 2], (z + 1, s, k)
            ),
        )
        if t == 0:
            ends = sh.at[1, 2 * cols:4 * cols, centre], sh.at[1, n:n + 2 * cols, centre]
            send_edges(ends, wide(sh, 1), sh_s, sh_r.at[1], z, None)
        else:
            ends = outer(top_hidden, 2 * cols)
        send_edges(ends, wide(sx, t), sx_s.at[t], sx_r.at[t], z + 1, z < sections - 1)
        if t == 0:
            narrow_here(cells.at[0], c_r)
        for c in range(2):
            chan = slice(c * half, (c + 1) * half)
            beside = jnp.concatenate([cells[t, above1, chan], cells[t, below1, chan]], axis=0)
            values = activate(conv_beside(t, c) + bias_of(c), beside)
            i_gate, f_gate, o_gate, cand, new, squash = values
            if t == 0:
                cells[1, above1, chan] = new[0:cols]
                cells[1, below1, chan] = new[cols:]
            for index, value in enumerate(factors(i_gate, f_gate, o_gate, cand, squash, beside)):
                coef[t, index, above1, chan] = value[0:cols]
                coef[t, index, below1, chan] = value[cols:]
            i_gate, f_gate, o_gate, cand, squash = (gates[index, :, chan] for index in range(5))
            for index, value in enumerate(
                factors(i_gate, f_gate, o_gate, cand, squash, cells[t, own1, chan])
            ):
                coef[t, index, own1, chan] = value

    pl.when(z < 2)(turn_all_weights)
    send_tile(0, 1, base)
    for t, part in ((0, 0), (1, 1), (1, 0)):
        send_tile(t, part, jnp.logical_not(roof))
    pl.when(z < 2)(turn_patches)

    def back_conv(t, weights):
        total = None
        for a in range(3):
            term = dot(sg[t, cols * (2 - a):cols * (2 - a) + n, :], weights[a])
            total = term if total is None else total + term
        return total.astype(BF16)

    for t in (1, 0):
        pl.when(jnp.logical_not(roof))(lambda t=t: arrived(gin.at[t, own1], gx_r.at[t, 2]))
        if t == 1:
            narrow_here(gin.at[t], gx_r.at[t])
        else:
            @pl.when(inner)
            def _():
                narrow_here(gin.at[0], gx_r.at[0])
                narrow_here(ghid, gh_r)
        for c in range(2):
            chan = slice(c * half, (c + 1) * half)
            grad_h = gin[t, :, chan].astype(F32)
            if t == 0:
                grad_h = grad_h + ghid[:, chan].astype(F32)
            grad_c = grad_h * coef[t, 0, :, chan]
            if t == 0:
                grad_c = grad_c + carry[:, chan]
            for g, value in enumerate((
                grad_c * coef[t, 1, :, chan],
                grad_c * coef[t, 2, :, chan],
                grad_h * coef[t, 3, :, chan],
                grad_c * coef[t, 4, :, chan],
            )):
                at = 4 * hid + c * gate_half + g * half
                sg[t, :, at:at + half] = value.astype(BF16)
            if t == 1:
                carry[:, chan] = grad_c * coef[t, 5, :, chan]
        send_grads(t, base)

        def widen(t=t):
            spread(sg, t, slice(0, 2 * cols + n), 4 * hid)

            @pl.when(top)
            def _():
                sg[t, above1, :] = jnp.zeros((cols, 12 * hid), BF16)

            @pl.when(bottom)
            def _():
                sg[t, below1, :] = jnp.zeros((cols, 12 * hid), BF16)

        def input_grad(t=t):
            gx_out[t] = back_conv(t, wxt)

        if t == 1:
            widen()
            pl.when(inner)(input_grad)
        else:
            @pl.when(inner)
            def _():
                widen()
                input_grad()

        send(
            inner,
            lambda t=t: remote(gx_out.at[t], gin.at[t, own1], gx_s.at[t, 2], gx_r.at[t, 2], (z - 1, s, k)),
        )
        send_edges(
            outer(gx_out.at[t], cols), narrow(gin.at[t]), gx_s.at[t], gx_r.at[t], z - 1,
            inner if t == 1 else z >= 2,
        )
        if t == 1:
            ghid[own1] = back_conv(t, wht)
            send_edges(
                (ghid.at[cols:2 * cols], ghid.at[n:n + cols]), narrow(ghid), gh_s, gh_r, z, inner
            )
        send_grads(t, inner)

    for t, part in ((0, 0), (1, 1), (1, 0)):
        send_tile(t, part, roof)
    pl.when(z >= 2)(turn_patches)

    for t in (1, 0):
        for slot in range(2 * LINE):
            arrived(grads_all.at[t, slot * n:(slot + 1) * n], ga_r.at[t, slot])
        if t == 1:
            for j in range(LINE):
                acc[j] = dot(turned[t, j], grads_all[t])
        else:
            for d in (1, 3, 2, 0):
                j = (me + d) % LINE
                leaving[d] = (acc[j] + dot(turned[t, j], grads_all[t])).astype(BF16)
                chip = jnp.where(k == 0, j * LINE + x, y * LINE + j)
                for q in range(2):
                    src, dst = leaving.at[d, q * rows:(q + 1) * rows], landed.at[k, me]
                    make = functools.partial(
                        remote, src, dst, rv_s.at[d * 2 + q], rv_r.at[k, me], (z, chip, q)
                    )
                    if d == 0:
                        pl.when(k == q)(
                            lambda src=src, dst=dst: pltpu.make_async_copy(
                                src, dst, rv_r.at[k, me]
                            ).start()
                        )
                    send(k != q if d == 0 else None, make)
    for c in range(2):
        for i in range(LINE):
            arrived(landed.at[c, i], rv_r.at[c, i])
        for g in range(4):
            total = landed[c, 0, :, g * half:(g + 1) * half].astype(F32)
            for i in range(1, LINE):
                total = total + landed[c, i, :, g * half:(g + 1) * half].astype(F32)
            out[:, g * hid + c * half:g * hid + (c + 1) * half] = total
    for wait in pending:
        wait()


def on_device(frames, cotangent, first_hidden, first_cell, gate_bias, gate_weight):
    steps, _, tile_rows, cols, hid = frames.shape
    n = tile_rows * cols
    pad = n + 2 * cols
    half = hid // 2
    gates = 4 * hid
    share = 18 * hid // (lax.axis_size("space") * lax.axis_size("batch"))
    block = 2 * share
    vmem = pl.BlockSpec(memory_space=pltpu.VMEM)
    dma = pltpu.SemaphoreType.DMA
    scratch = [
        pltpu.VMEM((2, 3, 3, hid, gates // 2), BF16),
        pltpu.VMEM((2, 3, 3, hid, gates // 2), BF16),
        pltpu.VMEM((3, 3 * gates, hid), BF16),
        pltpu.VMEM((3, 3 * gates, hid), BF16),
        pltpu.VMEM((steps, pad + 2 * cols, 3 * hid), BF16),
        pltpu.VMEM((steps, pad + 2 * cols, 3 * hid), BF16),
        pltpu.VMEM((steps, pad, 3 * gates), BF16),
        pltpu.VMEM((n, hid), BF16),
        pltpu.VMEM((n, gates), F32),
        pltpu.VMEM((5, n, hid), F32),
        pltpu.VMEM((steps, pad, hid), F32),
        pltpu.VMEM((pad, hid), F32),
        pltpu.VMEM((steps, 6, pad, hid), F32),
        pltpu.VMEM((steps, pad, hid), BF16),
        pltpu.VMEM((steps, n, hid), BF16),
        pltpu.VMEM((pad, hid), BF16),
        pltpu.VMEM((steps, 2, 2 * LINE, pad, hid), BF16),
        pltpu.VMEM((18 * hid, n), BF16),
        pltpu.VMEM((steps, LINE, block, 2 * LINE * n), BF16),
        pltpu.VMEM((steps, 2 * LINE * n, gates // 2), BF16),
        pltpu.VMEM((LINE, block, gates // 2), F32),
        pltpu.VMEM((LINE, block, gates // 2), BF16),
        pltpu.VMEM((2, LINE, share, gates // 2), BF16),
        dma((2, 2, 4)),
        dma((steps, 3)), dma((steps, 2)), dma((2,)), dma((steps, 3)), dma((2,)),
        dma((steps, 2, 2 * LINE)), dma((steps, 2 * LINE)), dma((2, LINE)),
        dma((steps, 2)), dma((2,)), dma((2,)), dma((steps, 2)),
        dma((steps, 3)), dma((2,)), dma((steps, 3)), dma((2,)),
        dma((steps, 2, 2 * LINE)), dma((steps, 2 * LINE)), dma((2 * LINE,)),
    ]
    result = pl.pallas_call(
        kernel,
        out_shape=jax.ShapeDtypeStruct((share, gates), F32),
        in_specs=[vmem] * 5 + [pl.BlockSpec(memory_space=pl.ANY)],
        out_specs=vmem,
        scratch_shapes=scratch,
        compiler_params=pltpu.CompilerParams(
            collective_id=0, has_side_effects=True, vmem_limit_bytes=56 * 2**20
        ),
    )(
        frames.reshape(steps, n, hid),
        cotangent.reshape(steps, n, hid),
        first_hidden.reshape(n, hid),
        first_cell.reshape(n, hid),
        gate_bias,
        gate_weight.reshape(3, 3, 2 * hid, gates),
    )
    return result[None]


def solution(mesh):
    return jax.shard_map(
        on_device,
        mesh=mesh,
        in_specs=(
            P(None, "batch", "space", None, None),
            P(None, "batch", "space", None, None),
            P("section", "batch", "space", None, None),
            P("section", "batch", "space", None, None),
            P("section", None),
            P("section", None, None),
        ),
        out_specs=P("section", ("space", "batch"), None),
        check_vma=False,
    )
```

time: 101 us -> 82.2 us (0.81)
  Pallas kernels: 99 us -> 80.1 us
    pallas_call x1, Pallas kernels: 99 us -> 80.1 us  [on_device(): pl.pallas_call(kernel, out_shape=jax.ShapeDtypeStruct((share, gates), F32...]
where the time goes in v2:
time: 82.2 us; the launch traced here: 82 us
  Pallas kernels  80.1 us (97%)
  local copies, waits for them, and re-layouts  1.93 us (2%)
    pallas_call x1, Pallas kernels, on_device(): pl.pallas_call(kernel, out_shape=jax.ShapeDtypeStruct((share, gates), F32...  80.1 us
    unnamed x1, local copies, waits for them, and re-layouts  1.93 us

profile of v2, /device:TPU:1, one launch (start us, length us, event | category | flops | bytes accessed | tf_op | source)
XLA Modules:
  0.0 82.0 jit_solution(4744339299037250669)
XLA Ops:
  0.0 80.1 %shard_map.64 = f32[144,1024]{1,0:T(8,128)} custom-call(bf16[2,128,256]{2,1,0:T(8,128)(2,1)} %bitcast.8, bf16[2,128,256]{2,1,0:T(8,128)(2,1)} %bitcast.9, bf16[128,256]{1,0:T(8,128)(2,1)} %bitcast.11, f32[128,256]{1,0:T(8,128)} %bitcast.10, f32[1,1024]{1,0:T(1,128)} %bias.1, bf16[3,3,512,1024]{3,2,1,0:T(8,128)(2,1)} %bitcast.6), custom_call_target="tpu_custom_call" | custom-call | tf_op jit(solution)/shard_map/pallas_call | solution.py:529
  80.1 1.9 %copy.8 = f32[1,144,1024]{2,1,0:T(8,128)} copy(f32[1,144,1024]{2,1,0:T(8,128)} %bitcast.7) | data formatting | bytes 1179648

commit v3 on v2

--- a/solution.py
+++ b/solution.py
@@ -21,8 +21,8 @@
     frames, cotangent, first_hidden, first_cell, bias, weight, out,
     wx, wh, wxt, wht, sx, sh, sg, top_hidden, preact, gates, cells, carry, coef, gin, gx_out, ghid,
     tiles_all, flipped, turned, grads_all, acc, leaving, landed,
-    w_sem, sx_r, sh_r, c_r, gx_r, gh_r, ti_r, ga_r, rv_r,
-    fr_s, fh_s, fc_s, ct_s, sx_s, sh_s, gx_s, gh_s, ti_s, ga_s, rv_s,
+    w_sem, in_sem, sx_r, sx_f, sh_r, sh_f, c_r, gx_r, gh_r, ti_r, ga_r, rv_r,
+    fr_s, fr_f, fh_s, fh_f, fc_s, ct_s, sx_s, sx_fs, sh_s, sh_fs, gx_s, gh_s, ti_s, ga_s, rv_s,
 ):
     z, s, k = lax.axis_index("section"), lax.axis_index("space"), lax.axis_index("batch")
     y, x = s // LINE, s % LINE
@@ -33,6 +33,8 @@
     half = hid // 2
     gate_half = 4 * half
     own2, above2, below2 = slice(2 * cols, 2 * cols + n), slice(0, 2 * cols), slice(2 * cols + n, 4 * cols + n)
+    near = slice(cols, 2 * cols), slice(2 * cols + n, 3 * cols + n)
+    far = slice(0, cols), slice(3 * cols + n, 4 * cols + n)
     own1, above1, below1 = slice(cols, cols + n), slice(0, cols), slice(cols + n, 2 * cols + n)
     centre = slice(hid, 2 * hid)
     top, bottom, base, roof = s == 0, s == tiles - 1, z == 0, z == sections - 1
@@ -44,8 +46,9 @@
             make().start()
             pending.append(lambda: make().wait_send())
         else:
-            pl.when(pred)(lambda: make().start())
-            pending.append(lambda: pl.when(pred)(lambda: make().wait_send()))
+            ask = pred if callable(pred) else lambda: pred
+            pl.when(ask())(lambda: make().start())
+            pending.append(lambda: pl.when(ask())(lambda: make().wait_send()))
 
     def remote(src, dst, send_sem, recv_sem, device):
         return pltpu.make_async_remote_copy(
@@ -65,10 +68,6 @@
                     buffer.at[c, :, :, :, g * half:(g + 1) * half],
                     w_sem.at[part, c, g],
                 )
-    for part in (1, 0):
-        for c in range(2):
-            for g in range(4):
-                loads[part, c, g].start()
 
     def weights_here(part):
         for c in range(2):
@@ -98,18 +97,30 @@
             pl.when(pred)(greet)
             expected = expected + jnp.where(pred, 1, 0)
 
-    sh[0, own2, centre] = first_hidden[...]
-    cells[0, own1] = first_cell[...]
+    half_lanes = [slice(hid + c * half, hid + (c + 1) * half) for c in range(2)]
+    own_hidden = pltpu.make_async_copy(first_hidden, sh.at[0, own2, centre], in_sem.at[0])
+    own_cell = pltpu.make_async_copy(first_cell, cells.at[0, own1], in_sem.at[1])
+    own_hidden.start()
 
     @pl.when(base)
     def _():
         for t in range(2):
-            sx[t, own2, centre] = frames[t]
+            for c in range(2):
+                pltpu.make_async_copy(
+                    frames.at[t, :, pl.ds(c * half, half)], sx.at[t, own2, half_lanes[c]], sx_r.at[t, c, 2]
+                ).start()
+
+    own_cell.start()
 
     @pl.when(roof)
     def _():
         for t in range(2):
-            gin[t, own1] = cotangent[t]
+            pltpu.make_async_copy(cotangent.at[t], gin.at[t, own1], gx_r.at[t, 2]).start()
+
+    for part in (1, 0):
+        for c in range(2):
+            for g in range(4):
+                loads[part, c, g].start()
 
     def clear(wide, narrow):
         for t in range(2):
@@ -125,25 +136,52 @@
     pl.semaphore_wait(barrier, expected)
 
     def send_edges(src, dst, send_sems, recv_sems, section, pred):
-        up, down = s > 0, s < tiles - 1
-        if pred is not None:
-            up, down = up & pred, down & pred
-        send(up, lambda: remote(src[0], dst[1], send_sems.at[0], recv_sems.at[1], (section, s - 1, k)))
-        send(down, lambda: remote(src[1], dst[0], send_sems.at[1], recv_sems.at[0], (section, s + 1, k)))
-
-    def wide(buffer, t):
-        return buffer.at[t, above2, centre], buffer.at[t, below2, centre]
+        edges(lambda: (src, dst, send_sems, recv_sems), section, pred)
+
+    def edges(parts, section, pred):
+        def up():
+            return s > 0 if pred is None else (s > 0) & pred
+
+        def down():
+            return s < tiles - 1 if pred is None else (s < tiles - 1) & pred
+
+        def make(end, device):
+            src, dst, send_sems, recv_sems = parts()
+            return remote(src[end], dst[1 - end], send_sems.at[end], recv_sems.at[1 - end], device)
+
+        send(up, lambda: make(0, (section, s - 1, k)))
+        send(down, lambda: make(1, (section, s + 1, k)))
 
     def outer(ref, width):
         return ref.at[0:width], ref.at[n - width:n]
 
+    def beyond(ref):
+        return ref.at[cols:2 * cols], ref.at[n - 2 * cols:n - cols]
+
     def narrow(ref):
         return ref.at[above1], ref.at[below1]
 
-    send_edges(outer(first_hidden, 2 * cols), wide(sh, 0), fh_s, sh_r.at[0], z, None)
-    for t in range(2):
-        send_edges(outer(frames.at[t], 2 * cols), wide(sx, t), fr_s.at[t], sx_r.at[t], z, base)
+    def at_rows(buffer, t, rows, lanes):
+        return buffer.at[t, rows[0], lanes], buffer.at[t, rows[1], lanes]
+
+    def halves(ref, c):
+        return ref.at[0:cols, pl.ds(c * half, half)], ref.at[n - cols:n, pl.ds(c * half, half)]
+
+    send_edges(outer(first_hidden, cols), at_rows(sh, 0, near, centre), fh_s, sh_r.at[0, 0], z, None)
+
+    def send_frames(t):
+        for c in range(2):
+            send_edges(
+                halves(frames.at[t], c), at_rows(sx, t, near, half_lanes[c]),
+                fr_s.at[t, c], sx_r.at[t, c], z, base,
+            )
+
+    send_frames(0)
+    send_edges(beyond(first_hidden), at_rows(sh, 0, far, centre), fh_f, sh_f.at[0], z, None)
     send_edges(outer(first_cell, cols), narrow(cells.at[0]), fc_s, c_r, z, None)
+    send_edges(beyond(frames.at[0]), at_rows(sx, 0, far, centre), fr_f.at[0], sx_f.at[0], z, base)
+    send_frames(1)
+    send_edges(beyond(frames.at[1]), at_rows(sx, 1, far, centre), fr_f.at[1], sx_f.at[1], z, base)
     for t in range(2):
         send_edges(outer(cotangent.at[t], cols), narrow(gin.at[t]), ct_s.at[t], gx_r.at[t], z, roof)
 
@@ -163,12 +201,20 @@
         pl.when(jnp.logical_not(top))(first)
         pl.when(jnp.logical_not(bottom))(second)
 
-    def wide_here(buffer, t, recv_sems):
-        def here(rows, index):
-            arrived(buffer.at[t, rows, centre], recv_sems.at[index])
-            spread(buffer, t, rows, hid)
-
-        when_edges(lambda: here(above2, 0), lambda: here(below2, 1))
+    def near_here(buffer, t, recv_sems, lanes):
+        def here(index):
+            for c, part in enumerate(lanes):
+                arrived(buffer.at[t, near[index], part], recv_sems.at[c, index])
+            spread(buffer, t, near[index], hid)
+
+        when_edges(lambda: here(0), lambda: here(1))
+
+    def far_here(buffer, t, recv_sems):
+        def here(index):
+            arrived(buffer.at[t, far[index], centre], recv_sems.at[index])
+            spread(buffer, t, far[index], hid)
+
+        when_edges(lambda: here(0), lambda: here(1))
 
     def narrow_here(ref, recv_sems):
         when_edges(
@@ -181,6 +227,16 @@
         for a in offsets:
             term = dot(
                 buffer[t, cols * (a + 1):cols * (a + 1) + n, :],
+                weights[c, a].reshape(3 * hid, gate_half),
+            )
+            total = term if total is None else total + term
+        return total
+
+    def conv_all(buffer, t, weights, c):
+        total = None
+        for a in range(3):
+            term = dot(
+                buffer[t, cols * a:cols * (a + 2) + n, :],
                 weights[c, a].reshape(3 * hid, gate_half),
             )
             total = term if total is None else total + term
@@ -263,12 +319,16 @@
             pred, lambda c, slot: (src, tiles_all.at[t, part, slot]), ti_s.at[t, part], ti_r.at[t, part]
         )
 
+    pairs = [slice(p * 2 * half, (p + 1) * 2 * half) for p in range(2)]
+
     def send_grads(t, pred):
-        def view(c, slot):
-            src = sg.at[t, own1, 4 * hid + c * gate_half:4 * hid + (c + 1) * gate_half]
-            return src, grads_all.at[t, pl.ds(pl.multiple_of(slot * n, n), n), :]
-
-        spread_to_group(pred, view, ga_s.at[t], ga_r.at[t])
+        for p, lanes in enumerate(pairs):
+            def view(c, slot):
+                at = 4 * hid + c * gate_half
+                src = sg.at[t, own1, at + lanes.start:at + lanes.stop]
+                return src, grads_all.at[t, pl.ds(pl.multiple_of(slot * n, n), n), lanes]
+
+            spread_to_group(pred, view, ga_s.at[t, p], ga_r.at[t, p])
 
     rows = out.shape[0]
     block = 2 * rows
@@ -303,73 +363,127 @@
         weights_here(0)
         turn_all_weights()
 
-    for t in range(2):
-        spread(sh, t, own2, hid)
-        if t == 0:
-            pl.when(z < 2)(lambda: weights_here(1))
+    not_roof = jnp.logical_not(roof)
+    z_up = z + 1
+
+    def save(t, into, values, old, chan):
+        i_gate, f_gate, o_gate, cand, squash = values
+        for index, value in enumerate(factors(i_gate, f_gate, o_gate, cand, squash, old)):
+            for cells_to, cells_from in into:
+                coef[t, index, cells_to, chan] = value[cells_from]
+
+    def x_here(t):
+        for c in range(2):
+            arrived(sx.at[t, own2, half_lanes[c]], sx_r.at[t, c, 2])
+        spread(sx, t, own2, hid)
+
+    def own_rows(t):
         part_sums = [conv(sh, t, wh, c, (1,)) + bias_of(c) for c in range(2)]
         for c in range(2):
-            preact[:, c * gate_half:(c + 1) * gate_half] = part_sums[c]
-        wide_here(sh, t, sh_r.at[t])
+            preact[0:n, c * gate_half:(c + 1) * gate_half] = part_sums[c]
+        near_here(sh, t, sh_r.at[t], (centre,) if t == 0 else half_lanes)
         if t == 0:
             send_tile(0, 1, inner)
         for c in range(2):
-            preact[:, c * gate_half:(c + 1) * gate_half] += conv(sh, t, wh, c, (0, 2))
-        pl.when(inner)(lambda t=t: arrived(sx.at[t, own2, centre], sx_r.at[t, 2]))
-        spread(sx, t, own2, hid)
+            preact[0:n, c * gate_half:(c + 1) * gate_half] += conv(sh, t, wh, c, (0, 2))
         if t == 0:
             pl.when(z < 2)(lambda: weights_here(0))
-        for c in range(2):
-            preact[:, c * gate_half:(c + 1) * gate_half] += conv(sx, t, wx, c, (1,))
-        wide_here(sx, t, sx_r.at[t])
-        for c in range(2):
-            chan = slice(c * half, (c + 1) * half)
-            now = preact[:, c * gate_half:(c + 1) * gate_half] + conv(sx, t, wx, c, (0, 2))
+        x_here(t)
+        for c in range(2):
+            preact[0:n, c * gate_half:(c + 1) * gate_half] += conv(sx, t, wx, c, (1,))
+        near_here(sx, t, sx_r.at[t], half_lanes)
+        if t == 0:
+            own_cell.wait()
+        for c in range(2):
+            chan, lanes = slice(c * half, (c + 1) * half), half_lanes[c]
+            now = preact[0:n, c * gate_half:(c + 1) * gate_half] + conv(sx, t, wx, c, (0, 2))
             i_gate, f_gate, o_gate, cand, new, squash = activate(now, cells[t, own1, chan])
             hidden = (o_gate * squash).astype(BF16)
             if t == 0:
-                sh[1, own2, hid + c * half:hid + (c + 1) * half] = hidden
+                sh[1, own2, lanes] = hidden
                 cells[1, own1, chan] = new
+                whole = sh.at[1, own2, lanes]
+                ends = sh.at[1, 2 * cols:3 * cols, lanes], sh.at[1, n + cols:n + 2 * cols, lanes]
             else:
                 top_hidden[:, chan] = hidden
+                whole = top_hidden.at[:, chan]
+                ends = top_hidden.at[0:cols, chan], top_hidden.at[n - cols:n, chan]
+            send(
+                not_roof,
+                lambda whole=whole, lanes=lanes, c=c: remote(
+                    whole, sx.at[t, own2, lanes], sx_s.at[t, c, 2], sx_r.at[t, c, 2], (z_up, s, k)
+                ),
+            )
+            if t == 0:
+                send_edges(ends, at_rows(sh, 1, near, lanes), sh_s.at[c], sh_r.at[1, c], z, None)
+            edges(
+                lambda ends=ends, lanes=lanes, c=c: (
+                    ends, at_rows(sx, t, near, lanes), sx_s.at[t, c], sx_r.at[t, c]
+                ),
+                z_up, not_roof,
+            )
             for index, value in enumerate((i_gate, f_gate, o_gate, cand, squash)):
                 gates[index, :, chan] = value
-        whole = sh.at[1, own2, centre] if t == 0 else top_hidden
-        send(
-            z < sections - 1,
-            lambda whole=whole, t=t: remote(
-                whole, sx.at[t, own2, centre], sx_s.at[t, 2], sx_r.at[t, 2], (z + 1, s, k)
-            ),
-        )
         if t == 0:
-            ends = sh.at[1, 2 * cols:4 * cols, centre], sh.at[1, n:n + 2 * cols, centre]
-            send_edges(ends, wide(sh, 1), sh_s, sh_r.at[1], z, None)
+            ends = sh.at[1, 3 * cols:4 * cols, centre], sh.at[1, n:n + cols, centre]
+            send_edges(ends, at_rows(sh, 1, far, centre), sh_fs, sh_f.at[1], z, None)
         else:
-            ends = outer(top_hidden, 2 * cols)
-        send_edges(ends, wide(sx, t), sx_s.at[t], sx_r.at[t], z + 1, z < sections - 1)
+            ends = beyond(top_hidden)
+        last = ends
+        edges(
+            lambda: (last, at_rows(sx, t, far, centre), sx_fs.at[t], sx_f.at[t]), z_up, not_roof
+        )
         if t == 0:
             narrow_here(cells.at[0], c_r)
+
+        far_here(sh, t, sh_f.at[t])
+        far_here(sx, t, sx_f.at[t])
         for c in range(2):
             chan = slice(c * half, (c + 1) * half)
             beside = jnp.concatenate([cells[t, above1, chan], cells[t, below1, chan]], axis=0)
-            values = activate(conv_beside(t, c) + bias_of(c), beside)
-            i_gate, f_gate, o_gate, cand, new, squash = values
+            i_gate, f_gate, o_gate, cand, new, squash = activate(conv_beside(t, c) + bias_of(c), beside)
             if t == 0:
                 cells[1, above1, chan] = new[0:cols]
                 cells[1, below1, chan] = new[cols:]
-            for index, value in enumerate(factors(i_gate, f_gate, o_gate, cand, squash, beside)):
-                coef[t, index, above1, chan] = value[0:cols]
-                coef[t, index, below1, chan] = value[cols:]
-            i_gate, f_gate, o_gate, cand, squash = (gates[index, :, chan] for index in range(5))
-            for index, value in enumerate(
-                factors(i_gate, f_gate, o_gate, cand, squash, cells[t, own1, chan])
-            ):
-                coef[t, index, own1, chan] = value
+            save(
+                t, ((above1, slice(0, cols)), (below1, slice(cols, 2 * cols))),
+                (i_gate, f_gate, o_gate, cand, squash), beside, chan,
+            )
+            save(
+                t, ((own1, slice(0, n)),),
+                tuple(gates[index, :, chan] for index in range(5)), cells[t, own1, chan], chan,
+            )
+
+    def all_rows():
+        near_here(sh, 1, sh_r.at[1], half_lanes)
+        far_here(sh, 1, sh_f.at[1])
+        for c in range(2):
+            preact[:, c * gate_half:(c + 1) * gate_half] = conv_all(sh, 1, wh, c) + bias_of(c)
+        x_here(1)
+        near_here(sx, 1, sx_r.at[1], half_lanes)
+        far_here(sx, 1, sx_f.at[1])
+        for c in range(2):
+            chan = slice(c * half, (c + 1) * half)
+            now = preact[:, c * gate_half:(c + 1) * gate_half] + conv_all(sx, 1, wx, c)
+            old = cells[1, :, chan]
+            i_gate, f_gate, o_gate, cand, new, squash = activate(now, old)
+            save(
+                1, ((slice(0, n + 2 * cols), slice(0, n + 2 * cols)),),
+                (i_gate, f_gate, o_gate, cand, squash), old, chan,
+            )
+
+    own_hidden.wait()
+    spread(sh, 0, own2, hid)
+    pl.when(z < 2)(lambda: weights_here(1))
+    own_rows(0)
+    spread(sh, 1, own2, hid)
+    pl.when(not_roof)(lambda: own_rows(1))
+    pl.when(roof)(all_rows)
 
     pl.when(z < 2)(turn_all_weights)
     send_tile(0, 1, base)
     for t, part in ((0, 0), (1, 1), (1, 0)):
-        send_tile(t, part, jnp.logical_not(roof))
+        send_tile(t, part, not_roof)
     pl.when(z < 2)(turn_patches)
 
     def back_conv(t, weights):
@@ -380,7 +494,7 @@
         return total.astype(BF16)
 
     for t in (1, 0):
-        pl.when(jnp.logical_not(roof))(lambda t=t: arrived(gin.at[t, own1], gx_r.at[t, 2]))
+        arrived(gin.at[t, own1], gx_r.at[t, 2])
         if t == 1:
             narrow_here(gin.at[t], gx_r.at[t])
         else:
@@ -444,43 +558,50 @@
             send_edges(
                 (ghid.at[cols:2 * cols], ghid.at[n:n + cols]), narrow(ghid), gh_s, gh_r, z, inner
             )
+            for step, part in ((0, 0), (1, 1), (1, 0)):
+                send_tile(step, part, roof)
         send_grads(t, inner)
 
-    for t, part in ((0, 0), (1, 1), (1, 0)):
-        send_tile(t, part, roof)
     pl.when(z >= 2)(turn_patches)
 
-    for t in (1, 0):
+    def grads_here(t, p):
         for slot in range(2 * LINE):
-            arrived(grads_all.at[t, slot * n:(slot + 1) * n], ga_r.at[t, slot])
-        if t == 1:
-            for j in range(LINE):
-                acc[j] = dot(turned[t, j], grads_all[t])
-        else:
-            for d in (1, 3, 2, 0):
-                j = (me + d) % LINE
-                leaving[d] = (acc[j] + dot(turned[t, j], grads_all[t])).astype(BF16)
-                chip = jnp.where(k == 0, j * LINE + x, y * LINE + j)
-                for q in range(2):
-                    src, dst = leaving.at[d, q * rows:(q + 1) * rows], landed.at[k, me]
-                    make = functools.partial(
-                        remote, src, dst, rv_s.at[d * 2 + q], rv_r.at[k, me], (z, chip, q)
+            arrived(grads_all.at[t, slot * n:(slot + 1) * n, pairs[p]], ga_r.at[t, p, slot])
+
+    grads_here(1, 0)
+    grads_here(1, 1)
+    for j in range(LINE):
+        acc[j] = dot(turned[1, j], grads_all[1])
+    for p, lanes in enumerate(pairs):
+        grads_here(0, p)
+        for d in (1, 3, 2, 0):
+            j = (me + d) % LINE
+            leaving[d, :, lanes] = (
+                acc[j, :, lanes] + dot(turned[0, j], grads_all[0, :, lanes])
+            ).astype(BF16)
+            chip = jnp.where(k == 0, j * LINE + x, y * LINE + j)
+            for q in range(2):
+                src, dst = leaving.at[d, q * rows:(q + 1) * rows, lanes], landed.at[k, me, :, lanes]
+                make = functools.partial(
+                    remote, src, dst, rv_s.at[p, d * 2 + q], rv_r.at[p, k, me], (z, chip, q)
+                )
+                if d == 0:
+                    pl.when(k == q)(
+                        functools.partial(
+                            lambda src, dst, sem: pltpu.make_async_copy(src, dst, sem).start(),
+                            src, dst, rv_r.at[p, k, me],
+                        )
                     )
-                    if d == 0:
-                        pl.when(k == q)(
-                            lambda src=src, dst=dst: pltpu.make_async_copy(
-                                src, dst, rv_r.at[k, me]
-                            ).start()
-                        )
-                    send(k != q if d == 0 else None, make)
-    for c in range(2):
-        for i in range(LINE):
-            arrived(landed.at[c, i], rv_r.at[c, i])
-        for g in range(4):
-            total = landed[c, 0, :, g * half:(g + 1) * half].astype(F32)
-            for i in range(1, LINE):
-                total = total + landed[c, i, :, g * half:(g + 1) * half].astype(F32)
-            out[:, g * hid + c * half:g * hid + (c + 1) * half] = total
+                send(k != q if d == 0 else None, make)
+    for p, lanes in enumerate(pairs):
+        for c in range(2):
+            for i in range(LINE):
+                arrived(landed.at[c, i, :, lanes], rv_r.at[p, c, i])
+            for g in (2 * p, 2 * p + 1):
+                total = landed[c, 0, :, g * half:(g + 1) * half].astype(F32)
+                for i in range(1, LINE):
+                    total = total + landed[c, i, :, g * half:(g + 1) * half].astype(F32)
+                out[:, g * hid + c * half:g * hid + (c + 1) * half] = total
     for wait in pending:
         wait()
 
@@ -494,6 +615,7 @@
     share = 18 * hid // (lax.axis_size("space") * lax.axis_size("batch"))
     block = 2 * share
     vmem = pl.BlockSpec(memory_space=pltpu.VMEM)
+    anywhere = pl.BlockSpec(memory_space=pl.ANY)
     dma = pltpu.SemaphoreType.DMA
     scratch = [
         pltpu.VMEM((2, 3, 3, hid, gates // 2), BF16),
@@ -504,7 +626,7 @@
         pltpu.VMEM((steps, pad + 2 * cols, 3 * hid), BF16),
         pltpu.VMEM((steps, pad, 3 * gates), BF16),
         pltpu.VMEM((n, hid), BF16),
-        pltpu.VMEM((n, gates), F32),
+        pltpu.VMEM((pad, gates), F32),
         pltpu.VMEM((5, n, hid), F32),
         pltpu.VMEM((steps, pad, hid), F32),
         pltpu.VMEM((pad, hid), F32),
@@ -519,17 +641,18 @@
         pltpu.VMEM((LINE, block, gates // 2), F32),
         pltpu.VMEM((LINE, block, gates // 2), BF16),
         pltpu.VMEM((2, LINE, share, gates // 2), BF16),
-        dma((2, 2, 4)),
-        dma((steps, 3)), dma((steps, 2)), dma((2,)), dma((steps, 3)), dma((2,)),
-        dma((steps, 2, 2 * LINE)), dma((steps, 2 * LINE)), dma((2, LINE)),
-        dma((steps, 2)), dma((2,)), dma((2,)), dma((steps, 2)),
-        dma((steps, 3)), dma((2,)), dma((steps, 3)), dma((2,)),
-        dma((steps, 2, 2 * LINE)), dma((steps, 2 * LINE)), dma((2 * LINE,)),
+        dma((2, 2, 4)), dma((2,)),
+        dma((steps, 2, 3)), dma((steps, 2)), dma((steps, 2, 2)), dma((steps, 2)),
+        dma((2,)), dma((steps, 3)), dma((2,)),
+        dma((steps, 2, 2 * LINE)), dma((steps, 2, 2 * LINE)), dma((2, 2, LINE)),
+        dma((steps, 2, 2)), dma((steps, 2)), dma((2,)), dma((2,)), dma((2,)), dma((steps, 2)),
+        dma((steps, 2, 3)), dma((steps, 2)), dma((2, 2)), dma((2,)), dma((steps, 3)), dma((2,)),
+        dma((steps, 2, 2 * LINE)), dma((steps, 2, 2 * LINE)), dma((2, 2 * LINE)),
     ]
     result = pl.pallas_call(
         kernel,
         out_shape=jax.ShapeDtypeStruct((share, gates), F32),
-        in_specs=[vmem] * 5 + [pl.BlockSpec(memory_space=pl.ANY)],
+        in_specs=[anywhere] * 4 + [vmem, anywhere],
         out_specs=vmem,
         scratch_shapes=scratch,
         compiler_params=pltpu.CompilerParams(

time: 82.2 us -> 88.8 us (1.080)
  Pallas kernels: 80.1 us -> 86.7 us
    pallas_call x1, Pallas kernels: 80.1 us -> 86.7 us  [on_device(): pl.pallas_call(kernel, out_shape=jax.ShapeDtypeStruct((share, gates), F32...]
where the time goes in v3:
time: 88.8 us; the launch traced here: 88.7 us
  Pallas kernels  86.7 us (98%)
  local copies, waits for them, and re-layouts  1.93 us (2%)
    pallas_call x1, Pallas kernels, on_device(): pl.pallas_call(kernel, out_shape=jax.ShapeDtypeStruct((share, gates), F32...  86.7 us
    unnamed x1, local copies, waits for them, and re-layouts  1.93 us

profile of v3, /device:TPU:1, one launch (start us, length us, event | category | flops | bytes accessed | tf_op | source)
XLA Modules:
  0.0 88.7 jit_solution(16574420304124217474)
XLA Ops:
  0.0 86.7 %shard_map.64 = f32[144,1024]{1,0:T(8,128)} custom-call(bf16[2,128,256]{2,1,0:T(8,128)(2,1)} %bitcast.8, bf16[2,128,256]{2,1,0:T(8,128)(2,1)} %bitcast.9, bf16[128,256]{1,0:T(8,128)(2,1)} %bitcast.11, f32[128,256]{1,0:T(8,128)} %bitcast.10, f32[1,1024]{1,0:T(1,128)} %bias.1, bf16[3,3,512,1024]{3,2,1,0:T(8,128)(2,1)} %bitcast.6), custom_call_target="tpu_custom_call" | custom-call | tf_op jit(solution)/shard_map/pallas_call | solution.py:652
  86.7 1.9 %copy.8 = f32[1,144,1024]{2,1,0:T(8,128)} copy(f32[1,144,1024]{2,1,0:T(8,128)} %bitcast.7) | data formatting | bytes 1179648

commit v4 on v3

--- a/solution.py
+++ b/solution.py
@@ -322,7 +322,7 @@
     pairs = [slice(p * 2 * half, (p + 1) * 2 * half) for p in range(2)]
 
     def send_grads(t, pred):
-        for p, lanes in enumerate(pairs):
+        for p, lanes in enumerate(pairs if t == 0 else [slice(0, gate_half)]):
             def view(c, slot):
                 at = 4 * hid + c * gate_half
                 src = sg.at[t, own1, at + lanes.start:at + lanes.stop]
@@ -377,35 +377,82 @@
             arrived(sx.at[t, own2, half_lanes[c]], sx_r.at[t, c, 2])
         spread(sx, t, own2, hid)
 
+    def add(c, term):
+        preact[0:n, c * gate_half:(c + 1) * gate_half] += term
+
     def own_rows(t):
+        hidden_lanes = (centre,) if t == 0 else half_lanes
         part_sums = [conv(sh, t, wh, c, (1,)) + bias_of(c) for c in range(2)]
         for c in range(2):
             preact[0:n, c * gate_half:(c + 1) * gate_half] = part_sums[c]
-        near_here(sh, t, sh_r.at[t], (centre,) if t == 0 else half_lanes)
+
+        def x_middle():
+            x_here(t)
+            for c in range(2):
+                add(c, conv(sx, t, wx, c, (1,)))
+
+        def x_edges():
+            near_here(sx, t, sx_r.at[t], half_lanes)
+
+        def h_edges():
+            near_here(sh, t, sh_r.at[t], hidden_lanes)
+
+        def h_outer():
+            for c in range(2):
+                add(c, conv(sh, t, wh, c, (0, 2)))
+
+        @pl.when(base)
+        def _():
+            if t == 0:
+                weights_here(0)
+            x_middle()
+            if t == 1:
+                x_edges()
+                for c in range(2):
+                    add(c, conv(sx, t, wx, c, (0, 2)))
+                h_edges()
+
         if t == 0:
+            h_edges()
+            h_outer()
             send_tile(0, 1, inner)
-        for c in range(2):
-            preact[0:n, c * gate_half:(c + 1) * gate_half] += conv(sh, t, wh, c, (0, 2))
+            pl.when(z == 1)(lambda: weights_here(0))
+
+        @pl.when(inner)
+        def _():
+            if t == 1:
+                h_edges()
+                h_outer()
+            x_middle()
+            if t == 1:
+                x_edges()
+
         if t == 0:
-            pl.when(z < 2)(lambda: weights_here(0))
-        x_here(t)
-        for c in range(2):
-            preact[0:n, c * gate_half:(c + 1) * gate_half] += conv(sx, t, wx, c, (1,))
-        near_here(sx, t, sx_r.at[t], half_lanes)
-        if t == 0:
+            x_edges()
             own_cell.wait()
-        for c in range(2):
+
+        def finish(buffer, weights, c):
             chan, lanes = slice(c * half, (c + 1) * half), half_lanes[c]
-            now = preact[0:n, c * gate_half:(c + 1) * gate_half] + conv(sx, t, wx, c, (0, 2))
+            now = preact[0:n, c * gate_half:(c + 1) * gate_half] + conv(buffer, t, weights, c, (0, 2))
             i_gate, f_gate, o_gate, cand, new, squash = activate(now, cells[t, own1, chan])
             hidden = (o_gate * squash).astype(BF16)
             if t == 0:
                 sh[1, own2, lanes] = hidden
                 cells[1, own1, chan] = new
+            else:
+                top_hidden[:, chan] = hidden
+            for index, value in enumerate((i_gate, f_gate, o_gate, cand, squash)):
+                gates[index, :, chan] = value
+
+        for c in range(2):
+            chan, lanes = slice(c * half, (c + 1) * half), half_lanes[c]
+            if t == 0:
+                finish(sx, wx, c)
                 whole = sh.at[1, own2, lanes]
                 ends = sh.at[1, 2 * cols:3 * cols, lanes], sh.at[1, n + cols:n + 2 * cols, lanes]
             else:
-                top_hidden[:, chan] = hidden
+                pl.when(base)(lambda c=c: finish(sh, wh, c))
+                pl.when(inner)(lambda c=c: finish(sx, wx, c))
                 whole = top_hidden.at[:, chan]
                 ends = top_hidden.at[0:cols, chan], top_hidden.at[n - cols:n, chan]
             send(
@@ -422,8 +469,6 @@
                 ),
                 z_up, not_roof,
             )
-            for index, value in enumerate((i_gate, f_gate, o_gate, cand, squash)):
-                gates[index, :, chan] = value
         if t == 0:
             ends = sh.at[1, 3 * cols:4 * cols, centre], sh.at[1, n:n + cols, centre]
             send_edges(ends, at_rows(sh, 1, far, centre), sh_fs, sh_f.at[1], z, None)
@@ -433,29 +478,31 @@
         edges(
             lambda: (last, at_rows(sx, t, far, centre), sx_fs.at[t], sx_f.at[t]), z_up, not_roof
         )
+        for c in range(2):
+            chan = slice(c * half, (c + 1) * half)
+            save(
+                t, ((own1, slice(0, n)),),
+                tuple(gates[index, :, chan] for index in range(5)), cells[t, own1, chan], chan,
+            )
+
+    def beside_rows(t):
         if t == 0:
             narrow_here(cells.at[0], c_r)
-
         far_here(sh, t, sh_f.at[t])
         far_here(sx, t, sx_f.at[t])
         for c in range(2):
             chan = slice(c * half, (c + 1) * half)
-            beside = jnp.concatenate([cells[t, above1, chan], cells[t, below1, chan]], axis=0)
-            i_gate, f_gate, o_gate, cand, new, squash = activate(conv_beside(t, c) + bias_of(c), beside)
+            old = jnp.concatenate([cells[t, above1, chan], cells[t, below1, chan]], axis=0)
+            i_gate, f_gate, o_gate, cand, new, squash = activate(conv_beside(t, c) + bias_of(c), old)
             if t == 0:
                 cells[1, above1, chan] = new[0:cols]
                 cells[1, below1, chan] = new[cols:]
             save(
                 t, ((above1, slice(0, cols)), (below1, slice(cols, 2 * cols))),
-                (i_gate, f_gate, o_gate, cand, squash), beside, chan,
-            )
-            save(
-                t, ((own1, slice(0, n)),),
-                tuple(gates[index, :, chan] for index in range(5)), cells[t, own1, chan], chan,
+                (i_gate, f_gate, o_gate, cand, squash), old, chan,
             )
 
     def all_rows():
-        near_here(sh, 1, sh_r.at[1], half_lanes)
         far_here(sh, 1, sh_f.at[1])
         for c in range(2):
             preact[:, c * gate_half:(c + 1) * gate_half] = conv_all(sh, 1, wh, c) + bias_of(c)
@@ -476,9 +523,28 @@
     spread(sh, 0, own2, hid)
     pl.when(z < 2)(lambda: weights_here(1))
     own_rows(0)
+    send_tile(0, 0, roof)
     spread(sh, 1, own2, hid)
-    pl.when(not_roof)(lambda: own_rows(1))
+
+    @pl.when(not_roof)
+    def _():
+        own_rows(1)
+        beside_rows(0)
+        beside_rows(1)
+
+    @pl.when(roof)
+    def _():
+        beside_rows(0)
+        near_here(sh, 1, sh_r.at[1], half_lanes)
+
+    send_tile(1, 1, roof)
     pl.when(roof)(all_rows)
+
+    def blank(outside):
+        coef[:, :, outside, :] = jnp.zeros((2, 6, cols, hid), F32)
+
+    pl.when(top)(lambda: blank(above1))
+    pl.when(bottom)(lambda: blank(below1))
 
     pl.when(z < 2)(turn_all_weights)
     send_tile(0, 1, base)
@@ -525,14 +591,6 @@
         def widen(t=t):
             spread(sg, t, slice(0, 2 * cols + n), 4 * hid)
 
-            @pl.when(top)
-            def _():
-                sg[t, above1, :] = jnp.zeros((cols, 12 * hid), BF16)
-
-            @pl.when(bottom)
-            def _():
-                sg[t, below1, :] = jnp.zeros((cols, 12 * hid), BF16)
-
         def input_grad(t=t):
             gx_out[t] = back_conv(t, wxt)
 
@@ -558,22 +616,22 @@
             send_edges(
                 (ghid.at[cols:2 * cols], ghid.at[n:n + cols]), narrow(ghid), gh_s, gh_r, z, inner
             )
-            for step, part in ((0, 0), (1, 1), (1, 0)):
-                send_tile(step, part, roof)
-        send_grads(t, inner)
+            send_tile(1, 0, roof)
+        else:
+            send_grads(1, inner)
+            send_grads(0, inner)
 
     pl.when(z >= 2)(turn_patches)
 
-    def grads_here(t, p):
+    def grads_here(t, p, lanes):
         for slot in range(2 * LINE):
-            arrived(grads_all.at[t, slot * n:(slot + 1) * n, pairs[p]], ga_r.at[t, p, slot])
-
-    grads_here(1, 0)
-    grads_here(1, 1)
+            arrived(grads_all.at[t, slot * n:(slot + 1) * n, lanes], ga_r.at[t, p, slot])
+
+    grads_here(1, 0, slice(0, gate_half))
     for j in range(LINE):
         acc[j] = dot(turned[1, j], grads_all[1])
     for p, lanes in enumerate(pairs):
-        grads_here(0, p)
+        grads_here(0, p, lanes)
         for d in (1, 3, 2, 0):
             j = (me + d) % LINE
             leaving[d, :, lanes] = (

time: 88.8 us -> 79.1 us (0.89)
  Pallas kernels: 86.7 us -> 77 us
    pallas_call x1, Pallas kernels: 86.7 us -> 77 us  [on_device(): pl.pallas_call(kernel, out_shape=jax.ShapeDtypeStruct((share, gates), F32...]
where the time goes in v4:
time: 79.1 us; the launch traced here: 78.9 us
  Pallas kernels  77 us (97%)
  local copies, waits for them, and re-layouts  1.93 us (2%)
    pallas_call x1, Pallas kernels, on_device(): pl.pallas_call(kernel, out_shape=jax.ShapeDtypeStruct((share, gates), F32...  77 us
    unnamed x1, local copies, waits for them, and re-layouts  1.93 us

profile of v4, /device:TPU:1, one launch (start us, length us, event | category | flops | bytes accessed | tf_op | source)
XLA Modules:
  0.0 78.9 jit_solution(5766684792964993987)
XLA Ops:
  0.0 77.0 %shard_map.64 = f32[144,1024]{1,0:T(8,128)} custom-call(bf16[2,128,256]{2,1,0:T(8,128)(2,1)} %bitcast.8, bf16[2,128,256]{2,1,0:T(8,128)(2,1)} %bitcast.9, bf16[128,256]{1,0:T(8,128)(2,1)} %bitcast.11, f32[128,256]{1,0:T(8,128)} %bitcast.10, f32[1,1024]{1,0:T(1,128)} %bias.1, bf16[3,3,512,1024]{3,2,1,0:T(8,128)(2,1)} %bitcast.6), custom_call_target="tpu_custom_call" | custom-call | tf_op jit(solution)/shard_map/pallas_call | solution.py:710
  77.0 1.9 %copy.8 = f32[1,144,1024]{2,1,0:T(8,128)} copy(f32[1,144,1024]{2,1,0:T(8,128)} %bitcast.7) | data formatting | bytes 1179648

commit v5 on v4

--- a/solution.py
+++ b/solution.py
@@ -74,28 +74,40 @@
             for g in range(4):
                 loads[part, c, g].wait()
 
-    partners = [(jnp.logical_not(top), (z, s - 1, k)), (jnp.logical_not(bottom), (z, s + 1, k))]
-    for step, ok in ((-1, z > 0), (1, z < sections - 1)):
-        partners.append((ok, (z + step, s, k)))
-        partners.append((ok & (s > 0), (z + step, s - 1, k)))
-        partners.append((ok & (s < tiles - 1), (z + step, s + 1, k)))
-    partners.append((None, (z, s, 1 - k)))
+    barrier = pltpu.get_barrier_semaphore()
+
+    def greet(partners):
+        for pred, device in partners:
+            call = functools.partial(
+                pl.semaphore_signal, barrier, inc=1, device_id=device, device_id_type=MESH
+            )
+            if pred is None:
+                call()
+            else:
+                pl.when(pred)(call)
+
+    def count(partners):
+        total = 0
+        for pred, _ in partners:
+            total = total + (1 if pred is None else jnp.where(pred, 1, 0))
+        return total
+
+    plane = [(jnp.logical_not(top), (z, s - 1, k)), (jnp.logical_not(bottom), (z, s + 1, k))]
+    plane.append((None, (z, s, 1 - k)))
     for d in range(1, LINE):
         for core in range(2):
-            partners.append((None, (z, y * LINE + (x + d) % LINE, core)))
-            partners.append((None, (z, ((y + d) % LINE) * LINE + x, core)))
-    barrier = pltpu.get_barrier_semaphore()
-    expected = 0
-    for pred, device in partners:
-        greet = functools.partial(
-            pl.semaphore_signal, barrier, inc=1, device_id=device, device_id_type=MESH
-        )
-        if pred is None:
-            greet()
-            expected = expected + 1
-        else:
-            pl.when(pred)(greet)
-            expected = expected + jnp.where(pred, 1, 0)
+            plane.append((None, (z, y * LINE + (x + d) % LINE, core)))
+            plane.append((None, (z, ((y + d) % LINE) * LINE + x, core)))
+
+    def section_at(step, ok):
+        return [
+            (ok, (z + step, s, k)),
+            (ok & (s > 0), (z + step, s - 1, k)),
+            (ok & (s < tiles - 1), (z + step, s + 1, k)),
+        ]
+
+    below, above = section_at(-1, z > 0), section_at(1, z < sections - 1)
+    greet(plane)
 
     half_lanes = [slice(hid + c * half, hid + (c + 1) * half) for c in range(2)]
     own_hidden = pltpu.make_async_copy(first_hidden, sh.at[0, own2, centre], in_sem.at[0])
@@ -133,7 +145,7 @@
     pl.when(top)(lambda: clear(above2, above1))
     pl.when(bottom)(lambda: clear(below2, below1))
 
-    pl.semaphore_wait(barrier, expected)
+    pl.semaphore_wait(barrier, count(plane) + count(below))
 
     def send_edges(src, dst, send_sems, recv_sems, section, pred):
         edges(lambda: (src, dst, send_sems, recv_sems), section, pred)
@@ -177,6 +189,8 @@
             )
 
     send_frames(0)
+    greet(above)
+    greet(below)
     send_edges(beyond(first_hidden), at_rows(sh, 0, far, centre), fh_f, sh_f.at[0], z, None)
     send_edges(outer(first_cell, cols), narrow(cells.at[0]), fc_s, c_r, z, None)
     send_edges(beyond(frames.at[0]), at_rows(sx, 0, far, centre), fr_f.at[0], sx_f.at[0], z, base)
@@ -430,6 +444,7 @@
         if t == 0:
             x_edges()
             own_cell.wait()
+            pl.when(not_roof)(lambda: pl.semaphore_wait(barrier, count(above)))
 
         def finish(buffer, weights, c):
             chan, lanes = slice(c * half, (c + 1) * half), half_lanes[c]
@@ -617,8 +632,9 @@
                 (ghid.at[cols:2 * cols], ghid.at[n:n + cols]), narrow(ghid), gh_s, gh_r, z, inner
             )
             send_tile(1, 0, roof)
+            send_grads(1, z == 1)
         else:
-            send_grads(1, inner)
+            send_grads(1, z >= 2)
             send_grads(0, inner)
 
     pl.when(z >= 2)(turn_patches)
@@ -630,6 +646,8 @@
     grads_here(1, 0, slice(0, gate_half))
     for j in range(LINE):
         acc[j] = dot(turned[1, j], grads_all[1])
+    earlier = list(pending)
+    pending.clear()
     for p, lanes in enumerate(pairs):
         grads_here(0, p, lanes)
         for d in (1, 3, 2, 0):
@@ -651,6 +669,8 @@
                         )
                     )
                 send(k != q if d == 0 else None, make)
+    for wait in earlier:
+        wait()
     for p, lanes in enumerate(pairs):
         for c in range(2):
             for i in range(LINE):

time: 79.1 us -> 78.2 us (0.989)
  Pallas kernels: 77 us -> 76.1 us
    pallas_call x1, Pallas kernels: 77 us -> 76.1 us  [on_device(): pl.pallas_call(kernel, out_shape=jax.ShapeDtypeStruct((share, gates), F32...]
where the time goes in v5:
time: 78.2 us; the launch traced here: 78.1 us
  Pallas kernels  76.1 us (97%)
  local copies, waits for them, and re-layouts  1.93 us (2%)
    pallas_call x1, Pallas kernels, on_device(): pl.pallas_call(kernel, out_shape=jax.ShapeDtypeStruct((share, gates), F32...  76.1 us
    unnamed x1, local copies, waits for them, and re-layouts  1.93 us

profile of v5, /device:TPU:1, one launch (start us, length us, event | category | flops | bytes accessed | tf_op | source)
XLA Modules:
  0.0 78.1 jit_solution(13290703383357649761)
XLA Ops:
  0.0 76.1 %shard_map.64 = f32[144,1024]{1,0:T(8,128)} custom-call(bf16[2,128,256]{2,1,0:T(8,128)(2,1)} %bitcast.8, bf16[2,128,256]{2,1,0:T(8,128)(2,1)} %bitcast.9, bf16[128,256]{1,0:T(8,128)(2,1)} %bitcast.11, f32[128,256]{1,0:T(8,128)} %bitcast.10, f32[1,1024]{1,0:T(1,128)} %bias.1, bf16[3,3,512,1024]{3,2,1,0:T(8,128)(2,1)} %bitcast.6), custom_call_target="tpu_custom_call" | custom-call | tf_op jit(solution)/shard_map/pallas_call | solution.py:730
  76.1 1.9 %copy.8 = f32[1,144,1024]{2,1,0:T(8,128)} copy(f32[1,144,1024]{2,1,0:T(8,128)} %bitcast.7) | data formatting | bytes 1179648

commit v6 on v5

--- a/solution.py
+++ b/solution.py
@@ -20,9 +20,9 @@
 def kernel(
     frames, cotangent, first_hidden, first_cell, bias, weight, out,
     wx, wh, wxt, wht, sx, sh, sg, top_hidden, preact, gates, cells, carry, coef, gin, gx_out, ghid,
-    tiles_all, flipped, turned, grads_all, acc, leaving, landed,
-    w_sem, in_sem, sx_r, sx_f, sh_r, sh_f, c_r, gx_r, gh_r, ti_r, ga_r, rv_r,
-    fr_s, fr_f, fh_s, fh_f, fc_s, ct_s, sx_s, sx_fs, sh_s, sh_fs, gx_s, gh_s, ti_s, ga_s, rv_s,
+    tiles_all, flipped, turned, grads_all, packed, packed_all, vec, vec_all, acc, leaving, landed,
+    w_sem, in_sem, sx_r, sx_f, sh_r, sh_f, c_r, gx_r, gh_r, ti_r, ga_r, co_r, ve_r, rv_r,
+    fr_s, fr_f, fh_s, fh_f, fc_s, ct_s, sx_s, sx_fs, sh_s, sh_fs, gx_s, gh_s, ti_s, ga_s, co_s, ve_s, rv_s,
 ):
     z, s, k = lax.axis_index("section"), lax.axis_index("space"), lax.axis_index("batch")
     y, x = s // LINE, s % LINE
@@ -344,6 +344,34 @@
 
             spread_to_group(pred, view, ga_s.at[t, p], ga_r.at[t, p])
 
+    early = z < 2
+
+    def send_factors(t):
+        def view(c, slot):
+            src = packed.at[t, :, c * gate_half:(c + 1) * gate_half]
+            return src, packed_all.at[t, pl.ds(pl.multiple_of(slot * n, n), n), :]
+
+        spread_to_group(early, view, co_s.at[t], co_r.at[t])
+
+    def pack_factors():
+        for c in range(2):
+            chan = slice(c * half, (c + 1) * half)
+            for t in range(2):
+                for g in range(4):
+                    value = coef[t, 1 + g, own1, chan]
+                    if t == 1 and g != 2:
+                        value = value * coef[t, 0, own1, chan]
+                    at = c * gate_half + g * half
+                    packed[t, :, at:at + half] = value.astype(BF16)
+
+    def send_vec(index, pred):
+        def view(c, slot):
+            chan = slice(c * half, (c + 1) * half)
+            src = gin.at[1, own1, chan] if index == 0 else vec.at[index - 1, :, chan]
+            return src, vec_all.at[index, pl.ds(pl.multiple_of(slot * n, n), n), :]
+
+        spread_to_group(pred, view, ve_s.at[index], ve_r.at[index])
+
     rows = out.shape[0]
     block = 2 * rows
     me = jnp.where(k == 0, y, x)
@@ -538,7 +566,7 @@
     spread(sh, 0, own2, hid)
     pl.when(z < 2)(lambda: weights_here(1))
     own_rows(0)
-    send_tile(0, 0, roof)
+    send_tile(0, 0, inner)
     spread(sh, 1, own2, hid)
 
     @pl.when(not_roof)
@@ -562,9 +590,13 @@
     pl.when(bottom)(lambda: blank(below1))
 
     pl.when(z < 2)(turn_all_weights)
+    pl.when(early)(pack_factors)
     send_tile(0, 1, base)
-    for t, part in ((0, 0), (1, 1), (1, 0)):
-        send_tile(t, part, not_roof)
+    send_tile(0, 0, base)
+    send_tile(1, 1, not_roof)
+    send_tile(1, 0, not_roof)
+    send_factors(1)
+    send_factors(0)
     pl.when(z < 2)(turn_patches)
 
     def back_conv(t, weights):
@@ -576,6 +608,8 @@
 
     for t in (1, 0):
         arrived(gin.at[t, own1], gx_r.at[t, 2])
+        if t == 1:
+            send_vec(0, base)
         if t == 1:
             narrow_here(gin.at[t], gx_r.at[t])
         else:
@@ -599,9 +633,14 @@
             )):
                 at = 4 * hid + c * gate_half + g * half
                 sg[t, :, at:at + half] = value.astype(BF16)
+            if t == 0:
+                vec[0, :, chan] = grad_c[cols:cols + n].astype(BF16)
+                vec[1, :, chan] = grad_h[cols:cols + n].astype(BF16)
             if t == 1:
                 carry[:, chan] = grad_c * coef[t, 5, :, chan]
-        send_grads(t, base)
+        if t == 0:
+            send_vec(1, early)
+            send_vec(2, early)
 
         def widen(t=t):
             spread(sg, t, slice(0, 2 * cols + n), 4 * hid)
@@ -632,10 +671,10 @@
                 (ghid.at[cols:2 * cols], ghid.at[n:n + cols]), narrow(ghid), gh_s, gh_r, z, inner
             )
             send_tile(1, 0, roof)
-            send_grads(1, z == 1)
+            send_vec(0, z == 1)
         else:
             send_grads(1, z >= 2)
-            send_grads(0, inner)
+            send_grads(0, z >= 2)
 
     pl.when(z >= 2)(turn_patches)
 
@@ -643,13 +682,44 @@
         for slot in range(2 * LINE):
             arrived(grads_all.at[t, slot * n:(slot + 1) * n, lanes], ga_r.at[t, p, slot])
 
-    grads_here(1, 0, slice(0, gate_half))
+    def vec_here(index):
+        for slot in range(2 * LINE):
+            arrived(vec_all.at[index, slot * n:(slot + 1) * n], ve_r.at[index, slot])
+
+    def factors_here(t):
+        for slot in range(2 * LINE):
+            arrived(packed_all.at[t, slot * n:(slot + 1) * n], co_r.at[t, slot])
+
+    def form(t, gates_of, index):
+        for g in gates_of:
+            lanes = slice(g * half, (g + 1) * half)
+            grads_all[t, :, lanes] = (
+                packed_all[t, :, lanes].astype(F32) * vec_all[index].astype(F32)
+            ).astype(BF16)
+
+    @pl.when(early)
+    def _():
+        factors_here(1)
+        factors_here(0)
+        vec_here(0)
+        form(1, range(4), 0)
+
+    pl.when(z >= 2)(lambda: grads_here(1, 0, slice(0, gate_half)))
     for j in range(LINE):
         acc[j] = dot(turned[1, j], grads_all[1])
     earlier = list(pending)
     pending.clear()
     for p, lanes in enumerate(pairs):
-        grads_here(0, p, lanes)
+        @pl.when(early)
+        def _():
+            vec_here(1 + p)
+            if p == 0:
+                form(0, (0, 1), 1)
+            else:
+                form(0, (2,), 2)
+                form(0, (3,), 1)
+
+        pl.when(z >= 2)(lambda: grads_here(0, p, lanes))
         for d in (1, 3, 2, 0):
             j = (me + d) % LINE
             leaving[d, :, lanes] = (
@@ -716,16 +786,22 @@
         pltpu.VMEM((18 * hid, n), BF16),
         pltpu.VMEM((steps, LINE, block, 2 * LINE * n), BF16),
         pltpu.VMEM((steps, 2 * LINE * n, gates // 2), BF16),
+        pltpu.VMEM((steps, n, gates), BF16),
+        pltpu.VMEM((steps, 2 * LINE * n, gates // 2), BF16),
+        pltpu.VMEM((2, n, hid), BF16),
+        pltpu.VMEM((3, 2 * LINE * n, half), BF16),
         pltpu.VMEM((LINE, block, gates // 2), F32),
         pltpu.VMEM((LINE, block, gates // 2), BF16),
         pltpu.VMEM((2, LINE, share, gates // 2), BF16),
         dma((2, 2, 4)), dma((2,)),
         dma((steps, 2, 3)), dma((steps, 2)), dma((steps, 2, 2)), dma((steps, 2)),
         dma((2,)), dma((steps, 3)), dma((2,)),
-        dma((steps, 2, 2 * LINE)), dma((steps, 2, 2 * LINE)), dma((2, 2, LINE)),
+        dma((steps, 2, 2 * LINE)), dma((steps, 2, 2 * LINE)), dma((steps, 2 * LINE)), dma((3, 2 * LINE)),
+        dma((2, 2, LINE)),
         dma((steps, 2, 2)), dma((steps, 2)), dma((2,)), dma((2,)), dma((2,)), dma((steps, 2)),
         dma((steps, 2, 3)), dma((steps, 2)), dma((2, 2)), dma((2,)), dma((steps, 3)), dma((2,)),
-        dma((steps, 2, 2 * LINE)), dma((steps, 2, 2 * LINE)), dma((2, 2 * LINE)),
+        dma((steps, 2, 2 * LINE)), dma((steps, 2, 2 * LINE)), dma((steps, 2 * LINE)), dma((3, 2 * LINE)),
+        dma((2, 2 * LINE)),
     ]
     result = pl.pallas_call(
         kernel,

time: 78.2 us -> 77.4 us (0.990)
  Pallas kernels: 76.1 us -> 75.1 us
    pallas_call x1, Pallas kernels: 76.1 us -> 75.1 us  [on_device(): pl.pallas_call(kernel, out_shape=jax.ShapeDtypeStruct((share, gates), F32...]
where the time goes in v6:
time: 77.4 us; the launch traced here: 77 us
  Pallas kernels  75.1 us (97%)
  local copies, waits for them, and re-layouts  1.93 us (2%)
    pallas_call x1, Pallas kernels, on_device(): pl.pallas_call(kernel, out_shape=jax.ShapeDtypeStruct((share, gates), F32...  75.1 us
    unnamed x1, local copies, waits for them, and re-layouts  1.93 us

profile of v6, /device:TPU:1, one launch (start us, length us, event | category | flops | bytes accessed | tf_op | source)
XLA Modules:
  0.0 77.0 jit_solution(17627898264379244013)
XLA Ops:
  0.0 75.1 %shard_map.64 = f32[144,1024]{1,0:T(8,128)} custom-call(bf16[2,128,256]{2,1,0:T(8,128)(2,1)} %bitcast.8, bf16[2,128,256]{2,1,0:T(8,128)(2,1)} %bitcast.9, bf16[128,256]{1,0:T(8,128)(2,1)} %bitcast.11, f32[128,256]{1,0:T(8,128)} %bitcast.10, f32[1,1024]{1,0:T(1,128)} %bias.1, bf16[3,3,512,1024]{3,2,1,0:T(8,128)(2,1)} %bitcast.6), custom_call_target="tpu_custom_call" | custom-call | tf_op jit(solution)/shard_map/pallas_call | solution.py:806
  75.1 1.9 %copy.8 = f32[1,144,1024]{2,1,0:T(8,128)} copy(f32[1,144,1024]{2,1,0:T(8,128)} %bitcast.7) | data formatting | bytes 1179648

commit v7 on v6

--- a/solution.py
+++ b/solution.py
@@ -305,53 +305,65 @@
         turn_weights(wh, wht)
         pl.when(inner)(lambda: turn_weights(wx, wxt))
 
-    def spread_to_group(pred, view, send_sems, recv_sems):
-        for d in (0, 1, 3, 2):
-            for c in range(2):
-                there = ((x if c == 0 else y) + d) % LINE
-                chip = y * LINE + there if c == 0 else there * LINE + x
-                slot = 2 * (x if c == 0 else y) + k
-                src, dst = view(c, slot)
-                make = functools.partial(
-                    remote, src, dst, send_sems.at[c * LINE + d], recv_sems.at[slot], (z, chip, c)
-                )
-                ok = pred
-                if d == 0:
-                    ok = (k != c) if pred is None else pred & (k != c)
-                    own = (k == c) if pred is None else pred & (k == c)
-                    pl.when(own)(
-                        functools.partial(
-                            lambda src, dst, sem: pltpu.make_async_copy(src, dst, sem).start(),
-                            src, dst, recv_sems.at[slot],
-                        )
-                    )
-                send(ok, make)
+    def spread_to_group(pred, view, seven, send_sem, recv_sem):
+        def go():
+            for d in (0, 1, 3, 2):
+                for c in range(2):
+                    there = ((x if c == 0 else y) + d) % LINE
+                    chip = y * LINE + there if c == 0 else there * LINE + x
+                    src, dst = view(c, 2 * (x if c == 0 else y) + k)
+                    copy = functools.partial(remote, src, dst, send_sem(), recv_sem(), (z, chip, c))
+                    if d == 0:
+                        pl.when(k == c)(lambda: pltpu.make_async_copy(src, dst, recv_sem()).start())
+                        pl.when(k != c)(lambda: copy().start())
+                    else:
+                        copy().start()
+
+        def done():
+            remote(seven(), seven(), send_sem(), recv_sem(), (z, s, 1 - k)).wait_send()
+
+        pl.when(pred)(go)
+        pending.append(lambda: pl.when(pred)(done))
+
+    def rows_of(slot):
+        return pl.ds(pl.multiple_of(slot * n, n), n)
+
+    most = slice(0, 7 * n)
 
     def send_tile(t, part, pred):
-        src = (sh if part else sx).at[t, cols:3 * cols + n, centre]
         spread_to_group(
-            pred, lambda c, slot: (src, tiles_all.at[t, part, slot]), ti_s.at[t, part], ti_r.at[t, part]
+            pred,
+            lambda c, slot: (
+                (sh if part else sx).at[t, cols:3 * cols + n, centre], tiles_all.at[t, part, slot]
+            ),
+            lambda: tiles_all.at[t, part, 0:7],
+            lambda: ti_s.at[t, part], lambda: ti_r.at[t, part],
         )
 
     pairs = [slice(p * 2 * half, (p + 1) * 2 * half) for p in range(2)]
 
     def send_grads(t, pred):
         for p, lanes in enumerate(pairs if t == 0 else [slice(0, gate_half)]):
-            def view(c, slot):
+            def view(c, slot, lanes=lanes):
                 at = 4 * hid + c * gate_half
                 src = sg.at[t, own1, at + lanes.start:at + lanes.stop]
-                return src, grads_all.at[t, pl.ds(pl.multiple_of(slot * n, n), n), lanes]
-
-            spread_to_group(pred, view, ga_s.at[t, p], ga_r.at[t, p])
+                return src, grads_all.at[t, rows_of(slot), lanes]
+
+            spread_to_group(
+                pred, view, lambda lanes=lanes: grads_all.at[t, most, lanes],
+                lambda p=p: ga_s.at[t, p], lambda p=p: ga_r.at[t, p],
+            )
 
     early = z < 2
 
     def send_factors(t):
         def view(c, slot):
             src = packed.at[t, :, c * gate_half:(c + 1) * gate_half]
-            return src, packed_all.at[t, pl.ds(pl.multiple_of(slot * n, n), n), :]
-
-        spread_to_group(early, view, co_s.at[t], co_r.at[t])
+            return src, packed_all.at[t, rows_of(slot), :]
+
+        spread_to_group(
+            early, view, lambda: packed_all.at[t, most], lambda: co_s.at[t], lambda: co_r.at[t]
+        )
 
     def pack_factors():
         for c in range(2):
@@ -368,9 +380,11 @@
         def view(c, slot):
             chan = slice(c * half, (c + 1) * half)
             src = gin.at[1, own1, chan] if index == 0 else vec.at[index - 1, :, chan]
-            return src, vec_all.at[index, pl.ds(pl.multiple_of(slot * n, n), n), :]
-
-        spread_to_group(pred, view, ve_s.at[index], ve_r.at[index])
+            return src, vec_all.at[index, rows_of(slot), :]
+
+        spread_to_group(
+            pred, view, lambda: vec_all.at[index, most], lambda: ve_s.at[index], lambda: ve_r.at[index]
+        )
 
     rows = out.shape[0]
     block = 2 * rows
@@ -379,8 +393,7 @@
     def turn_patches():
         for t in range(2):
             for part in range(2):
-                for slot in range(2 * LINE):
-                    arrived(tiles_all.at[t, part, slot], ti_r.at[t, part, slot])
+                arrived(tiles_all.at[t, part], ti_r.at[t, part])
 
             def one(slot, carried):
                 for part in range(2):
@@ -679,16 +692,13 @@
     pl.when(z >= 2)(turn_patches)
 
     def grads_here(t, p, lanes):
-        for slot in range(2 * LINE):
-            arrived(grads_all.at[t, slot * n:(slot + 1) * n, lanes], ga_r.at[t, p, slot])
+        arrived(grads_all.at[t, :, lanes], ga_r.at[t, p])
 
     def vec_here(index):
-        for slot in range(2 * LINE):
-            arrived(vec_all.at[index, slot * n:(slot + 1) * n], ve_r.at[index, slot])
+        arrived(vec_all.at[index], ve_r.at[index])
 
     def factors_here(t):
-        for slot in range(2 * LINE):
-            arrived(packed_all.at[t, slot * n:(slot + 1) * n], co_r.at[t, slot])
+        arrived(packed_all.at[t], co_r.at[t])
 
     def form(t, gates_of, index):
         for g in gates_of:
@@ -707,8 +717,6 @@
     pl.when(z >= 2)(lambda: grads_here(1, 0, slice(0, gate_half)))
     for j in range(LINE):
         acc[j] = dot(turned[1, j], grads_all[1])
-    earlier = list(pending)
-    pending.clear()
     for p, lanes in enumerate(pairs):
         @pl.when(early)
         def _():
@@ -728,30 +736,29 @@
             chip = jnp.where(k == 0, j * LINE + x, y * LINE + j)
             for q in range(2):
                 src, dst = leaving.at[d, q * rows:(q + 1) * rows, lanes], landed.at[k, me, :, lanes]
-                make = functools.partial(
-                    remote, src, dst, rv_s.at[p, d * 2 + q], rv_r.at[p, k, me], (z, chip, q)
+                copy = functools.partial(
+                    remote, src, dst, rv_s.at[p, min(d, 1)], rv_r.at[p], (z, chip, q)
                 )
                 if d == 0:
                     pl.when(k == q)(
-                        functools.partial(
-                            lambda src, dst, sem: pltpu.make_async_copy(src, dst, sem).start(),
-                            src, dst, rv_r.at[p, k, me],
-                        )
+                        lambda: pltpu.make_async_copy(src, dst, rv_r.at[p]).start()
                     )
-                send(k != q if d == 0 else None, make)
-    for wait in earlier:
+                    pl.when(k != q)(lambda: copy().start())
+                else:
+                    copy().start()
+    for wait in pending:
         wait()
     for p, lanes in enumerate(pairs):
-        for c in range(2):
-            for i in range(LINE):
-                arrived(landed.at[c, i, :, lanes], rv_r.at[p, c, i])
+        arrived(landed.at[:, :, :, lanes], rv_r.at[p])
+        for c in range(2):
             for g in (2 * p, 2 * p + 1):
                 total = landed[c, 0, :, g * half:(g + 1) * half].astype(F32)
                 for i in range(1, LINE):
                     total = total + landed[c, i, :, g * half:(g + 1) * half].astype(F32)
                 out[:, g * hid + c * half:g * hid + (c + 1) * half] = total
-    for wait in pending:
-        wait()
+    for p, lanes in enumerate(pairs):
+        for ref, sem in ((leaving.at[0, 0:rows, lanes], rv_s.at[p, 0]), (leaving.at[1:4, :, lanes], rv_s.at[p, 1])):
+            remote(ref, ref, sem, sem, (z, s, 1 - k)).wait_send()
 
 
 def on_device(frames, cotangent, first_hidden, first_cell, gate_bias, gate_weight):
@@ -796,12 +803,10 @@
         dma((2, 2, 4)), dma((2,)),
         dma((steps, 2, 3)), dma((steps, 2)), dma((steps, 2, 2)), dma((steps, 2)),
         dma((2,)), dma((steps, 3)), dma((2,)),
-        dma((steps, 2, 2 * LINE)), dma((steps, 2, 2 * LINE)), dma((steps, 2 * LINE)), dma((3, 2 * LINE)),
-        dma((2, 2, LINE)),
+        dma((steps, 2)), dma((steps, 2)), dma((steps,)), dma((3,)), dma((2,)),
         dma((steps, 2, 2)), dma((steps, 2)), dma((2,)), dma((2,)), dma((2,)), dma((steps, 2)),
         dma((steps, 2, 3)), dma((steps, 2)), dma((2, 2)), dma((2,)), dma((steps, 3)), dma((2,)),
-        dma((steps, 2, 2 * LINE)), dma((steps, 2, 2 * LINE)), dma((steps, 2 * LINE)), dma((3, 2 * LINE)),
-        dma((2, 2 * LINE)),
+        dma((steps, 2)), dma((steps, 2)), dma((steps,)), dma((3,)), dma((2, 2)),
     ]
     result = pl.pallas_call(
         kernel,

time: 77.4 us -> 77 us (level)
  no operation moved by 1% of the time
where the time goes in v7:
time: 77 us; the launch traced here: 76.8 us
  Pallas kernels  74.9 us (97%)
  local copies, waits for them, and re-layouts  1.93 us (3%)
    pallas_call x1, Pallas kernels, on_device(): pl.pallas_call(kernel, out_shape=jax.ShapeDtypeStruct((share, gates), F32...  74.9 us
    unnamed x1, local copies, waits for them, and re-layouts  1.93 us

profile of v7, /device:TPU:1, one launch (start us, length us, event | category | flops | bytes accessed | tf_op | source)
XLA Modules:
  0.0 76.8 jit_solution(9882487754537246470)
XLA Ops:
  0.0 74.9 %shard_map.64 = f32[144,1024]{1,0:T(8,128)} custom-call(bf16[2,128,256]{2,1,0:T(8,128)(2,1)} %bitcast.8, bf16[2,128,256]{2,1,0:T(8,128)(2,1)} %bitcast.9, bf16[128,256]{1,0:T(8,128)(2,1)} %bitcast.11, f32[128,256]{1,0:T(8,128)} %bitcast.10, f32[1,1024]{1,0:T(1,128)} %bias.1, bf16[3,3,512,1024]{3,2,1,0:T(8,128)(2,1)} %bitcast.6), custom_call_target="tpu_custom_call" | custom-call | tf_op jit(solution)/shard_map/pallas_call | solution.py:811
  74.9 1.9 %copy.8 = f32[1,144,1024]{2,1,0:T(8,128)} copy(f32[1,144,1024]{2,1,0:T(8,128)} %bitcast.7) | data formatting | bytes 1179648

commit v8 on v7

--- a/solution.py
+++ b/solution.py
@@ -20,9 +20,9 @@
 def kernel(
     frames, cotangent, first_hidden, first_cell, bias, weight, out,
     wx, wh, wxt, wht, sx, sh, sg, top_hidden, preact, gates, cells, carry, coef, gin, gx_out, ghid,
-    tiles_all, flipped, turned, grads_all, packed, packed_all, vec, vec_all, acc, leaving, landed,
+    tiles_all, flipped, turned, grads_all, packed, packed_all, vec_all, acc, leaving, landed,
     w_sem, in_sem, sx_r, sx_f, sh_r, sh_f, c_r, gx_r, gh_r, ti_r, ga_r, co_r, ve_r, rv_r,
-    fr_s, fr_f, fh_s, fh_f, fc_s, ct_s, sx_s, sx_fs, sh_s, sh_fs, gx_s, gh_s, ti_s, ga_s, co_s, ve_s, rv_s,
+    fr_s, fr_f, fh_s, fh_f, fc_s, ct_s, sx_s, sx_fs, sh_s, sh_fs, gx_s, gh_s, ti_s, ga_s, co_s, ve_s, vd_s, rv_s,
 ):
     z, s, k = lax.axis_index("section"), lax.axis_index("space"), lax.axis_index("batch")
     y, x = s // LINE, s % LINE
@@ -107,6 +107,10 @@
         ]
 
     below, above = section_at(-1, z > 0), section_at(1, z < sections - 1)
+    group = [
+        (base, (z + 1, jnp.where(k == 0, y * LINE + j, j * LINE + x), core))
+        for j in range(LINE) for core in range(2)
+    ]
     greet(plane)
 
     half_lanes = [slice(hid + c * half, hid + (c + 1) * half) for c in range(2)]
@@ -145,7 +149,9 @@
     pl.when(top)(lambda: clear(above2, above1))
     pl.when(bottom)(lambda: clear(below2, below1))
 
-    pl.semaphore_wait(barrier, count(plane) + count(below))
+    pl.semaphore_wait(
+        barrier, count(plane) + count(below) + jnp.where(z == 1, len(group), 0)
+    )
 
     def send_edges(src, dst, send_sems, recv_sems, section, pred):
         edges(lambda: (src, dst, send_sems, recv_sems), section, pred)
@@ -190,6 +196,7 @@
 
     send_frames(0)
     greet(above)
+    greet(group)
     greet(below)
     send_edges(beyond(first_hidden), at_rows(sh, 0, far, centre), fh_f, sh_f.at[0], z, None)
     send_edges(outer(first_cell, cols), narrow(cells.at[0]), fc_s, c_r, z, None)
@@ -307,7 +314,7 @@
 
     def spread_to_group(pred, view, seven, send_sem, recv_sem):
         def go():
-            for d in (0, 1, 3, 2):
+            for d in (2, 1, 3, 0):
                 for c in range(2):
                     there = ((x if c == 0 else y) + d) % LINE
                     chip = y * LINE + there if c == 0 else there * LINE + x
@@ -342,23 +349,24 @@
 
     pairs = [slice(p * 2 * half, (p + 1) * 2 * half) for p in range(2)]
 
-    def send_grads(t, pred):
-        for p, lanes in enumerate(pairs if t == 0 else [slice(0, gate_half)]):
-            def view(c, slot, lanes=lanes):
-                at = 4 * hid + c * gate_half
-                src = sg.at[t, own1, at + lanes.start:at + lanes.stop]
-                return src, grads_all.at[t, rows_of(slot), lanes]
-
-            spread_to_group(
-                pred, view, lambda lanes=lanes: grads_all.at[t, most, lanes],
-                lambda p=p: ga_s.at[t, p], lambda p=p: ga_r.at[t, p],
-            )
+    def send_grads(t, p, pred):
+        lanes = pairs[p]
+
+        def view(c, slot):
+            at = 4 * hid + c * gate_half
+            src = sg.at[t, own1, at + lanes.start:at + lanes.stop]
+            return src, grads_all.at[t, rows_of(slot), lanes]
+
+        spread_to_group(
+            pred, view, lambda: grads_all.at[t, most, lanes],
+            lambda: ga_s.at[t, p], lambda: ga_r.at[t, p],
+        )
 
     early = z < 2
 
     def send_factors(t):
         def view(c, slot):
-            src = packed.at[t, :, c * gate_half:(c + 1) * gate_half]
+            src = packed.at[t, :, c * 5 * half:(c + 1) * 5 * half]
             return src, packed_all.at[t, rows_of(slot), :]
 
         spread_to_group(
@@ -369,22 +377,44 @@
         for c in range(2):
             chan = slice(c * half, (c + 1) * half)
             for t in range(2):
-                for g in range(4):
-                    value = coef[t, 1 + g, own1, chan]
-                    if t == 1 and g != 2:
-                        value = value * coef[t, 0, own1, chan]
-                    at = c * gate_half + g * half
+                first = coef[t, 0, own1, chan]
+                for g in range(5):
+                    if g == 4:
+                        value = first * coef[t, 5, own1, chan] if t == 1 else first
+                    else:
+                        value = coef[t, 1 + g, own1, chan]
+                        if t == 1 and g != 2:
+                            value = value * first
+                    at = (c * 5 + g) * half
                     packed[t, :, at:at + half] = value.astype(BF16)
 
     def send_vec(index, pred):
         def view(c, slot):
             chan = slice(c * half, (c + 1) * half)
-            src = gin.at[1, own1, chan] if index == 0 else vec.at[index - 1, :, chan]
+            src = ghid.at[own1, chan] if index == 2 else gin.at[1 - index, own1, chan]
             return src, vec_all.at[index, rows_of(slot), :]
 
         spread_to_group(
             pred, view, lambda: vec_all.at[index, most], lambda: ve_s.at[index], lambda: ve_r.at[index]
         )
+
+    def send_down():
+        def go():
+            for d in (2, 1, 3, 0):
+                for c in range(2):
+                    there = ((x if c == 0 else y) + d) % LINE
+                    chip = y * LINE + there if c == 0 else there * LINE + x
+                    remote(
+                        gx_out.at[0, :, c * half:(c + 1) * half],
+                        vec_all.at[1, rows_of(2 * (x if c == 0 else y) + k), :],
+                        vd_s.at[0], ve_r.at[1], (z - 1, chip, c),
+                    ).start()
+
+        def done():
+            remote(vec_all.at[1], vec_all.at[1], vd_s.at[0], ve_r.at[1], (z, s, 1 - k)).wait_send()
+
+        pl.when(z == 1)(go)
+        pending.append(lambda: pl.when(z == 1)(done))
 
     rows = out.shape[0]
     block = 2 * rows
@@ -619,17 +649,7 @@
             total = term if total is None else total + term
         return total.astype(BF16)
 
-    for t in (1, 0):
-        arrived(gin.at[t, own1], gx_r.at[t, 2])
-        if t == 1:
-            send_vec(0, base)
-        if t == 1:
-            narrow_here(gin.at[t], gx_r.at[t])
-        else:
-            @pl.when(inner)
-            def _():
-                narrow_here(gin.at[0], gx_r.at[0])
-                narrow_here(ghid, gh_r)
+    def gate_grads(t):
         for c in range(2):
             chan = slice(c * half, (c + 1) * half)
             grad_h = gin[t, :, chan].astype(F32)
@@ -646,48 +666,50 @@
             )):
                 at = 4 * hid + c * gate_half + g * half
                 sg[t, :, at:at + half] = value.astype(BF16)
-            if t == 0:
-                vec[0, :, chan] = grad_c[cols:cols + n].astype(BF16)
-                vec[1, :, chan] = grad_h[cols:cols + n].astype(BF16)
             if t == 1:
                 carry[:, chan] = grad_c * coef[t, 5, :, chan]
-        if t == 0:
-            send_vec(1, early)
-            send_vec(2, early)
-
-        def widen(t=t):
-            spread(sg, t, slice(0, 2 * cols + n), 4 * hid)
-
-        def input_grad(t=t):
-            gx_out[t] = back_conv(t, wxt)
-
-        if t == 1:
-            widen()
-            pl.when(inner)(input_grad)
-        else:
-            @pl.when(inner)
-            def _():
-                widen()
-                input_grad()
-
+        spread(sg, t, slice(0, 2 * cols + n), 4 * hid)
+
+    def send_input_grad(t, pred):
         send(
-            inner,
-            lambda t=t: remote(gx_out.at[t], gin.at[t, own1], gx_s.at[t, 2], gx_r.at[t, 2], (z - 1, s, k)),
-        )
-        send_edges(
-            outer(gx_out.at[t], cols), narrow(gin.at[t]), gx_s.at[t], gx_r.at[t], z - 1,
-            inner if t == 1 else z >= 2,
-        )
-        if t == 1:
-            ghid[own1] = back_conv(t, wht)
-            send_edges(
-                (ghid.at[cols:2 * cols], ghid.at[n:n + cols]), narrow(ghid), gh_s, gh_r, z, inner
-            )
-            send_tile(1, 0, roof)
-            send_vec(0, z == 1)
-        else:
-            send_grads(1, z >= 2)
-            send_grads(0, z >= 2)
+            pred,
+            lambda: remote(gx_out.at[t], gin.at[t, own1], gx_s.at[t, 2], gx_r.at[t, 2], (z - 1, s, k)),
+        )
+        send_edges(outer(gx_out.at[t], cols), narrow(gin.at[t]), gx_s.at[t], gx_r.at[t], z - 1, pred)
+
+    arrived(gin.at[1, own1], gx_r.at[1, 2])
+    send_vec(0, base)
+    narrow_here(gin.at[1], gx_r.at[1])
+    gate_grads(1)
+
+    @pl.when(inner)
+    def _():
+        gx_out[1] = back_conv(1, wxt)
+
+    send_input_grad(1, inner)
+    ghid[own1] = back_conv(1, wht)
+    send_edges((ghid.at[cols:2 * cols], ghid.at[n:n + cols]), narrow(ghid), gh_s, gh_r, z, inner)
+    send_vec(0, z == 1)
+    send_vec(2, early)
+    send_tile(1, 0, roof)
+    send_grads(1, 0, z == 2)
+
+    pl.when(inner)(lambda: arrived(gin.at[0, own1], gx_r.at[0, 2]))
+    send_vec(1, z == 1)
+
+    @pl.when(inner)
+    def _():
+        narrow_here(gin.at[0], gx_r.at[0])
+        narrow_here(ghid, gh_r)
+        gate_grads(0)
+        gx_out[0] = back_conv(0, wxt)
+
+    send_down()
+    send_input_grad(0, z >= 2)
+    send_grads(1, 0, roof)
+    send_grads(1, 1, z >= 2)
+    send_grads(0, 0, z >= 2)
+    send_grads(0, 1, z >= 2)
 
     pl.when(z >= 2)(turn_patches)
 
@@ -700,35 +722,40 @@
     def factors_here(t):
         arrived(packed_all.at[t], co_r.at[t])
 
-    def form(t, gates_of, index):
-        for g in gates_of:
-            lanes = slice(g * half, (g + 1) * half)
-            grads_all[t, :, lanes] = (
-                packed_all[t, :, lanes].astype(F32) * vec_all[index].astype(F32)
-            ).astype(BF16)
+    def factor(t, g):
+        return packed_all[t, :, g * half:(g + 1) * half].astype(F32)
+
+    def put(t, g, value):
+        grads_all[t, :, g * half:(g + 1) * half] = (factor(t, g) * value).astype(BF16)
 
     @pl.when(early)
     def _():
         factors_here(1)
         factors_here(0)
         vec_here(0)
-        form(1, range(4), 0)
-
-    pl.when(z >= 2)(lambda: grads_here(1, 0, slice(0, gate_half)))
+        for g in range(4):
+            put(1, g, vec_all[0].astype(F32))
+
+    @pl.when(z >= 2)
+    def _():
+        grads_here(1, 0, pairs[0])
+        grads_here(1, 1, pairs[1])
+
     for j in range(LINE):
         acc[j] = dot(turned[1, j], grads_all[1])
     for p, lanes in enumerate(pairs):
         @pl.when(early)
         def _():
-            vec_here(1 + p)
             if p == 0:
-                form(0, (0, 1), 1)
-            else:
-                form(0, (2,), 2)
-                form(0, (3,), 1)
+                vec_here(2)
+                vec_here(1)
+            grad_h = vec_all[1].astype(F32) + vec_all[2].astype(F32)
+            grad_c = vec_all[0].astype(F32) * factor(1, 4) + grad_h * factor(0, 4)
+            put(0, 2 * p, grad_h if p else grad_c)
+            put(0, 2 * p + 1, grad_c)
 
         pl.when(z >= 2)(lambda: grads_here(0, p, lanes))
-        for d in (1, 3, 2, 0):
+        for d in (2, 1, 3, 0):
             j = (me + d) % LINE
             leaving[d, :, lanes] = (
                 acc[j, :, lanes] + dot(turned[0, j], grads_all[0, :, lanes])
@@ -793,9 +820,8 @@
         pltpu.VMEM((18 * hid, n), BF16),
         pltpu.VMEM((steps, LINE, block, 2 * LINE * n), BF16),
         pltpu.VMEM((steps, 2 * LINE * n, gates // 2), BF16),
-        pltpu.VMEM((steps, n, gates), BF16),
-        pltpu.VMEM((steps, 2 * LINE * n, gates // 2), BF16),
-        pltpu.VMEM((2, n, hid), BF16),
+        pltpu.VMEM((steps, n, 5 * hid), BF16),
+        pltpu.VMEM((steps, 2 * LINE * n, 5 * half), BF16),
         pltpu.VMEM((3, 2 * LINE * n, half), BF16),
         pltpu.VMEM((LINE, block, gates // 2), F32),
         pltpu.VMEM((LINE, block, gates // 2), BF16),
@@ -806,7 +832,7 @@
         dma((steps, 2)), dma((steps, 2)), dma((steps,)), dma((3,)), dma((2,)),
         dma((steps, 2, 2)), dma((steps, 2)), dma((2,)), dma((2,)), dma((2,)), dma((steps, 2)),
         dma((steps, 2, 3)), dma((steps, 2)), dma((2, 2)), dma((2,)), dma((steps, 3)), dma((2,)),
-        dma((steps, 2)), dma((steps, 2)), dma((steps,)), dma((3,)), dma((2, 2)),
+        dma((steps, 2)), dma((steps, 2)), dma((steps,)), dma((3,)), dma((1,)), dma((2, 2)),
     ]
     result = pl.pallas_call(
         kernel,

time: 77 us -> 74.6 us (0.969)
  Pallas kernels: 74.9 us -> 72.5 us
    pallas_call x1, Pallas kernels: 74.9 us -> 72.5 us  [on_device(): pl.pallas_call(kernel, out_shape=jax.ShapeDtypeStruct((share, gates), F32...]
where the time goes in v8:
time: 74.6 us; the launch traced here: 74.4 us
  Pallas kernels  72.5 us (97%)
  local copies, waits for them, and re-layouts  1.93 us (3%)
    pallas_call x1, Pallas kernels, on_device(): pl.pallas_call(kernel, out_shape=jax.ShapeDtypeStruct((share, gates), F32...  72.5 us
    unnamed x1, local copies, waits for them, and re-layouts  1.93 us

profile of v8, /device:TPU:1, one launch (start us, length us, event | category | flops | bytes accessed | tf_op | source)
XLA Modules:
  0.0 74.4 jit_solution(5333933882347673863)
XLA Ops:
  0.0 72.5 %shard_map.64 = f32[144,1024]{1,0:T(8,128)} custom-call(bf16[2,128,256]{2,1,0:T(8,128)(2,1)} %bitcast.8, bf16[2,128,256]{2,1,0:T(8,128)(2,1)} %bitcast.9, bf16[128,256]{1,0:T(8,128)(2,1)} %bitcast.11, f32[128,256]{1,0:T(8,128)} %bitcast.10, f32[1,1024]{1,0:T(1,128)} %bias.1, bf16[3,3,512,1024]{3,2,1,0:T(8,128)(2,1)} %bitcast.6), custom_call_target="tpu_custom_call" | custom-call | tf_op jit(solution)/shard_map/pallas_call | solution.py:837
  72.5 1.9 %copy.8 = f32[1,144,1024]{2,1,0:T(8,128)} copy(f32[1,144,1024]{2,1,0:T(8,128)} %bitcast.7) | data formatting | bytes 1179648

commit v9 on v8

--- a/solution.py
+++ b/solution.py
@@ -20,9 +20,9 @@
 def kernel(
     frames, cotangent, first_hidden, first_cell, bias, weight, out,
     wx, wh, wxt, wht, sx, sh, sg, top_hidden, preact, gates, cells, carry, coef, gin, gx_out, ghid,
-    tiles_all, flipped, turned, grads_all, packed, packed_all, vec_all, acc, leaving, landed,
+    tiles_all, flipped, turned, grads_all, packed, packed_all, vec_all, acc, leaving, landed, result,
     w_sem, in_sem, sx_r, sx_f, sh_r, sh_f, c_r, gx_r, gh_r, ti_r, ga_r, co_r, ve_r, rv_r,
-    fr_s, fr_f, fh_s, fh_f, fc_s, ct_s, sx_s, sx_fs, sh_s, sh_fs, gx_s, gh_s, ti_s, ga_s, co_s, ve_s, vd_s, rv_s,
+    fr_s, fr_f, fh_s, fh_f, fc_s, ct_s, sx_s, sx_fs, sh_s, sh_fs, gx_s, gh_s, ti_s, ga_s, co_s, ve_s, vd_s, rv_s, out_sem,
 ):
     z, s, k = lax.axis_index("section"), lax.axis_index("space"), lax.axis_index("batch")
     y, x = s // LINE, s % LINE
@@ -541,6 +541,12 @@
                 pl.when(inner)(lambda c=c: finish(sx, wx, c))
                 whole = top_hidden.at[:, chan]
                 ends = top_hidden.at[0:cols, chan], top_hidden.at[n - cols:n, chan]
+            edges(
+                lambda ends=ends, lanes=lanes, c=c: (
+                    ends, at_rows(sx, t, near, lanes), sx_s.at[t, c], sx_r.at[t, c]
+                ),
+                z_up, not_roof,
+            )
             send(
                 not_roof,
                 lambda whole=whole, lanes=lanes, c=c: remote(
@@ -549,12 +555,6 @@
             )
             if t == 0:
                 send_edges(ends, at_rows(sh, 1, near, lanes), sh_s.at[c], sh_r.at[1, c], z, None)
-            edges(
-                lambda ends=ends, lanes=lanes, c=c: (
-                    ends, at_rows(sx, t, near, lanes), sx_s.at[t, c], sx_r.at[t, c]
-                ),
-                z_up, not_roof,
-            )
         if t == 0:
             ends = sh.at[1, 3 * cols:4 * cols, centre], sh.at[1, n:n + cols, centre]
             send_edges(ends, at_rows(sh, 1, far, centre), sh_fs, sh_f.at[1], z, None)
@@ -668,26 +668,46 @@
                 sg[t, :, at:at + half] = value.astype(BF16)
             if t == 1:
                 carry[:, chan] = grad_c * coef[t, 5, :, chan]
-        spread(sg, t, slice(0, 2 * cols + n), 4 * hid)
+
+    def first_conv(t, weights):
+        total = None
+        for b in (1, 0, 2):
+            lanes = slice(b * 4 * hid, (b + 1) * 4 * hid)
+            if b == 0:
+                spread(sg, t, slice(0, 2 * cols + n), 4 * hid)
+            for a in range(3):
+                low = cols * (2 - a)
+                term = dot(sg[t, low:low + n, lanes], weights[a, lanes, :])
+                total = term if total is None else total + term
+        return total.astype(BF16)
 
     def send_input_grad(t, pred):
+        send_edges(outer(gx_out.at[t], cols), narrow(gin.at[t]), gx_s.at[t], gx_r.at[t], z - 1, pred)
         send(
             pred,
             lambda: remote(gx_out.at[t], gin.at[t, own1], gx_s.at[t, 2], gx_r.at[t, 2], (z - 1, s, k)),
         )
-        send_edges(outer(gx_out.at[t], cols), narrow(gin.at[t]), gx_s.at[t], gx_r.at[t], z - 1, pred)
 
     arrived(gin.at[1, own1], gx_r.at[1, 2])
     send_vec(0, base)
     narrow_here(gin.at[1], gx_r.at[1])
-    gate_grads(1)
 
     @pl.when(inner)
     def _():
-        gx_out[1] = back_conv(1, wxt)
+        gate_grads(1)
+        gx_out[1] = first_conv(1, wxt)
 
     send_input_grad(1, inner)
-    ghid[own1] = back_conv(1, wht)
+
+    @pl.when(inner)
+    def _():
+        ghid[own1] = back_conv(1, wht)
+
+    @pl.when(base)
+    def _():
+        gate_grads(1)
+        ghid[own1] = first_conv(1, wht)
+
     send_edges((ghid.at[cols:2 * cols], ghid.at[n:n + cols]), narrow(ghid), gh_s, gh_r, z, inner)
     send_vec(0, z == 1)
     send_vec(2, early)
@@ -702,7 +722,7 @@
         narrow_here(gin.at[0], gx_r.at[0])
         narrow_here(ghid, gh_r)
         gate_grads(0)
-        gx_out[0] = back_conv(0, wxt)
+        gx_out[0] = first_conv(0, wxt)
 
     send_down()
     send_input_grad(0, z >= 2)
@@ -775,6 +795,10 @@
                     copy().start()
     for wait in pending:
         wait()
+    def final(p):
+        wide = slice(2 * p * hid, 2 * (p + 1) * hid)
+        return pltpu.make_async_copy(result.at[:, wide], out.at[:, wide], out_sem.at[p])
+
     for p, lanes in enumerate(pairs):
         arrived(landed.at[:, :, :, lanes], rv_r.at[p])
         for c in range(2):
@@ -782,10 +806,12 @@
                 total = landed[c, 0, :, g * half:(g + 1) * half].astype(F32)
                 for i in range(1, LINE):
                     total = total + landed[c, i, :, g * half:(g + 1) * half].astype(F32)
-                out[:, g * hid + c * half:g * hid + (c + 1) * half] = total
+                result[:, g * hid + c * half:g * hid + (c + 1) * half] = total
+        final(p).start()
     for p, lanes in enumerate(pairs):
         for ref, sem in ((leaving.at[0, 0:rows, lanes], rv_s.at[p, 0]), (leaving.at[1:4, :, lanes], rv_s.at[p, 1])):
             remote(ref, ref, sem, sem, (z, s, 1 - k)).wait_send()
+        final(p).wait()
 
 
 def on_device(frames, cotangent, first_hidden, first_cell, gate_bias, gate_weight):
@@ -826,19 +852,20 @@
         pltpu.VMEM((LINE, block, gates // 2), F32),
         pltpu.VMEM((LINE, block, gates // 2), BF16),
         pltpu.VMEM((2, LINE, share, gates // 2), BF16),
+        pltpu.VMEM((share, gates), F32),
         dma((2, 2, 4)), dma((2,)),
         dma((steps, 2, 3)), dma((steps, 2)), dma((steps, 2, 2)), dma((steps, 2)),
         dma((2,)), dma((steps, 3)), dma((2,)),
         dma((steps, 2)), dma((steps, 2)), dma((steps,)), dma((3,)), dma((2,)),
         dma((steps, 2, 2)), dma((steps, 2)), dma((2,)), dma((2,)), dma((2,)), dma((steps, 2)),
         dma((steps, 2, 3)), dma((steps, 2)), dma((2, 2)), dma((2,)), dma((steps, 3)), dma((2,)),
-        dma((steps, 2)), dma((steps, 2)), dma((steps,)), dma((3,)), dma((1,)), dma((2, 2)),
+        dma((steps, 2)), dma((steps, 2)), dma((steps,)), dma((3,)), dma((1,)), dma((2, 2)), dma((2,)),
     ]
     result = pl.pallas_call(
         kernel,
         out_shape=jax.ShapeDtypeStruct((share, gates), F32),
         in_specs=[anywhere] * 4 + [vmem, anywhere],
-        out_specs=vmem,
+        out_specs=anywhere,
         scratch_shapes=scratch,
         compiler_params=pltpu.CompilerParams(
             collective_id=0, has_side_effects=True, vmem_limit_bytes=56 * 2**20

time: 74.6 us -> 75.4 us (1.011)
  Pallas kernels: 72.5 us -> 73.3 us
    pallas_call x1, Pallas kernels: 72.5 us -> 73.3 us  [on_device(): pl.pallas_call(kernel, out_shape=jax.ShapeDtypeStruct((share, gates), F32...]
where the time goes in v9:
time: 75.4 us; the launch traced here: 75.2 us
  Pallas kernels  73.3 us (97%)
  local copies, waits for them, and re-layouts  1.93 us (3%)
    pallas_call x1, Pallas kernels, on_device(): pl.pallas_call(kernel, out_shape=jax.ShapeDtypeStruct((share, gates), F32...  73.3 us
    unnamed x1, local copies, waits for them, and re-layouts  1.93 us

profile of v9, /device:TPU:1, one launch (start us, length us, event | category | flops | bytes accessed | tf_op | source)
XLA Modules:
  0.0 75.2 jit_solution(3845404978148753005)
XLA Ops:
  0.0 73.3 %shard_map.64 = f32[144,1024]{1,0:T(8,128)} custom-call(bf16[2,128,256]{2,1,0:T(8,128)(2,1)} %bitcast.8, bf16[2,128,256]{2,1,0:T(8,128)(2,1)} %bitcast.9, bf16[128,256]{1,0:T(8,128)(2,1)} %bitcast.11, f32[128,256]{1,0:T(8,128)} %bitcast.10, f32[1,1024]{1,0:T(1,128)} %bias.1, bf16[3,3,512,1024]{3,2,1,0:T(8,128)(2,1)} %bitcast.6), custom_call_target="tpu_custom_call" | custom-call | tf_op jit(solution)/shard_map/pallas_call | solution.py:864
  73.3 1.9 %copy.8 = f32[1,144,1024]{2,1,0:T(8,128)} copy(f32[1,144,1024]{2,1,0:T(8,128)} %bitcast.7) | data formatting | bytes 1179648

commit v10 on v9

--- a/solution.py
+++ b/solution.py
@@ -612,27 +612,7 @@
     send_tile(0, 0, inner)
     spread(sh, 1, own2, hid)
 
-    @pl.when(not_roof)
-    def _():
-        own_rows(1)
-        beside_rows(0)
-        beside_rows(1)
-
-    @pl.when(roof)
-    def _():
-        beside_rows(0)
-        near_here(sh, 1, sh_r.at[1], half_lanes)
-
-    send_tile(1, 1, roof)
-    pl.when(roof)(all_rows)
-
-    def blank(outside):
-        coef[:, :, outside, :] = jnp.zeros((2, 6, cols, hid), F32)
-
-    pl.when(top)(lambda: blank(above1))
-    pl.when(bottom)(lambda: blank(below1))
-
-    pl.when(z < 2)(turn_all_weights)
+    pl.when(not_roof)(lambda: own_rows(1))
     pl.when(early)(pack_factors)
     send_tile(0, 1, base)
     send_tile(0, 0, base)
@@ -640,6 +620,27 @@
     send_tile(1, 0, not_roof)
     send_factors(1)
     send_factors(0)
+
+    @pl.when(not_roof)
+    def _():
+        beside_rows(0)
+        beside_rows(1)
+
+    @pl.when(roof)
+    def _():
+        beside_rows(0)
+        near_here(sh, 1, sh_r.at[1], half_lanes)
+
+    send_tile(1, 1, roof)
+    pl.when(roof)(all_rows)
+
+    def blank(outside):
+        coef[:, :, outside, :] = jnp.zeros((2, 6, cols, hid), F32)
+
+    pl.when(top)(lambda: blank(above1))
+    pl.when(bottom)(lambda: blank(below1))
+
+    pl.when(z < 2)(turn_all_weights)
     pl.when(z < 2)(turn_patches)
 
     def back_conv(t, weights):

time: 75.4 us -> 73.3 us (0.972)
  Pallas kernels: 73.3 us -> 71.2 us
    pallas_call x1, Pallas kernels: 73.3 us -> 71.2 us  [on_device(): pl.pallas_call(kernel, out_shape=jax.ShapeDtypeStruct((share, gates), F32...]
where the time goes in v10:
time: 73.3 us; the launch traced here: 73.2 us
  Pallas kernels  71.2 us (97%)
  local copies, waits for them, and re-layouts  1.93 us (3%)
    pallas_call x1, Pallas kernels, on_device(): pl.pallas_call(kernel, out_shape=jax.ShapeDtypeStruct((share, gates), F32...  71.2 us
    unnamed x1, local copies, waits for them, and re-layouts  1.93 us

profile of v10, /device:TPU:1, one launch (start us, length us, event | category | flops | bytes accessed | tf_op | source)
XLA Modules:
  0.0 73.2 jit_solution(11511673065483768578)
XLA Ops:
  0.0 71.2 %shard_map.64 = f32[144,1024]{1,0:T(8,128)} custom-call(bf16[2,128,256]{2,1,0:T(8,128)(2,1)} %bitcast.8, bf16[2,128,256]{2,1,0:T(8,128)(2,1)} %bitcast.9, bf16[128,256]{1,0:T(8,128)(2,1)} %bitcast.11, f32[128,256]{1,0:T(8,128)} %bitcast.10, f32[1,1024]{1,0:T(1,128)} %bias.1, bf16[3,3,512,1024]{3,2,1,0:T(8,128)(2,1)} %bitcast.6), custom_call_target="tpu_custom_call" | custom-call | tf_op jit(solution)/shard_map/pallas_call | solution.py:865
  71.2 1.9 %copy.8 = f32[1,144,1024]{2,1,0:T(8,128)} copy(f32[1,144,1024]{2,1,0:T(8,128)} %bitcast.7) | data formatting | bytes 1179648

commit v11 on v10

--- a/solution.py
+++ b/solution.py
@@ -253,9 +253,9 @@
             total = term if total is None else total + term
         return total
 
-    def conv_all(buffer, t, weights, c):
+    def conv_all(buffer, t, weights, c, offsets):
         total = None
-        for a in range(3):
+        for a in offsets:
             term = dot(
                 buffer[t, cols * a:cols * (a + 2) + n, :],
                 weights[c, a].reshape(3 * hid, gate_half),
@@ -588,16 +588,25 @@
                 (i_gate, f_gate, o_gate, cand, squash), old, chan,
             )
 
-    def all_rows():
+    def add_all(buffer, weights, offsets):
+        for c in range(2):
+            preact[:, c * gate_half:(c + 1) * gate_half] += conv_all(buffer, 1, weights, c, offsets)
+
+    def all_rows_h():
+        near_here(sh, 1, sh_r.at[1], half_lanes)
+        for c in range(2):
+            preact[:, c * gate_half:(c + 1) * gate_half] = conv_all(sh, 1, wh, c, (1,)) + bias_of(c)
         far_here(sh, 1, sh_f.at[1])
-        for c in range(2):
-            preact[:, c * gate_half:(c + 1) * gate_half] = conv_all(sh, 1, wh, c) + bias_of(c)
+        add_all(sh, wh, (0, 2))
+
+    def all_rows_x():
         x_here(1)
         near_here(sx, 1, sx_r.at[1], half_lanes)
+        add_all(sx, wx, (1,))
         far_here(sx, 1, sx_f.at[1])
         for c in range(2):
             chan = slice(c * half, (c + 1) * half)
-            now = preact[:, c * gate_half:(c + 1) * gate_half] + conv_all(sx, 1, wx, c)
+            now = preact[:, c * gate_half:(c + 1) * gate_half] + conv_all(sx, 1, wx, c, (0, 2))
             old = cells[1, :, chan]
             i_gate, f_gate, o_gate, cand, new, squash = activate(now, old)
             save(
@@ -629,10 +638,10 @@
     @pl.when(roof)
     def _():
         beside_rows(0)
-        near_here(sh, 1, sh_r.at[1], half_lanes)
+        all_rows_h()
 
     send_tile(1, 1, roof)
-    pl.when(roof)(all_rows)
+    pl.when(roof)(all_rows_x)
 
     def blank(outside):
         coef[:, :, outside, :] = jnp.zeros((2, 6, cols, hid), F32)
@@ -716,7 +725,6 @@
     send_grads(1, 0, z == 2)
 
     pl.when(inner)(lambda: arrived(gin.at[0, own1], gx_r.at[0, 2]))
-    send_vec(1, z == 1)
 
     @pl.when(inner)
     def _():
@@ -726,6 +734,7 @@
         gx_out[0] = first_conv(0, wxt)
 
     send_down()
+    send_vec(1, z == 1)
     send_input_grad(0, z >= 2)
     send_grads(1, 0, roof)
     send_grads(1, 1, z >= 2)

time: 73.3 us -> 72.9 us (level)
  no operation moved by 1% of the time
where the time goes in v11:
time: 72.9 us; the launch traced here: 72.7 us
  Pallas kernels  70.8 us (97%)
  local copies, waits for them, and re-layouts  1.93 us (3%)
    pallas_call x1, Pallas kernels, on_device(): pl.pallas_call(kernel, out_shape=jax.ShapeDtypeStruct((share, gates), F32...  70.8 us
    unnamed x1, local copies, waits for them, and re-layouts  1.93 us

profile of v11, /device:TPU:1, one launch (start us, length us, event | category | flops | bytes accessed | tf_op | source)
XLA Modules:
  0.0 72.7 jit_solution(3284808224922291725)
XLA Ops:
  0.0 70.8 %shard_map.64 = f32[144,1024]{1,0:T(8,128)} custom-call(bf16[2,128,256]{2,1,0:T(8,128)(2,1)} %bitcast.8, bf16[2,128,256]{2,1,0:T(8,128)(2,1)} %bitcast.9, bf16[128,256]{1,0:T(8,128)(2,1)} %bitcast.11, f32[128,256]{1,0:T(8,128)} %bitcast.10, f32[1,1024]{1,0:T(1,128)} %bias.1, bf16[3,3,512,1024]{3,2,1,0:T(8,128)(2,1)} %bitcast.6), custom_call_target="tpu_custom_call" | custom-call | tf_op jit(solution)/shard_map/pallas_call | solution.py:874
  70.8 1.9 %copy.8 = f32[1,144,1024]{2,1,0:T(8,128)} copy(f32[1,144,1024]{2,1,0:T(8,128)} %bitcast.7) | data formatting | bytes 1179648

commit v12 on v11

--- a/solution.py
+++ b/solution.py
@@ -364,13 +364,13 @@
 
     early = z < 2
 
-    def send_factors(t):
+    def send_factors(t, pred):
         def view(c, slot):
             src = packed.at[t, :, c * 5 * half:(c + 1) * 5 * half]
             return src, packed_all.at[t, rows_of(slot), :]
 
         spread_to_group(
-            early, view, lambda: packed_all.at[t, most], lambda: co_s.at[t], lambda: co_r.at[t]
+            pred, view, lambda: packed_all.at[t, most], lambda: co_s.at[t], lambda: co_r.at[t]
         )
 
     def pack_factors():
@@ -622,13 +622,13 @@
     spread(sh, 1, own2, hid)
 
     pl.when(not_roof)(lambda: own_rows(1))
-    pl.when(early)(pack_factors)
+    pl.when(not_roof)(pack_factors)
     send_tile(0, 1, base)
     send_tile(0, 0, base)
     send_tile(1, 1, not_roof)
     send_tile(1, 0, not_roof)
-    send_factors(1)
-    send_factors(0)
+    send_factors(1, not_roof)
+    send_factors(0, early)
 
     @pl.when(not_roof)
     def _():
@@ -719,12 +719,12 @@
         ghid[own1] = first_conv(1, wht)
 
     send_edges((ghid.at[cols:2 * cols], ghid.at[n:n + cols]), narrow(ghid), gh_s, gh_r, z, inner)
-    send_vec(0, z == 1)
+    send_vec(0, inner & not_roof)
     send_vec(2, early)
     send_tile(1, 0, roof)
-    send_grads(1, 0, z == 2)
 
     pl.when(inner)(lambda: arrived(gin.at[0, own1], gx_r.at[0, 2]))
+    send_vec(1, z == 1)
 
     @pl.when(inner)
     def _():
@@ -734,10 +734,9 @@
         gx_out[0] = first_conv(0, wxt)
 
     send_down()
-    send_vec(1, z == 1)
     send_input_grad(0, z >= 2)
     send_grads(1, 0, roof)
-    send_grads(1, 1, z >= 2)
+    send_grads(1, 1, roof)
     send_grads(0, 0, z >= 2)
     send_grads(0, 1, z >= 2)
 
@@ -758,15 +757,16 @@
     def put(t, g, value):
         grads_all[t, :, g * half:(g + 1) * half] = (factor(t, g) * value).astype(BF16)
 
-    @pl.when(early)
+    pl.when(early)(lambda: factors_here(0))
+
+    @pl.when(not_roof)
     def _():
         factors_here(1)
-        factors_here(0)
         vec_here(0)
         for g in range(4):
             put(1, g, vec_all[0].astype(F32))
 
-    @pl.when(z >= 2)
+    @pl.when(roof)
     def _():
         grads_here(1, 0, pairs[0])
         grads_here(1, 1, pairs[1])

time: 72.9 us -> 74.4 us (1.021)
  Pallas kernels: 70.8 us -> 72.2 us
    pallas_call x1, Pallas kernels: 70.8 us -> 72.2 us  [on_device(): pl.pallas_call(kernel, out_shape=jax.ShapeDtypeStruct((share, gates), F32...]
where the time goes in v12:
time: 74.4 us; the launch traced here: 74.2 us
  Pallas kernels  72.2 us (97%)
  local copies, waits for them, and re-layouts  1.93 us (3%)
    pallas_call x1, Pallas kernels, on_device(): pl.pallas_call(kernel, out_shape=jax.ShapeDtypeStruct((share, gates), F32...  72.2 us
    unnamed x1, local copies, waits for them, and re-layouts  1.93 us

profile of v12, /device:TPU:1, one launch (start us, length us, event | category | flops | bytes accessed | tf_op | source)
XLA Modules:
  0.0 74.2 jit_solution(1182632768104077405)
XLA Ops:
  0.0 72.2 %shard_map.64 = f32[144,1024]{1,0:T(8,128)} custom-call(bf16[2,128,256]{2,1,0:T(8,128)(2,1)} %bitcast.8, bf16[2,128,256]{2,1,0:T(8,128)(2,1)} %bitcast.9, bf16[128,256]{1,0:T(8,128)(2,1)} %bitcast.11, f32[128,256]{1,0:T(8,128)} %bitcast.10, f32[1,1024]{1,0:T(1,128)} %bias.1, bf16[3,3,512,1024]{3,2,1,0:T(8,128)(2,1)} %bitcast.6), custom_call_target="tpu_custom_call" | custom-call | tf_op jit(solution)/shard_map/pallas_call | solution.py:874
  72.2 1.9 %copy.8 = f32[1,144,1024]{2,1,0:T(8,128)} copy(f32[1,144,1024]{2,1,0:T(8,128)} %bitcast.7) | data formatting | bytes 1179648

commit v13 on v11

--- a/solution.py
+++ b/solution.py
@@ -466,7 +466,6 @@
         preact[0:n, c * gate_half:(c + 1) * gate_half] += term
 
     def own_rows(t):
-        hidden_lanes = (centre,) if t == 0 else half_lanes
         part_sums = [conv(sh, t, wh, c, (1,)) + bias_of(c) for c in range(2)]
         for c in range(2):
             preact[0:n, c * gate_half:(c + 1) * gate_half] = part_sums[c]
@@ -480,7 +479,7 @@
             near_here(sx, t, sx_r.at[t], half_lanes)
 
         def h_edges():
-            near_here(sh, t, sh_r.at[t], hidden_lanes)
+            near_here(sh, t, sh_r.at[t], (centre,))
 
         def h_outer():
             for c in range(2):
@@ -553,9 +552,9 @@
                     whole, sx.at[t, own2, lanes], sx_s.at[t, c, 2], sx_r.at[t, c, 2], (z_up, s, k)
                 ),
             )
-            if t == 0:
-                send_edges(ends, at_rows(sh, 1, near, lanes), sh_s.at[c], sh_r.at[1, c], z, None)
         if t == 0:
+            ends = sh.at[1, 2 * cols:3 * cols, centre], sh.at[1, n + cols:n + 2 * cols, centre]
+            send_edges(ends, at_rows(sh, 1, near, centre), sh_s.at[0], sh_r.at[1, 0], z, None)
             ends = sh.at[1, 3 * cols:4 * cols, centre], sh.at[1, n:n + cols, centre]
             send_edges(ends, at_rows(sh, 1, far, centre), sh_fs, sh_f.at[1], z, None)
         else:
@@ -593,7 +592,7 @@
             preact[:, c * gate_half:(c + 1) * gate_half] += conv_all(buffer, 1, weights, c, offsets)
 
     def all_rows_h():
-        near_here(sh, 1, sh_r.at[1], half_lanes)
+        near_here(sh, 1, sh_r.at[1], (centre,))
         for c in range(2):
             preact[:, c * gate_half:(c + 1) * gate_half] = conv_all(sh, 1, wh, c, (1,)) + bias_of(c)
         far_here(sh, 1, sh_f.at[1])

time: 72.9 us -> 73.2 us (level)
  no operation moved by 1% of the time
where the time goes in v13:
time: 73.2 us; the launch traced here: 73.1 us
  Pallas kernels  71.1 us (97%)
  local copies, waits for them, and re-layouts  1.93 us (3%)
    pallas_call x1, Pallas kernels, on_device(): pl.pallas_call(kernel, out_shape=jax.ShapeDtypeStruct((share, gates), F32...  71.1 us
    unnamed x1, local copies, waits for them, and re-layouts  1.93 us

profile of v13, /device:TPU:1, one launch (start us, length us, event | category | flops | bytes accessed | tf_op | source)
XLA Modules:
  0.0 73.1 jit_solution(13765001376944613982)
XLA Ops:
  0.0 71.1 %shard_map.64 = f32[144,1024]{1,0:T(8,128)} custom-call(bf16[2,128,256]{2,1,0:T(8,128)(2,1)} %bitcast.8, bf16[2,128,256]{2,1,0:T(8,128)(2,1)} %bitcast.9, bf16[128,256]{1,0:T(8,128)(2,1)} %bitcast.11, f32[128,256]{1,0:T(8,128)} %bitcast.10, f32[1,1024]{1,0:T(1,128)} %bias.1, bf16[3,3,512,1024]{3,2,1,0:T(8,128)(2,1)} %bitcast.6), custom_call_target="tpu_custom_call" | custom-call | tf_op jit(solution)/shard_map/pallas_call | solution.py:873
  71.1 1.9 %copy.8 = f32[1,144,1024]{2,1,0:T(8,128)} copy(f32[1,144,1024]{2,1,0:T(8,128)} %bitcast.7) | data formatting | bytes 1179648
